TPU v7x, 32 devices: a whole 2x2x4 slice. The times are simulated.
32 devices in a mesh: groups: 2 (over x), wide: 16 (over z, y, core).
Axes of the slice: x: 2, y: 2, z: 4, core: 2. Of those that a mesh axis runs over, the one named last changes fastest.
Arguments:
- embeddings: bfloat16 [65536, 768], P(('groups', 'wide')), parts along dimension 0
- pca_basis: bfloat16 [768, 256], P('wide'), may hold values from -0.21875 to 0.21875
- pca_center: bfloat16 [768], P('wide'), may hold values from -6 to 6
- row_labels: int32 [65536], P(('groups', 'wide')), parts along dimension 0, may hold values from 0 to 63, as said below
- row_ranks: int32 [65536], P(('groups', 'wide')), parts along dimension 0, may hold values from 0 to 4095, as said below
Outputs:
- nearest: float32 [65536], P(('groups', 'wide')), parts along dimension 0
There are 2 independent parts, one for each index of `groups`. A program takes and returns all parts, laid end to end along the dimension named above; an argument that names none is the same for every part. Nothing has to cross between parts.
Inputs may be any that keep to these rules, and one draw needn't show every extreme that they name: `row_labels`: clusters o * 4 to (o + 1) * 4 - 1 form owner group o. Each device's rows fall in every owner group with at most 256 rows; in every draw some owner groups get exactly 256 rows from every device. `row_ranks`: within each cluster the rows' ranks are 0 up to the cluster's size - 1, each once. A cluster holds at most 4096 rows, and in every draw some cluster holds exactly that many.
All inputs are finite; a program needn't handle non-finite values.
Results may differ from a plain program's by a relative error of at most 0.00053.
Values may be sent and summed in bfloat16 or wider, within the bound.
No kernel may reach another device: no remote copies, remote signals or barrier semaphores. Data moves between devices by JAX's collectives and lax.ppermute only.
A program may use at most 64 MiB of HBM per device.

v0:
```python
import jax
import jax.numpy as jnp
from jax import lax
from jax.sharding import PartitionSpec as P

CL_DEV = 4


def project(row_block, pca_basis, pca_center):
    basis_piece = lax.all_gather(pca_basis, "wide", axis=0, tiled=True)
    center_piece = lax.all_gather(pca_center, "wide", axis=0, tiled=True)
    partial_rows = jnp.dot(row_block, basis_piece, preferred_element_type=jnp.float32)
    partial_offset = jnp.dot(center_piece, basis_piece, preferred_element_type=jnp.float32)
    projected = partial_rows
    projected = projected - partial_offset[None, :]
    scale_back = lax.rsqrt(jnp.sum(projected * projected, axis=1, keepdims=True) + 1e-06)
    return (projected * scale_back).astype(jnp.bfloat16)


def paired_maxima(unit_rows, got_labels, got_ranks):
    row_count = unit_rows.shape[0]
    block_rows = min(512, row_count)

    def one_block(block_index):
        row_start = block_index * block_rows
        queries = lax.dynamic_slice_in_dim(unit_rows, row_start, block_rows, 0)
        query_labels = lax.dynamic_slice_in_dim(got_labels, row_start, block_rows, 0)
        query_ranks = lax.dynamic_slice_in_dim(got_ranks, row_start, block_rows, 0)
        cosines = lax.dot_general(
            queries, unit_rows, (((1,), (1,)), ((), ())), preferred_element_type=jnp.float32
        )
        allowed = (
            (query_labels[:, None] == got_labels[None, :])
            & (got_ranks[None, :] < query_ranks[:, None])
            & (query_labels[:, None] >= 0)
        )
        return jnp.max(jnp.where(allowed, cosines, jnp.float32(-1.0)), axis=1)

    return lax.map(one_block, jnp.arange(row_count // block_rows, dtype=jnp.int32)).reshape(-1)


def shards(embeddings, pca_basis, pca_center, row_labels, row_ranks):
    peer_count = lax.axis_size("wide")
    local_rows = embeddings.shape[0]
    slot_rows = 2 * local_rows // peer_count
    buffer_rows = peer_count * slot_rows
    owners = row_labels // CL_DEV
    owner_hit = (owners[:, None] == jnp.arange(peer_count, dtype=jnp.int32)[None, :]).astype(
        jnp.int32
    )
    within = jnp.sum(jnp.cumsum(owner_hit, axis=0) * owner_hit, axis=1) - 1
    place = owners * slot_rows + within
    sent_labels = (
        jnp.full((buffer_rows,), -1, jnp.int32)
        .at[place]
        .set(row_labels)
        .reshape(peer_count, slot_rows)
    )
    sent_ranks = (
        jnp.zeros((buffer_rows,), jnp.int32).at[place].set(row_ranks).reshape(peer_count, slot_rows)
    )
    unit_rows = project(embeddings, pca_basis, pca_center)
    sent_rows = (
        jnp.zeros((buffer_rows, unit_rows.shape[1]), jnp.bfloat16)
        .at[place]
        .set(unit_rows)
        .reshape(peer_count, slot_rows, -1)
    )
    arrived, got_labels, got_ranks = (
        lax.all_to_all(sent_rows, "wide", split_axis=0, concat_axis=0, tiled=True),
        lax.all_to_all(sent_labels, "wide", split_axis=0, concat_axis=0, tiled=True),
        lax.all_to_all(sent_ranks, "wide", split_axis=0, concat_axis=0, tiled=True),
    )
    arrived_units = arrived.reshape(buffer_rows, -1)
    got_labels = got_labels.reshape(-1)
    got_ranks = got_ranks.reshape(-1)
    found = paired_maxima(arrived_units, got_labels, got_ranks)
    returned = lax.all_to_all(
        found.reshape(peer_count, slot_rows), "wide", split_axis=0, concat_axis=0, tiled=True
    )
    return returned.reshape(-1)[place]


def solution(mesh):
    return jax.shard_map(
        shards,
        mesh=mesh,
        in_specs=(
            P(("groups", "wide"), None),
            P("wide", None),
            P("wide"),
            P(("groups", "wide")),
            P(("groups", "wide")),
        ),
        out_specs=P(("groups", "wide")),
        check_vma=False,
    )
```

profile of v0, /device:TPU:0, one launch (start us, length us, event | category | flops | bytes accessed | tf_op | source)
XLA Modules:
  0.0 244.3 jit_solution(11044829855806012872)
XLA Ops:
  0.9 4.5 %reduce-window.6 = s32[16,16,128]{2,1,0:T(8,128)S(1)} reduce-window(s32[16,16,128]{2,1,0:T(8,128)S(1)} %fusion.6, s32[]{:T(128)} %constant.24.clone.1), window={size=1x1x128 pad=0_0x0_0x127_0}, to_apply=%region_0.1 | reduce-window | flops 4161536 | bytes 262148 | tf_op jit(solution)/shard_map/reduce-window
  7.5 8.8 %scatter_custom_fusion.1 = s32[4096]{0:T(1024)} fusion(s32[2048]{0:T(1024)S(1)} %get-tuple-element.67, s32[2048]{0:T(1024)} %param.11, s32[]{:T(128)} %constant.24.clone.1), kind=kCustom, calls=%fused_computation.30 | custom fusion | bytes 16896 | tf_op jit(solution)/shard_map/scatter | solution.py:60
  16.3 7.4 %all-to-all-start.1 = ((s32[16,1,256]{2,1,0:T(1,128)}), s32[16,1,256]{2,1,0:T(1,128)S(1)}, u32[]{:S(2)}, u32[]{:S(2)}) async-start(s32[16,1,256]{2,1,0:T(1,128)} %bitcast.6), calls=%async_computation.1 | async-start | bytes 32768 | tf_op jit(solution)/shard_map/all_to_all | solution.py:72
  23.7 23.0 %all_gather.6 = bf16[768,256]{1,0:T(8,128)(2,1)S(1)} all-gather(bf16[48,256]{1,0:T(8,128)(2,1)} %param.8), channel_id=1, replica_groups=mesh['groups'=2,'wide'=16] {'wide'}, dimensions={0}, use_global_device_ids=true | all-gather | bytes 417792 | tf_op jit(solution)/shard_map/all_gather | solution.py:10
  50.6 30.4 %all-reduce = bf16[768]{0:T(1024)(128)(2,1)} all-reduce(bf16[768]{0:T(1024)(128)(2,1)} %dynamic-update-slice), channel_id=1, replica_groups=mesh['groups'=2,'wide'=16] {'wide'}, use_global_device_ids=true, to_apply=%add | all-reduce | flops 768 | bytes 3072
  81.8 2.4 multiply_reduce_fusion
  84.2 8.8 %scatter_custom_fusion = s32[4096]{0:T(1024)} fusion(s32[2048]{0:T(1024)} %copy-done.2, s32[2048]{0:T(1024)} %param.10, s32[]{:T(128)} %constant.51.clone.1), kind=kCustom, calls=%fused_computation.33 | custom fusion | bytes 16896 | tf_op jit(solution)/shard_map/scatter | solution.py:56
  93.0 3.5 %all-to-all-start = ((s32[16,1,256]{2,1,0:T(1,128)}), s32[16,1,256]{2,1,0:T(1,128)S(1)}, u32[]{:S(2)}, u32[]{:S(2)}) async-start(s32[16,1,256]{2,1,0:T(1,128)} %bitcast.4), calls=%async_computation | async-start | bytes 32768 | tf_op jit(solution)/shard_map/all_to_all | solution.py:71
  96.4 2.8 %multiply_convert_fusion = bf16[2048,256]{0,1:T(8,128)(2,1)} fusion(f32[2048,256]{0,1:T(8,128)} %get-tuple-element.71, f32[2048]{0:T(1024)S(1)} %add_rsqrt_fusion), kind=kLoop, calls=%fused_computation.9 | loop fusion | flops 1048576 | bytes 3153920 | tf_op jit(solution)/shard_map/convert_element_type | solution.py:17
  99.2 2.3 copy.7
  101.5 11.2 %scatter_custom_fusion.2 = bf16[4096,256]{1,0:T(8,128)(2,1)} fusion(s32[2048]{0:T(1024)} %copy-done.2, bf16[2048,256]{1,0:T(8,128)(2,1)} %copy.7, bf16[]{:T(256)} %constant.34.clone.1), kind=kCustom, calls=%fused_computation.11 | custom fusion | bytes 2097664 | tf_op jit(solution)/shard_map/scatter | solution.py:66
  112.7 6.0 %all-to-all-start.2 = ((bf16[16,256,256]{2,1,0:T(8,128)(2,1)}), bf16[16,256,256]{2,1,0:T(8,128)(2,1)}, u32[]{:S(2)}, u32[]{:S(2)}) async-start(bf16[16,256,256]{2,1,0:T(8,128)(2,1)} %bitcast.57), calls=%async_computation.2 | async-start | bytes 4194304 | tf_op jit(solution)/shard_map/all_to_all | solution.py:70
  118.8 41.1 %all-to-all-done.2 = bf16[16,256,256]{2,1,0:T(8,128)(2,1)} async-done(((bf16[16,256,256]{2,1,0:T(8,128)(2,1)}), bf16[16,256,256]{2,1,0:T(8,128)(2,1)}, u32[]{:S(2)}, u32[]{:S(2)}) %all-to-all-start.2) | async-done | bytes 2097184 | tf_op jit(solution)/shard_map/all_to_all | solution.py:70
  159.9 46.3 %while.10 = (s32[]{:T(128)}, f32[8,512]{1,0:T(8,128)S(1)}, s32[8]{0:T(128)S(1)}, s32[4096]{0:T(1024)S(1)}, s32[16,256]{1,0:T(8,128)S(1)}, /*index=5*/s32[16,256]...) while((s32[]{:T(128)}, f32[8,512]{1,0:T(8,128)S(1)}, ...), condition=%wide.region_9.10_spmd, body=%wide.region_7.9_spmd.sunk | while | flops 1086324736 | bytes 2477247 | solution.py:39
  161.3 4.3 %select_reduce_fusion.2 = f32[512]{0:T(512)S(1)} fusion(bf16[4096,256]{1,0:T(8,128)(2,1)} %get-tuple-element.156, s32[4096]{0:T(1024)S(1)} %bitcast.63, s32[4096]{0:T(1024)S(1)} %bitcast.64, s32[512]{0:T(512)S(1)} %dynamic_slice.23, s32[512]{0:T(512)S(1)} %get-tuple-element.123, pred[512]{0:T(512)(128)(4,1)S(1)} %get-tuple-element.124, s32[]{:T(128)S(6)} %select_n.34), kind=kOutput, calls=%fused_computation.4.clone.1 | convolution fusion | flops 1086324224 | bytes 2398724 | tf_op jit(solution)/shard_map/while/body/eval_jaxpr/dot_general | solution.py:29
  167.1 4.3 %select_reduce_fusion.2 = f32[512]{0:T(512)S(1)} fusion(bf16[4096,256]{1,0:T(8,128)(2,1)} %get-tuple-element.156, s32[4096]{0:T(1024)S(1)} %bitcast.63, s32[4096]{0:T(1024)S(1)} %bitcast.64, s32[512]{0:T(512)S(1)} %dynamic_slice.23, s32[512]{0:T(512)S(1)} %get-tuple-element.123, pred[512]{0:T(512)(128)(4,1)S(1)} %get-tuple-element.124, s32[]{:T(128)S(6)} %select_n.34), kind=kOutput, calls=%fused_computation.4.clone.1 | convolution fusion | flops 1086324224 | bytes 2398724 | tf_op jit(solution)/shard_map/while/body/eval_jaxpr/dot_general | solution.py:29
  172.9 4.3 %select_reduce_fusion.2 = f32[512]{0:T(512)S(1)} fusion(bf16[4096,256]{1,0:T(8,128)(2,1)} %get-tuple-element.156, s32[4096]{0:T(1024)S(1)} %bitcast.63, s32[4096]{0:T(1024)S(1)} %bitcast.64, s32[512]{0:T(512)S(1)} %dynamic_slice.23, s32[512]{0:T(512)S(1)} %get-tuple-element.123, pred[512]{0:T(512)(128)(4,1)S(1)} %get-tuple-element.124, s32[]{:T(128)S(6)} %select_n.34), kind=kOutput, calls=%fused_computation.4.clone.1 | convolution fusion | flops 1086324224 | bytes 2398724 | tf_op jit(solution)/shard_map/while/body/eval_jaxpr/dot_general | solution.py:29
  178.7 4.3 %select_reduce_fusion.2 = f32[512]{0:T(512)S(1)} fusion(bf16[4096,256]{1,0:T(8,128)(2,1)} %get-tuple-element.156, s32[4096]{0:T(1024)S(1)} %bitcast.63, s32[4096]{0:T(1024)S(1)} %bitcast.64, s32[512]{0:T(512)S(1)} %dynamic_slice.23, s32[512]{0:T(512)S(1)} %get-tuple-element.123, pred[512]{0:T(512)(128)(4,1)S(1)} %get-tuple-element.124, s32[]{:T(128)S(6)} %select_n.34), kind=kOutput, calls=%fused_computation.4.clone.1 | convolution fusion | flops 1086324224 | bytes 2398724 | tf_op jit(solution)/shard_map/while/body/eval_jaxpr/dot_general | solution.py:29
  184.5 4.3 %select_reduce_fusion.2 = f32[512]{0:T(512)S(1)} fusion(bf16[4096,256]{1,0:T(8,128)(2,1)} %get-tuple-element.156, s32[4096]{0:T(1024)S(1)} %bitcast.63, s32[4096]{0:T(1024)S(1)} %bitcast.64, s32[512]{0:T(512)S(1)} %dynamic_slice.23, s32[512]{0:T(512)S(1)} %get-tuple-element.123, pred[512]{0:T(512)(128)(4,1)S(1)} %get-tuple-element.124, s32[]{:T(128)S(6)} %select_n.34), kind=kOutput, calls=%fused_computation.4.clone.1 | convolution fusion | flops 1086324224 | bytes 2398724 | tf_op jit(solution)/shard_map/while/body/eval_jaxpr/dot_general | solution.py:29
  190.3 4.3 %select_reduce_fusion.2 = f32[512]{0:T(512)S(1)} fusion(bf16[4096,256]{1,0:T(8,128)(2,1)} %get-tuple-element.156, s32[4096]{0:T(1024)S(1)} %bitcast.63, s32[4096]{0:T(1024)S(1)} %bitcast.64, s32[512]{0:T(512)S(1)} %dynamic_slice.23, s32[512]{0:T(512)S(1)} %get-tuple-element.123, pred[512]{0:T(512)(128)(4,1)S(1)} %get-tuple-element.124, s32[]{:T(128)S(6)} %select_n.34), kind=kOutput, calls=%fused_computation.4.clone.1 | convolution fusion | flops 1086324224 | bytes 2398724 | tf_op jit(solution)/shard_map/while/body/eval_jaxpr/dot_general | solution.py:29
  196.1 4.3 %select_reduce_fusion.2 = f32[512]{0:T(512)S(1)} fusion(bf16[4096,256]{1,0:T(8,128)(2,1)} %get-tuple-element.156, s32[4096]{0:T(1024)S(1)} %bitcast.63, s32[4096]{0:T(1024)S(1)} %bitcast.64, s32[512]{0:T(512)S(1)} %dynamic_slice.23, s32[512]{0:T(512)S(1)} %get-tuple-element.123, pred[512]{0:T(512)(128)(4,1)S(1)} %get-tuple-element.124, s32[]{:T(128)S(6)} %select_n.34), kind=kOutput, calls=%fused_computation.4.clone.1 | convolution fusion | flops 1086324224 | bytes 2398724 | tf_op jit(solution)/shard_map/while/body/eval_jaxpr/dot_general | solution.py:29
  201.9 4.3 %select_reduce_fusion.2 = f32[512]{0:T(512)S(1)} fusion(bf16[4096,256]{1,0:T(8,128)(2,1)} %get-tuple-element.156, s32[4096]{0:T(1024)S(1)} %bitcast.63, s32[4096]{0:T(1024)S(1)} %bitcast.64, s32[512]{0:T(512)S(1)} %dynamic_slice.23, s32[512]{0:T(512)S(1)} %get-tuple-element.123, pred[512]{0:T(512)(128)(4,1)S(1)} %get-tuple-element.124, s32[]{:T(128)S(6)} %select_n.34), kind=kOutput, calls=%fused_computation.4.clone.1 | convolution fusion | flops 1086324224 | bytes 2398724 | tf_op jit(solution)/shard_map/while/body/eval_jaxpr/dot_general | solution.py:29
  206.3 17.5 %all_to_all.38 = f32[16,1,256]{2,1,0:T(1,128)S(1)} all-to-all(f32[16,1,256]{2,1,0:T(1,128)S(1)} %all_to_all.32), channel_id=1, replica_groups=mesh['groups'=2,'wide'=16] {'wide'}, dimensions={0} | all-to-all | bytes 32768 | tf_op jit(solution)/shard_map/all_to_all | solution.py:78
  223.8 20.5 %gather_fusion = f32[2048]{0:T(1024)} fusion(f32[4096]{0:T(1024)S(1)} %bitcast.56, s32[2048]{0:T(1024)S(1)} %copy-done.1), kind=kCustom, calls=%fused_computation | custom fusion | bytes 24576 | tf_op jit(solution)/shard_map/gather | solution.py:81
  (74 shorter events, 13.8 us)
Async XLA Ops:
  0.0 81.8 %copy-start = (bf16[2048,768]{1,0:T(8,128)(2,1)S(1)}, bf16[2048,768]{1,0:T(8,128)(2,1)}, u32[]{:S(2)}) copy-start(bf16[2048,768]{1,0:T(8,128)(2,1)} %param.7) | copy-start | bytes 9437188
  7.5 16.2 %copy-start.2 = (s32[2048]{0:T(1024)}, s32[2048]{0:T(1024)S(1)}, u32[]{:S(2)}) copy-start(s32[2048]{0:T(1024)S(1)} %get-tuple-element.67) | copy-start | bytes 24580
  16.3 76.7 %all-to-all-start.1 = ((s32[16,1,256]{2,1,0:T(1,128)}), s32[16,1,256]{2,1,0:T(1,128)S(1)}, u32[]{:S(2)}, u32[]{:S(2)}) async-start(s32[16,1,256]{2,1,0:T(1,128)} %bitcast.6), calls=%async_computation.1 | async-start | bytes 32768 | tf_op jit(solution)/shard_map/all_to_all | solution.py:72
  93.0 19.8 %all-to-all-start = ((s32[16,1,256]{2,1,0:T(1,128)}), s32[16,1,256]{2,1,0:T(1,128)S(1)}, u32[]{:S(2)}, u32[]{:S(2)}) async-start(s32[16,1,256]{2,1,0:T(1,128)} %bitcast.4), calls=%async_computation | async-start | bytes 32768 | tf_op jit(solution)/shard_map/all_to_all | solution.py:71
  112.7 47.2 %all-to-all-start.2 = ((bf16[16,256,256]{2,1,0:T(8,128)(2,1)}), bf16[16,256,256]{2,1,0:T(8,128)(2,1)}, u32[]{:S(2)}, u32[]{:S(2)}) async-start(bf16[16,256,256]{2,1,0:T(8,128)(2,1)} %bitcast.57), calls=%async_computation.2 | async-start | bytes 4194304 | tf_op jit(solution)/shard_map/all_to_all | solution.py:70
  159.9 63.9 %copy-start.1 = (s32[2048]{0:T(1024)S(1)}, s32[2048]{0:T(1024)}, u32[]{:S(2)}) copy-start(s32[2048]{0:T(1024)} %get-tuple-element.66) | copy-start | bytes 24580
where the time goes:
time: 245 us; the launch traced here: 244 us
  blocking collectives  71 us (29%)
  local copies, waits for them, and re-layouts  62 us (25%)
  waiting for transfers between devices  41.1 us (17%)
  matrix products  36.9 us (15%)
  starting transfers between devices  16.9 us (7%)
  other arithmetic  10.5 us (4%)
  loops' own time  5.22 us (2%)
    all_to_all x1, waiting for transfers between devices, shards(): lax.all_to_all(sent_rows, 'wide', split_axis=0, concat_axis=0, tiled=True)  41.1 us
    dot_general x8, matrix products, one_block(): lax.dot_general(queries, unit_rows, (((1,), (1,)), ((), ())), preferred_e...  34.3 us
    unnamed x1, blocking collectives  30.4 us
    all_gather x1, blocking collectives, project(): basis_piece = lax.all_gather(pca_basis, 'wide', axis=0, tiled=True)  23 us
    gather x1, local copies, waits for them, and re-layouts, shards(): return returned.reshape(-1)[place]  20.5 us
    all_to_all x1, blocking collectives, shards(): lax.all_to_all(found.reshape(peer_count, slot_rows), 'wide', split_axis=0...  17.5 us
    scatter x1, local copies, waits for them, and re-layouts, shards(): sent_rows = jnp.zeros((buffer_rows, unit_rows.shape[1]), jnp.bfloat16).at...  11.2 us
    scatter x1, local copies, waits for them, and re-layouts, shards(): jnp.zeros((buffer_rows,), jnp.int32).at[place].set(row_ranks)  8.78 us
  transfers between devices with their start and end apart: 3, of which 1 were waited for; matrix products, arithmetic and copies ran while one was open for 13% of the time, Pallas kernels for 0%

commit v1 on v0

v1 whole, which is shorter than its diff:
```python
import functools

import jax
import jax.numpy as jnp
from jax import lax
from jax.experimental import pallas as pl
from jax.experimental.pallas import tpu as pltpu
from jax.sharding import PartitionSpec as P

CL_DEV = 4
RANK_SPAN = 4096
KEY_LOW = 128
PIECE_TILE = 16
CHUNK = 256
IN_FLIGHT = 4
VMEM_BYTES = 48 * 1024 * 1024
VMEM = pl.BlockSpec(memory_space=pltpu.VMEM)
SMEM = pl.BlockSpec(memory_space=pltpu.SMEM)
F32 = jnp.float32
BF16 = jnp.bfloat16


def call(kernel, outs, operands, scratch=(), smem=(), flops=0, moved=0):
    return pl.pallas_call(
        kernel,
        out_shape=outs,
        in_specs=[SMEM if i in smem else VMEM for i in range(len(operands))],
        out_specs=jax.tree.map(lambda _: VMEM, outs),
        scratch_shapes=list(scratch),
        compiler_params=pltpu.CompilerParams(vmem_limit_bytes=VMEM_BYTES),
        cost_estimate=pl.CostEstimate(flops=flops, bytes_accessed=moved, transcendentals=0),
    )(*operands)


def masks_of(peers):
    far = list(range(peers // 2, peers))
    near = list(range(peers // 4, peers // 2)) + list(range(1, peers // 4))
    order = []
    for i in range(max(len(far), len(near))):
        order += far[i : i + 1] + near[i : i + 1]
    return order


def swap(x, mask, peers):
    return lax.ppermute(x, "wide", [(i, i ^ mask) for i in range(peers)])


def hits(owners, peers):
    return owners == lax.broadcasted_iota(jnp.int32, (peers, owners.shape[1]), 0)


def places_kernel(peers, slot, labels_ref, ranks_ref, place_ref, keys_ref):
    rows = labels_ref.shape[1]
    step = min(CHUNK, rows)
    labels = labels_ref[...]
    owners = labels // CL_DEV
    hit = hits(owners, peers)
    hit_f = jnp.where(hit, 1.0, 0.0)
    earlier = jnp.where(
        lax.broadcasted_iota(jnp.int32, (step, step), 0) < lax.broadcasted_iota(jnp.int32, (step, step), 1), 1.0, 0.0
    ).astype(BF16)
    seen = jnp.zeros((peers, 1), F32)
    within = []
    for b in range(rows // step):
        hit_b = hit_f[:, b * step : (b + 1) * step]
        counts = jnp.dot(hit_b.astype(BF16), earlier, preferred_element_type=F32) + seen
        within.append(jnp.sum(hit_b * counts, axis=0, keepdims=True))
        seen = seen + jnp.sum(hit_b, axis=1, keepdims=True)
    within = jnp.concatenate(within, axis=1).astype(jnp.int32)
    place_ref[...] = owners * slot + within
    keys = (labels % CL_DEV + 1) * RANK_SPAN + ranks_ref[...]
    high = (keys // KEY_LOW).astype(F32)
    low = (keys % KEY_LOW).astype(F32)
    spread = jnp.where(within == lax.broadcasted_iota(jnp.int32, (slot, rows), 0), 1.0, 0.0).astype(BF16)
    parts = jnp.concatenate([hit_f * high, hit_f * low], axis=0).astype(BF16)
    slots = lax.dot_general(parts, spread, (((1,), (1,)), ((), ())), preferred_element_type=F32)
    keys_ref[...] = (slots[:peers] * KEY_LOW + slots[peers:]).astype(jnp.int32)


def project(embeddings_ref, basis, offset, units_ref):
    rows = embeddings_ref.shape[0]
    step = min(CHUNK, rows)
    for b in range(rows // step):
        block = slice(b * step, (b + 1) * step)
        projected = jnp.dot(embeddings_ref[block], basis, preferred_element_type=F32) - offset
        scale_back = lax.rsqrt(jnp.sum(projected * projected, axis=1, keepdims=True) + 1e-06)
        units_ref[block] = (projected * scale_back).astype(BF16)


def project_whole_kernel(embeddings_ref, basis_ref, center_ref, units_ref):
    basis = basis_ref[...]
    offset = jnp.dot(center_ref[...], basis, preferred_element_type=F32)
    project(embeddings_ref, basis, offset, units_ref)


def project_pieces_kernel(spots, piece_rows, me_ref, embeddings_ref, gathered_ref, units_ref, basis_ref):
    tile = gathered_ref.shape[0] // len(spots)
    offset = None
    for q, mask in enumerate(spots):
        piece = gathered_ref[q * tile : q * tile + piece_rows]
        start = pl.multiple_of((me_ref[0] ^ mask) * piece_rows, piece_rows)
        basis_ref[pl.ds(start, piece_rows), :] = piece
        center = gathered_ref[q * tile + piece_rows : (q + 1) * tile, :piece_rows]
        part = jnp.dot(center, piece, preferred_element_type=F32)
        offset = part if offset is None else offset + part
    project(embeddings_ref, basis_ref[...], offset[:1], units_ref)


def slots_kernel(masks, me_ref, place_ref, units_ref, *out_refs):
    slot = out_refs[0].shape[0]
    rows = place_ref.shape[1]
    units = units_ref[...]
    for mask, out_ref in zip(masks, out_refs, strict=True):
        here = place_ref[...] - (me_ref[0] ^ mask) * slot
        spread = jnp.where(here == lax.broadcasted_iota(jnp.int32, (slot, rows), 0), 1.0, 0.0).astype(BF16)
        out_ref[...] = jnp.dot(spread, units, preferred_element_type=F32).astype(BF16)


def keys_kernel(masks, me_ref, keys_ref, row_ref, column_ref):
    slot = keys_ref.shape[1]
    for n, mask in enumerate(masks):
        keys = keys_ref[pl.ds(me_ref[0] ^ mask, 1), :]
        row_ref[:, n * slot : (n + 1) * slot] = keys
        column_ref[n * slot : (n + 1) * slot] = jnp.transpose(jnp.broadcast_to(keys, (128, slot)))


def pairs_kernel(starts, first, best_in_ref, row_ref, column_ref, *refs):
    *group_refs, best_ref, line_ref = refs
    new_ref = group_refs[-1]
    new_start = starts[len(group_refs) - 1]
    fresh = new_ref.shape[0]
    width = best_ref.shape[1]
    if first:
        best_ref[...] = jnp.full((1, width), -1.0, F32)
    else:
        best_ref[...] = best_in_ref[...]
    step = min(CHUNK, fresh)

    for t in range(fresh // step):
        rows = new_ref[t * step : (t + 1) * step]
        at = new_start + t * step
        key_col = column_ref[at : at + step]
        label_col = key_col // RANK_SPAN
        line_ref[...] = jnp.full(line_ref.shape, -1.0, F32)

        def pairs(others, lanes, both):
            cosines = lax.dot_general(rows, others, (((1,), (1,)), ((), ())), preferred_element_type=F32)
            for lane in range(0, others.shape[0], 128):
                key_row = row_ref[:, pl.ds(lanes + lane, 128)]
                label_row = key_row // RANK_SPAN
                down = None
                for s in range(0, step, 64):
                    c = cosines[s : s + 64, lane : lane + 128]
                    c = jnp.where(label_col[s : s + 64] == label_row, c, -1.0)
                    earlier = key_col[s : s + 64] < key_row
                    d = jnp.where(earlier, c, -1.0)
                    d = jnp.max(d.reshape(8, 8, 128), axis=0)
                    down = d if down is None else jnp.maximum(down, d)
                    if both:
                        line_ref[s : s + 64] = jnp.maximum(line_ref[s : s + 64], jnp.where(earlier, -1.0, c))
                here = pl.ds(lanes + lane, 128)
                best_ref[:, here] = jnp.maximum(best_ref[:, here], jnp.max(down, axis=0, keepdims=True))

        pairs(rows, at, False)
        for g, group_ref in enumerate(group_refs):
            count = t if g == len(group_refs) - 1 else group_ref.shape[0] // step
            if count:

                def one(i, carry, group_ref=group_ref, g=g):
                    start = pl.multiple_of(i * step, step)
                    pairs(group_ref[pl.ds(start, step), :], pl.multiple_of(starts[g] + start, 128), True)
                    return carry

                lax.fori_loop(0, count, one, 0)
        if t or len(group_refs) > 1:
            line = jnp.max(jnp.transpose(line_ref[...]), axis=0, keepdims=True)
            best_ref[:, at : at + step] = jnp.maximum(best_ref[:, at : at + step], line)


def back_kernel(masks, slot, place_ref, returned_ref, out_ref):
    peers = returned_ref.shape[0]
    place = place_ref[...]
    rows = place.shape[1]
    values = returned_ref[...]
    high = values.astype(BF16)
    rest = values - high.astype(F32)
    middle = rest.astype(BF16)
    low = (rest - middle.astype(F32)).astype(BF16)
    parts = jnp.concatenate([high, middle, low], axis=0)
    spread = jnp.where(place % slot == lax.broadcasted_iota(jnp.int32, (slot, rows), 0), 1.0, 0.0).astype(BF16)
    found = jnp.dot(parts, spread, preferred_element_type=F32)
    found = (found[:peers] + found[peers : 2 * peers]) + found[2 * peers :]
    out_ref[...] = jnp.sum(jnp.where(hits(place // slot, peers), found, 0.0), axis=0, keepdims=True)


def sds(shape, dtype):
    return jax.ShapeDtypeStruct(shape, dtype)


def shards(embeddings, pca_basis, pca_center, row_labels, row_ranks):
    peers = lax.axis_size("wide")
    me = lax.axis_index("wide").astype(jnp.int32).reshape(1)
    rows, depth = embeddings.shape
    width = pca_basis.shape[1]
    piece_rows = pca_basis.shape[0]
    slot = 2 * rows // peers
    order = masks_of(peers)
    masks = [0, *order]

    place, keys = call(
        functools.partial(places_kernel, peers, slot),
        (sds((1, rows), jnp.int32), sds((peers, slot), jnp.int32)),
        (row_labels.reshape(1, rows), row_ranks.reshape(1, rows)),
        flops=2 * 3 * peers * rows * slot,
    )
    got_keys = lax.all_to_all(keys, "wide", split_axis=0, concat_axis=0, tiled=True)

    cost = dict(flops=2 * rows * depth * width, moved=2 * rows * depth)
    if piece_rows % PIECE_TILE:
        basis = lax.all_gather(pca_basis, "wide", axis=0, tiled=True)
        center = lax.all_gather(pca_center, "wide", axis=0, tiled=True).reshape(1, depth)
        units = call(project_whole_kernel, sds((rows, width), BF16), (embeddings, basis, center), **cost)
    else:
        tail = jnp.zeros((PIECE_TILE, width), BF16).at[0, :piece_rows].set(pca_center)
        gathered = jnp.concatenate([pca_basis, tail], axis=0)
        spots = [0]
        bit = peers // 2
        while bit:
            gathered = jnp.concatenate([gathered, swap(gathered, bit, peers)], axis=0)
            spots = spots + [spot ^ bit for spot in spots]
            bit //= 2
        units = call(
            functools.partial(project_pieces_kernel, spots, piece_rows),
            sds((rows, width), BF16),
            (me, embeddings, gathered),
            scratch=[pltpu.VMEM((depth, width), BF16)],
            smem=(0,),
            **cost,
        )

    sent = []
    leading = min(IN_FLIGHT, len(order))
    for part in (order[:leading], order[leading:] + [0]):
        sent += call(
            functools.partial(slots_kernel, part),
            tuple(sds((slot, width), BF16) for _ in part),
            (me, place, units),
            smem=(0,),
            flops=2 * len(part) * slot * rows * width,
        )
    blocks = [sent[-1]]
    for n, mask in enumerate(order):
        block = sent[n]
        if n >= IN_FLIGHT:
            block, blocks[n - IN_FLIGHT + 1] = lax.optimization_barrier((block, blocks[n - IN_FLIGHT + 1]))
        blocks.append(swap(block, mask, peers))

    total = peers * slot
    key_row, key_column = call(
        functools.partial(keys_kernel, masks),
        (sds((1, total), jnp.int32), sds((total, 128), jnp.int32)),
        (me, got_keys),
        smem=(0,),
    )
    quarter, end = peers // 4, peers // 16
    cuts = [0, quarter, 2 * quarter, 3 * quarter, peers - end, peers]
    groups, starts = [], []
    best = jnp.zeros((1, total), F32)
    for lo, hi in zip(cuts[:-1], cuts[1:], strict=True):
        groups.append(jnp.concatenate(blocks[lo:hi], axis=0) if hi - lo > 1 else blocks[lo])
        starts.append(lo * slot)
        best = call(
            functools.partial(pairs_kernel, tuple(starts), lo == 0),
            sds((1, total), F32),
            (best, key_row, key_column, *groups),
            scratch=[pltpu.VMEM((min(CHUNK, (hi - lo) * slot), 128), F32)],
            flops=2 * (hi - lo) * slot * hi * slot * width,
        )
    best = best.reshape(peers, slot)
    source = jnp.bitwise_xor(me[0], jnp.asarray(masks, jnp.int32))
    best = jnp.zeros_like(best).at[source].set(best)
    returned = lax.all_to_all(best, "wide", split_axis=0, concat_axis=0, tiled=True)
    nearest = call(
        functools.partial(back_kernel, masks, slot),
        sds((1, rows), F32),
        (place, returned),
        flops=2 * 3 * peers * rows * slot,
    )
    return nearest.reshape(-1)


def solution(mesh):
    return jax.shard_map(
        shards,
        mesh=mesh,
        in_specs=(
            P(("groups", "wide"), None),
            P("wide", None),
            P("wide"),
            P(("groups", "wide")),
            P(("groups", "wide")),
        ),
        out_specs=P(("groups", "wide")),
        check_vma=False,
    )
```

time: 245 us -> 126 us (0.51)
  blocking collectives: 71 us -> 9.68 us
  local copies, waits for them, and re-layouts: 62 us -> 6.7 us
  Pallas kernels: 0 us -> 42.2 us
  matrix products: 36.9 us -> 0 us
  starting transfers between devices: 16.9 us -> 35.9 us
  waiting for transfers between devices: 41.1 us -> 27.3 us
  other arithmetic: 10.5 us -> 3.57 us
  loops' own time: 5.22 us -> 0 us
    pallas_call x0 -> x11, Pallas kernels: none -> 42.2 us  [call(): pl.pallas_call(kernel, out_shape=outs, in_specs=[SMEM if i in smem else V...]
    dot_general x10 -> x0, matrix products: 36.9 us -> none  [the longest x8 34.3 us: one_block(): lax.dot_general(queries, unit_rows, (((1,), (1,)), ((), ())), preferred_e...]
    all_to_all x3 -> x1, waiting for transfers between devices: 41.1 us -> 5.83 us  [shards(): lax.all_to_all(keys, 'wide', split_axis=0, concat_axis=0, tiled=True)]
    unnamed x1 -> x0, blocking collectives: 30.4 us -> none
    ppermute x0 -> x19, starting transfers between devices: none -> 29.6 us  [swap(): return lax.ppermute(x, 'wide', [(i, i ^ mask) for i in range(peers)])]
    scatter x3 -> x1, local copies, waits for them, and re-layouts: 28.8 us -> 0.65 us  [shards(): best = jnp.zeros_like(best).at[source].set(best)]
    all_gather x1 -> x0, blocking collectives: 23 us -> none  [project(): basis_piece = lax.all_gather(pca_basis, 'wide', axis=0, tiled=True)]
    ppermute x0 -> x19, waiting for transfers between devices: none -> 21.5 us  [swap(): return lax.ppermute(x, 'wide', [(i, i ^ mask) for i in range(peers)])]
  transfers between devices with their start and end apart: 3 -> 20, of which waited for: 1 -> 9; matrix products, arithmetic and copies ran while one was open for 13% -> 1% of each run, Pallas kernels for 0% -> 28%
where the time goes in v1:
time: 126 us
  Pallas kernels  42.2 us (33%)
  starting transfers between devices  35.9 us (28%)
  waiting for transfers between devices  27.3 us (22%)
  blocking collectives  9.68 us (8%)
  local copies, waits for them, and re-layouts  6.7 us (5%)
  other arithmetic  3.57 us (3%)
    pallas_call x11, Pallas kernels, call(): pl.pallas_call(kernel, out_shape=outs, in_specs=[SMEM if i in smem else V...  42.2 us
    ppermute x19, starting transfers between devices, swap(): return lax.ppermute(x, 'wide', [(i, i ^ mask) for i in range(peers)])  29.6 us
    ppermute x19, waiting for transfers between devices, swap(): return lax.ppermute(x, 'wide', [(i, i ^ mask) for i in range(peers)])  21.5 us
    all_to_all x1, blocking collectives, shards(): lax.all_to_all(best, 'wide', split_axis=0, concat_axis=0, tiled=True)  9.68 us
    all_to_all x1, starting transfers between devices, shards(): lax.all_to_all(keys, 'wide', split_axis=0, concat_axis=0, tiled=True)  6.26 us
    all_to_all x1, waiting for transfers between devices, shards(): lax.all_to_all(keys, 'wide', split_axis=0, concat_axis=0, tiled=True)  5.83 us
    unnamed x23, local copies, waits for them, and re-layouts  4.81 us
  transfers between devices with their start and end apart: 20, of which 9 were waited for; matrix products, arithmetic and copies ran while one was open for 1% of the time, Pallas kernels for 28%

profile of v1, /device:TPU:0, one launch (start us, length us, event | category | flops | bytes accessed | tf_op | source)
XLA Modules:
  0.0 125.6 jit_solution(15662780993059319434)
XLA Ops:
  2.1 4.0 %collective-permute-start = (bf16[64,256]{1,0:T(8,128)(2,1)S(1)}, bf16[64,256]{1,0:T(8,128)(2,1)S(1)}, u32[]{:S(2)}, u32[]{:S(2)}) collective-permute-start(bf16[64,256]{1,0:T(8,128)(2,1)S(1)} %pad_maximum_fusion.2), channel_id=1, source_target_pairs={{0,8},{1,9},{2,10},{3,11},{4,12},{5,13},{6,14},{7,15},{8,0},{9,1},... | collective-permute-start | bytes 98312 | tf_op jit(solution)/shard_map/ppermute | solution.py:45
  6.2 2.2 %collective-permute-done = bf16[64,256]{1,0:T(8,128)(2,1)S(1)} collective-permute-done((bf16[64,256]{1,0:T(8,128)(2,1)S(1)}, bf16[64,256]{1,0:T(8,128)(2,1)S(1)}, u32[]{:S(2)}, u32[]{:S(2)}) %collective-permute-start) | collective-permute-done | bytes 32800 | tf_op jit(solution)/shard_map/ppermute | solution.py:45
  10.7 2.7 %collective-permute-done.1 = bf16[128,256]{1,0:T(8,128)(2,1)S(1)} collective-permute-done((bf16[128,256]{1,0:T(8,128)(2,1)S(1)}, bf16[128,256]{1,0:T(8,128)(2,1)S(1)}, u32[]{:S(2)}, u32[]{:S(2)}) %collective-permute-start.1) | collective-permute-done | bytes 65568 | tf_op jit(solution)/shard_map/ppermute | solution.py:45
  14.2 1.8 %collective-permute-start.2 = (bf16[256,256]{1,0:T(8,128)(2,1)S(1)}, bf16[256,256]{1,0:T(8,128)(2,1)S(1)}, u32[]{:S(2)}, u32[]{:S(2)}) collective-permute-start(bf16[256,256]{1,0:T(8,128)(2,1)S(1)} %pad_maximum_fusion), channel_id=1, source_target_pairs={{0,2},{1,3},{2,0},{3,1},{4,6},{5,7},{6,4},{7,5},{8,10},{9,11},{10,... | collective-permute-start | bytes 393224 | tf_op jit(solution)/shard_map/ppermute | solution.py:45
  16.0 3.2 %collective-permute-done.2 = bf16[256,256]{1,0:T(8,128)(2,1)S(1)} collective-permute-done((bf16[256,256]{1,0:T(8,128)(2,1)S(1)}, bf16[256,256]{1,0:T(8,128)(2,1)S(1)}, u32[]{:S(2)}, u32[]{:S(2)}) %collective-permute-start.2) | collective-permute-done | bytes 131104 | tf_op jit(solution)/shard_map/ppermute | solution.py:45
  22.0 6.3 %all-to-all-start = ((s32[16,1,256]{2,1,0:T(1,128)}), s32[16,1,256]{2,1,0:T(1,128)S(1)}, u32[]{:S(2)}, u32[]{:S(2)}) async-start(s32[16,1,256]{2,1,0:T(1,128)} %copy.7), calls=%async_computation | async-start | bytes 32768 | tf_op jit(solution)/shard_map/all_to_all | solution.py:216
  28.9 5.8 %all-to-all-done = s32[16,1,256]{2,1,0:T(1,128)S(1)} async-done(((s32[16,1,256]{2,1,0:T(1,128)}), s32[16,1,256]{2,1,0:T(1,128)S(1)}, u32[]{:S(2)}, u32[]{:S(2)}) %all-to-all-start) | async-done | bytes 16416 | tf_op jit(solution)/shard_map/all_to_all | solution.py:216
  35.4 1.9 %copy-done = bf16[2048,768]{1,0:T(8,128)(2,1)S(1)} copy-done((bf16[2048,768]{1,0:T(8,128)(2,1)S(1)}, bf16[2048,768]{1,0:T(8,128)(2,1)}, u32[]{:S(2)}) %copy-start) | copy-done | bytes 3145752
  42.3 2.1 %collective-permute-start.7 = (bf16[256,256]{1,0:T(8,128)(2,1)S(1)}, bf16[256,256]{1,0:T(8,128)(2,1)S(1)}, u32[]{:S(2)}, u32[]{:S(2)}) collective-permute-start(bf16[256,256]{1,0:T(8,128)(2,1)S(1)} %get-tuple-element.74), channel_id=1, source_target_pairs={{0,5},{1,4},{2,7},{3,6},{4,1},{5,0},{6,3},{7,2},{8,13},{9,12},{10,... | collective-permute-start | bytes 393224 | tf_op jit(solution)/shard_map/ppermute | solution.py:45
  44.4 3.4 %shard_map.67 = (bf16[256,256]{1,0:T(8,128)(2,1)S(1)}, bf16[256,256]{1,0:T(8,128)(2,1)S(1)}, bf16[256,256]{1,0:T(8,128)(2,1)S(1)}, bf16[256,256]{1,0:T(8,128)(2,...) custom-call(s32[1]{0:T(128)} %bitcast.2.me_ref, ...), custom_call_target="tpu_custom_call" | custom-call | flops 3221225472 | tf_op jit(solution)/shard_map/pallas_call | solution.py:24
  47.9 3.2 %collective-permute-done.4 = bf16[256,256]{1,0:T(8,128)(2,1)S(1)} collective-permute-done((bf16[256,256]{1,0:T(8,128)(2,1)S(1)}, bf16[256,256]{1,0:T(8,128)(2,1)S(1)}, u32[]{:S(2)}, u32[]{:S(2)}) %collective-permute-start.4) | collective-permute-done | bytes 131104 | tf_op jit(solution)/shard_map/ppermute | solution.py:45
  51.1 2.8 %collective-permute-done.6 = bf16[256,256]{1,0:T(8,128)(2,1)S(1)} collective-permute-done((bf16[256,256]{1,0:T(8,128)(2,1)S(1)}, bf16[256,256]{1,0:T(8,128)(2,1)S(1)}, u32[]{:S(2)}, u32[]{:S(2)}) %collective-permute-start.6) | collective-permute-done | bytes 131104 | tf_op jit(solution)/shard_map/ppermute | solution.py:45
  57.0 3.4 %collective-permute-start.8 = (bf16[256,256]{1,0:T(8,128)(2,1)S(1)}, bf16[256,256]{1,0:T(8,128)(2,1)S(1)}, u32[]{:S(2)}, u32[]{:S(2)}) collective-permute-start(bf16[256,256]{1,0:T(8,128)(2,1)S(1)} %get-tuple-element.77), channel_id=1, source_target_pairs={{0,10},{1,11},{2,8},{3,9},{4,14},{5,15},{6,12},{7,13},{8,2},{9,3},... | collective-permute-start | bytes 393224 | tf_op jit(solution)/shard_map/ppermute | solution.py:45
  60.5 2.3 %shard_map.69.best_in_ref = f32[1,4096]{1,0:T(1,128)S(1)} custom-call(f32[1,4096]{1,0:T(1,128)S(1)} %broadcast_in_dim.12.best_in_ref, s32[1,4096]{1,0:T(1,128)S(1)} %get-tuple-element.61.row_ref, s32[4096,128]{1,0:T(8,128)S(1)} %get-tuple-element.62.column_ref, bf16[1024,256]{1,0:T(8,128)(2,1)S(1)} %constant_dynamic-update-slice_fusion.11.refs_0_), custom_call_target="tpu_custom_call" | custom-call | flops 536870912 | tf_op jit(solution)/shard_map/pallas_call | solution.py:24
  64.2 2.0 %collective-permute-start.14 = (bf16[256,256]{1,0:T(8,128)(2,1)S(1)}, bf16[256,256]{1,0:T(8,128)(2,1)S(1)}, u32[]{:S(2)}, u32[]{:S(2)}) collective-permute-start(bf16[256,256]{1,0:T(8,128)(2,1)S(1)} %get-tuple-element.95), channel_id=1, source_target_pairs={{0,13},{1,12},{2,15},{3,14},{4,9},{5,8},{6,11},{7,10},{8,5},{9,4},... | collective-permute-start | bytes 393224 | tf_op jit(solution)/shard_map/ppermute | solution.py:45
  66.2 2.1 %collective-permute-done.9 = bf16[256,256]{1,0:T(8,128)(2,1)S(1)} collective-permute-done((bf16[256,256]{1,0:T(8,128)(2,1)S(1)}, bf16[256,256]{1,0:T(8,128)(2,1)S(1)}, u32[]{:S(2)}, u32[]{:S(2)}) %collective-permute-start.9) | collective-permute-done | bytes 131104 | tf_op jit(solution)/shard_map/ppermute | solution.py:45
  68.3 4.9 %collective-permute-done.8 = bf16[256,256]{1,0:T(8,128)(2,1)S(1)} collective-permute-done((bf16[256,256]{1,0:T(8,128)(2,1)S(1)}, bf16[256,256]{1,0:T(8,128)(2,1)S(1)}, u32[]{:S(2)}, u32[]{:S(2)}) %collective-permute-start.8) | collective-permute-done | bytes 131104 | tf_op jit(solution)/shard_map/ppermute | solution.py:45
  73.2 6.6 %shard_map.70.best_in_ref = f32[1,4096]{1,0:T(1,128)S(1)} custom-call(f32[1,4096]{1,0:T(1,128)S(1)} %shard_map.69.best_in_ref, s32[1,4096]{1,0:T(1,128)S(1)} %get-tuple-element.61.row_ref, s32[4096,128]{1,0:T(8,128)S(1)} %get-tuple-element.62.column_ref, bf16[1024,256]{1,0:T(8,128)(2,1)S(1)} %constant_dynamic-update-slice_fusion.11.refs_0_, ...), custom_call_target="tpu_custom_call" | custom-call | flops 1073741824 | tf_op jit(solution)/shard_map/pallas_call | solution.py:24
  79.8 3.6 %collective-permute-start.18 = (bf16[256,256]{1,0:T(8,128)(2,1)S(1)}, bf16[256,256]{1,0:T(8,128)(2,1)S(1)}, u32[]{:S(2)}, u32[]{:S(2)}) collective-permute-start(bf16[256,256]{1,0:T(8,128)(2,1)S(1)} %get-tuple-element.100), channel_id=1, source_target_pairs={{0,15},{1,14},{2,13},{3,12},{4,11},{5,10},{6,9},{7,8},{8,7},{9,6},... | collective-permute-start | bytes 393224 | tf_op jit(solution)/shard_map/ppermute | solution.py:45
  84.9 2.7 %collective-permute-start.16 = (bf16[256,256]{1,0:T(8,128)(2,1)S(1)}, bf16[256,256]{1,0:T(8,128)(2,1)S(1)}, u32[]{:S(2)}, u32[]{:S(2)}) collective-permute-start(bf16[256,256]{1,0:T(8,128)(2,1)S(1)} %get-tuple-element.98), channel_id=1, source_target_pairs={{0,14},{1,15},{2,12},{3,13},{4,10},{5,11},{6,8},{7,9},{8,6},{9,7},... | collective-permute-start | bytes 393224 | tf_op jit(solution)/shard_map/ppermute | solution.py:45
  87.6 10.6 %shard_map.71.best_in_ref = f32[1,4096]{1,0:T(1,128)S(1)} custom-call(f32[1,4096]{1,0:T(1,128)S(1)} %shard_map.70.best_in_ref, s32[1,4096]{1,0:T(1,128)S(1)} %get-tuple-element.61.row_ref, s32[4096,128]{1,0:T(8,128)S(1)} %get-tuple-element.62.column_ref, bf16[1024,256]{1,0:T(8,128)(2,1)S(1)} %constant_dynamic-update-slice_fusion.11.refs_0_, ...), custom_call_target="tpu_custom_call" | custom-call | flops 1610612736 | tf_op jit(solution)/shard_map/pallas_call | solution.py:24
  98.4 10.6 %shard_map.72.best_in_ref = f32[1,4096]{1,0:T(1,128)S(1)} custom-call(f32[1,4096]{1,0:T(1,128)S(1)} %shard_map.71.best_in_ref, s32[1,4096]{1,0:T(1,128)S(1)} %get-tuple-element.61.row_ref, s32[4096,128]{1,0:T(8,128)S(1)} %get-tuple-element.62.column_ref, bf16[1024,256]{1,0:T(8,128)(2,1)S(1)} %constant_dynamic-update-slice_fusion.11.refs_0_, ...), custom_call_target="tpu_custom_call" | custom-call | flops 1509949440 | tf_op jit(solution)/shard_map/pallas_call | solution.py:24
  109.0 4.2 %shard_map.73 = f32[1,4096]{1,0:T(1,128)S(1)} custom-call(f32[1,4096]{1,0:T(1,128)S(1)} %shard_map.72.best_in_ref, s32[1,4096]{1,0:T(1,128)S(1)} %get-tuple-element.61.row_ref, s32[4096,128]{1,0:T(8,128)S(1)} %get-tuple-element.62.column_ref, bf16[1024,256]{1,0:T(8,128)(2,1)S(1)} %constant_dynamic-update-slice_fusion.11.refs_0_, ...), custom_call_target="tpu_custom_call" | custom-call | flops 536870912 | tf_op jit(solution)/shard_map/pallas_call | solution.py:24
  115.1 9.7 %all_to_all.22 = f32[16,1,256]{2,1,0:T(1,128)S(1)} all-to-all(f32[16,1,256]{2,1,0:T(1,128)S(1)} %all_to_all.17), channel_id=1, replica_groups=mesh['groups'=2,'wide'=16] {'wide'}, dimensions={0} | all-to-all | bytes 32768 | tf_op jit(solution)/shard_map/all_to_all | solution.py:282
  (68 shorter events, 23.2 us)
Async XLA Ops:
  2.1 6.3 %collective-permute-start = (bf16[64,256]{1,0:T(8,128)(2,1)S(1)}, bf16[64,256]{1,0:T(8,128)(2,1)S(1)}, u32[]{:S(2)}, u32[]{:S(2)}) collective-permute-start(bf16[64,256]{1,0:T(8,128)(2,1)S(1)} %pad_maximum_fusion.2), channel_id=1, source_target_pairs={{0,8},{1,9},{2,10},{3,11},{4,12},{5,13},{6,14},{7,15},{8,0},{9,1},... | collective-permute-start | bytes 98312 | tf_op jit(solution)/shard_map/ppermute | solution.py:45
  9.2 4.3 %collective-permute-start.1 = (bf16[128,256]{1,0:T(8,128)(2,1)S(1)}, bf16[128,256]{1,0:T(8,128)(2,1)S(1)}, u32[]{:S(2)}, u32[]{:S(2)}) collective-permute-start(bf16[128,256]{1,0:T(8,128)(2,1)S(1)} %pad_maximum_fusion.1), channel_id=1, source_target_pairs={{0,4},{1,5},{2,6},{3,7},{4,0},{5,1},{6,2},{7,3},{8,12},{9,13},{10,... | collective-permute-start | bytes 196616 | tf_op jit(solution)/shard_map/ppermute | solution.py:45
  14.2 5.0 %collective-permute-start.2 = (bf16[256,256]{1,0:T(8,128)(2,1)S(1)}, bf16[256,256]{1,0:T(8,128)(2,1)S(1)}, u32[]{:S(2)}, u32[]{:S(2)}) collective-permute-start(bf16[256,256]{1,0:T(8,128)(2,1)S(1)} %pad_maximum_fusion), channel_id=1, source_target_pairs={{0,2},{1,3},{2,0},{3,1},{4,6},{5,7},{6,4},{7,5},{8,10},{9,11},{10,... | collective-permute-start | bytes 393224 | tf_op jit(solution)/shard_map/ppermute | solution.py:45
  19.2 16.1 %collective-permute-start.3 = (bf16[512,256]{1,0:T(8,128)(2,1)S(1)}, bf16[512,256]{1,0:T(8,128)(2,1)S(1)}, u32[]{:S(2)}, u32[]{:S(2)}) collective-permute-start(bf16[512,256]{1,0:T(8,128)(2,1)S(1)} %get-tuple-element.101), channel_id=1, source_target_pairs={{0,1},{1,0},{2,3},{3,2},{4,5},{5,4},{6,7},{7,6},{8,9},{9,8},{10,11... | collective-permute-start | bytes 786440 | tf_op jit(solution)/shard_map/ppermute | solution.py:45
  19.3 0.7 copy-start.1
  20.0 0.7 copy-start.2
  22.0 12.8 %all-to-all-start = ((s32[16,1,256]{2,1,0:T(1,128)}), s32[16,1,256]{2,1,0:T(1,128)S(1)}, u32[]{:S(2)}, u32[]{:S(2)}) async-start(s32[16,1,256]{2,1,0:T(1,128)} %copy.7), calls=%async_computation | async-start | bytes 32768 | tf_op jit(solution)/shard_map/all_to_all | solution.py:216
  35.4 1.9 %copy-start = (bf16[2048,768]{1,0:T(8,128)(2,1)S(1)}, bf16[2048,768]{1,0:T(8,128)(2,1)}, u32[]{:S(2)}) copy-start(bf16[2048,768]{1,0:T(8,128)(2,1)} %embeddings_ref.1) | copy-start | bytes 9437188
  39.7 11.4 %collective-permute-start.4 = (bf16[256,256]{1,0:T(8,128)(2,1)S(1)}, bf16[256,256]{1,0:T(8,128)(2,1)S(1)}, u32[]{:S(2)}, u32[]{:S(2)}) collective-permute-start(bf16[256,256]{1,0:T(8,128)(2,1)S(1)} %get-tuple-element.65), channel_id=1, source_target_pairs={{0,8},{1,9},{2,10},{3,11},{4,12},{5,13},{6,14},{7,15},{8,0},{9,1},... | collective-permute-start | bytes 393224 | tf_op jit(solution)/shard_map/ppermute | solution.py:45
  40.2 10.9 %collective-permute-start.5 = (bf16[256,256]{1,0:T(8,128)(2,1)S(1)}, bf16[256,256]{1,0:T(8,128)(2,1)S(1)}, u32[]{:S(2)}, u32[]{:S(2)}) collective-permute-start(bf16[256,256]{1,0:T(8,128)(2,1)S(1)} %get-tuple-element.68), channel_id=1, source_target_pairs={{0,4},{1,5},{2,6},{3,7},{4,0},{5,1},{6,2},{7,3},{8,12},{9,13},{10,... | collective-permute-start | bytes 393224 | tf_op jit(solution)/shard_map/ppermute | solution.py:45
  40.8 13.1 %collective-permute-start.6 = (bf16[256,256]{1,0:T(8,128)(2,1)S(1)}, bf16[256,256]{1,0:T(8,128)(2,1)S(1)}, u32[]{:S(2)}, u32[]{:S(2)}) collective-permute-start(bf16[256,256]{1,0:T(8,128)(2,1)S(1)} %get-tuple-element.71), channel_id=1, source_target_pairs={{0,9},{1,8},{2,11},{3,10},{4,13},{5,12},{6,15},{7,14},{8,1},{9,0},... | collective-permute-start | bytes 393224 | tf_op jit(solution)/shard_map/ppermute | solution.py:45
  42.3 11.6 %collective-permute-start.7 = (bf16[256,256]{1,0:T(8,128)(2,1)S(1)}, bf16[256,256]{1,0:T(8,128)(2,1)S(1)}, u32[]{:S(2)}, u32[]{:S(2)}) collective-permute-start(bf16[256,256]{1,0:T(8,128)(2,1)S(1)} %get-tuple-element.74), channel_id=1, source_target_pairs={{0,5},{1,4},{2,7},{3,6},{4,1},{5,0},{6,3},{7,2},{8,13},{9,12},{10,... | collective-permute-start | bytes 393224 | tf_op jit(solution)/shard_map/ppermute | solution.py:45
  53.9 8.8 %collective-permute-start.11 = (bf16[256,256]{1,0:T(8,128)(2,1)S(1)}, bf16[256,256]{1,0:T(8,128)(2,1)S(1)}, u32[]{:S(2)}, u32[]{:S(2)}) collective-permute-start(bf16[256,256]{1,0:T(8,128)(2,1)S(1)} %get-tuple-element.86), channel_id=1, source_target_pairs={{0,7},{1,6},{2,5},{3,4},{4,3},{5,2},{6,1},{7,0},{8,15},{9,14},{10,... | collective-permute-start | bytes 393224 | tf_op jit(solution)/shard_map/ppermute | solution.py:45
  53.9 10.3 %collective-permute-start.10 = (bf16[256,256]{1,0:T(8,128)(2,1)S(1)}, bf16[256,256]{1,0:T(8,128)(2,1)S(1)}, u32[]{:S(2)}, u32[]{:S(2)}) collective-permute-start(bf16[256,256]{1,0:T(8,128)(2,1)S(1)} %get-tuple-element.83), channel_id=1, source_target_pairs={{0,11},{1,10},{2,9},{3,8},{4,15},{5,14},{6,13},{7,12},{8,3},{9,2},... | collective-permute-start | bytes 393224 | tf_op jit(solution)/shard_map/ppermute | solution.py:45
  55.6 12.7 %collective-permute-start.9 = (bf16[256,256]{1,0:T(8,128)(2,1)S(1)}, bf16[256,256]{1,0:T(8,128)(2,1)S(1)}, u32[]{:S(2)}, u32[]{:S(2)}) collective-permute-start(bf16[256,256]{1,0:T(8,128)(2,1)S(1)} %get-tuple-element.80), channel_id=1, source_target_pairs={{0,6},{1,7},{2,4},{3,5},{4,2},{5,3},{6,0},{7,1},{8,14},{9,15},{10,... | collective-permute-start | bytes 393224 | tf_op jit(solution)/shard_map/ppermute | solution.py:45
  57.0 16.1 %collective-permute-start.8 = (bf16[256,256]{1,0:T(8,128)(2,1)S(1)}, bf16[256,256]{1,0:T(8,128)(2,1)S(1)}, u32[]{:S(2)}, u32[]{:S(2)}) collective-permute-start(bf16[256,256]{1,0:T(8,128)(2,1)S(1)} %get-tuple-element.77), channel_id=1, source_target_pairs={{0,10},{1,11},{2,8},{3,9},{4,14},{5,15},{6,12},{7,13},{8,2},{9,3},... | collective-permute-start | bytes 393224 | tf_op jit(solution)/shard_map/ppermute | solution.py:45
  62.8 35.5 %collective-permute-start.15 = (bf16[256,256]{1,0:T(8,128)(2,1)S(1)}, bf16[256,256]{1,0:T(8,128)(2,1)S(1)}, u32[]{:S(2)}, u32[]{:S(2)}) collective-permute-start(bf16[256,256]{1,0:T(8,128)(2,1)S(1)} %get-tuple-element.97), channel_id=1, source_target_pairs={{0,2},{1,3},{2,0},{3,1},{4,6},{5,7},{6,4},{7,5},{8,10},{9,11},{10,... | collective-permute-start | bytes 393224 | tf_op jit(solution)/shard_map/ppermute | solution.py:45
  64.2 15.6 %collective-permute-start.14 = (bf16[256,256]{1,0:T(8,128)(2,1)S(1)}, bf16[256,256]{1,0:T(8,128)(2,1)S(1)}, u32[]{:S(2)}, u32[]{:S(2)}) collective-permute-start(bf16[256,256]{1,0:T(8,128)(2,1)S(1)} %get-tuple-element.95), channel_id=1, source_target_pairs={{0,13},{1,12},{2,15},{3,14},{4,9},{5,8},{6,11},{7,10},{8,5},{9,4},... | collective-permute-start | bytes 393224 | tf_op jit(solution)/shard_map/ppermute | solution.py:45
  68.2 15.1 %collective-permute-start.13 = (bf16[256,256]{1,0:T(8,128)(2,1)S(1)}, bf16[256,256]{1,0:T(8,128)(2,1)S(1)}, u32[]{:S(2)}, u32[]{:S(2)}) collective-permute-start(bf16[256,256]{1,0:T(8,128)(2,1)S(1)} %get-tuple-element.92), channel_id=1, source_target_pairs={{0,1},{1,0},{2,3},{3,2},{4,5},{5,4},{6,7},{7,6},{8,9},{9,8},{10,11... | collective-permute-start | bytes 393224 | tf_op jit(solution)/shard_map/ppermute | solution.py:45
  73.1 11.7 %collective-permute-start.12 = (bf16[256,256]{1,0:T(8,128)(2,1)S(1)}, bf16[256,256]{1,0:T(8,128)(2,1)S(1)}, u32[]{:S(2)}, u32[]{:S(2)}) collective-permute-start(bf16[256,256]{1,0:T(8,128)(2,1)S(1)} %get-tuple-element.89), channel_id=1, source_target_pairs={{0,12},{1,13},{2,14},{3,15},{4,8},{5,9},{6,10},{7,11},{8,4},{9,5},... | collective-permute-start | bytes 393224 | tf_op jit(solution)/shard_map/ppermute | solution.py:45
  79.8 29.2 %collective-permute-start.18 = (bf16[256,256]{1,0:T(8,128)(2,1)S(1)}, bf16[256,256]{1,0:T(8,128)(2,1)S(1)}, u32[]{:S(2)}, u32[]{:S(2)}) collective-permute-start(bf16[256,256]{1,0:T(8,128)(2,1)S(1)} %get-tuple-element.100), channel_id=1, source_target_pairs={{0,15},{1,14},{2,13},{3,12},{4,11},{5,10},{6,9},{7,8},{8,7},{9,6},... | collective-permute-start | bytes 393224 | tf_op jit(solution)/shard_map/ppermute | solution.py:45
  83.4 14.9 %collective-permute-start.17 = (bf16[256,256]{1,0:T(8,128)(2,1)S(1)}, bf16[256,256]{1,0:T(8,128)(2,1)S(1)}, u32[]{:S(2)}, u32[]{:S(2)}) collective-permute-start(bf16[256,256]{1,0:T(8,128)(2,1)S(1)} %get-tuple-element.99), channel_id=1, source_target_pairs={{0,3},{1,2},{2,1},{3,0},{4,7},{5,6},{6,5},{7,4},{8,11},{9,10},{10,... | collective-permute-start | bytes 393224 | tf_op jit(solution)/shard_map/ppermute | solution.py:45
  84.9 13.4 %collective-permute-start.16 = (bf16[256,256]{1,0:T(8,128)(2,1)S(1)}, bf16[256,256]{1,0:T(8,128)(2,1)S(1)}, u32[]{:S(2)}, u32[]{:S(2)}) collective-permute-start(bf16[256,256]{1,0:T(8,128)(2,1)S(1)} %get-tuple-element.98), channel_id=1, source_target_pairs={{0,14},{1,15},{2,12},{3,13},{4,10},{5,11},{6,8},{7,9},{8,6},{9,7},... | collective-permute-start | bytes 393224 | tf_op jit(solution)/shard_map/ppermute | solution.py:45

commit v2 on v1

--- a/solution.py
+++ b/solution.py
@@ -74,7 +74,13 @@
     spread = jnp.where(within == lax.broadcasted_iota(jnp.int32, (slot, rows), 0), 1.0, 0.0).astype(BF16)
     parts = jnp.concatenate([hit_f * high, hit_f * low], axis=0).astype(BF16)
     slots = lax.dot_general(parts, spread, (((1,), (1,)), ((), ())), preferred_element_type=F32)
-    keys_ref[...] = (slots[:peers] * KEY_LOW + slots[peers:]).astype(jnp.int32)
+    keys_ref[...] = (slots[:peers] * KEY_LOW + slots[peers:]).astype(jnp.int32).reshape(peers, 1, slot)
+
+
+def stage_kernel(embeddings_ref, staged_ref, semaphore):
+    copy = pltpu.make_async_copy(embeddings_ref, staged_ref, semaphore)
+    copy.start()
+    copy.wait()
 
 
 def project(embeddings_ref, basis, offset, units_ref):
@@ -117,71 +123,144 @@
 
 
 def keys_kernel(masks, me_ref, keys_ref, row_ref, column_ref):
-    slot = keys_ref.shape[1]
+    slot = keys_ref.shape[2]
     for n, mask in enumerate(masks):
-        keys = keys_ref[pl.ds(me_ref[0] ^ mask, 1), :]
+        keys = keys_ref[me_ref[0] ^ mask]
         row_ref[:, n * slot : (n + 1) * slot] = keys
         column_ref[n * slot : (n + 1) * slot] = jnp.transpose(jnp.broadcast_to(keys, (128, slot)))
 
 
-def pairs_kernel(starts, first, best_in_ref, row_ref, column_ref, *refs):
-    *group_refs, best_ref, line_ref = refs
-    new_ref = group_refs[-1]
-    new_start = starts[len(group_refs) - 1]
-    fresh = new_ref.shape[0]
-    width = best_ref.shape[1]
-    if first:
-        best_ref[...] = jnp.full((1, width), -1.0, F32)
-    else:
-        best_ref[...] = best_in_ref[...]
-    step = min(CHUNK, fresh)
-
-    for t in range(fresh // step):
-        rows = new_ref[t * step : (t + 1) * step]
-        at = new_start + t * step
-        key_col = column_ref[at : at + step]
-        label_col = key_col // RANK_SPAN
-        line_ref[...] = jnp.full(line_ref.shape, -1.0, F32)
-
-        def pairs(others, lanes, both):
-            cosines = lax.dot_general(rows, others, (((1,), (1,)), ((), ())), preferred_element_type=F32)
-            for lane in range(0, others.shape[0], 128):
-                key_row = row_ref[:, pl.ds(lanes + lane, 128)]
-                label_row = key_row // RANK_SPAN
-                down = None
-                for s in range(0, step, 64):
-                    c = cosines[s : s + 64, lane : lane + 128]
-                    c = jnp.where(label_col[s : s + 64] == label_row, c, -1.0)
-                    earlier = key_col[s : s + 64] < key_row
-                    d = jnp.where(earlier, c, -1.0)
-                    d = jnp.max(d.reshape(8, 8, 128), axis=0)
-                    down = d if down is None else jnp.maximum(down, d)
-                    if both:
-                        line_ref[s : s + 64] = jnp.maximum(line_ref[s : s + 64], jnp.where(earlier, -1.0, c))
-                here = pl.ds(lanes + lane, 128)
-                best_ref[:, here] = jnp.maximum(best_ref[:, here], jnp.max(down, axis=0, keepdims=True))
-
-        pairs(rows, at, False)
-        for g, group_ref in enumerate(group_refs):
-            count = t if g == len(group_refs) - 1 else group_ref.shape[0] // step
-            if count:
-
-                def one(i, carry, group_ref=group_ref, g=g):
-                    start = pl.multiple_of(i * step, step)
-                    pairs(group_ref[pl.ds(start, step), :], pl.multiple_of(starts[g] + start, 128), True)
-                    return carry
-
-                lax.fori_loop(0, count, one, 0)
-        if t or len(group_refs) > 1:
-            line = jnp.max(jnp.transpose(line_ref[...]), axis=0, keepdims=True)
-            best_ref[:, at : at + step] = jnp.maximum(best_ref[:, at : at + step], line)
-
-
-def back_kernel(masks, slot, place_ref, returned_ref, out_ref):
+def best_of(cosine, key_col, label_col, key_row, label_row, below, beside):
+    cosine = jnp.where(label_col == label_row, cosine, -1.0)
+    earlier = key_col < key_row
+    below = jnp.maximum(below, jnp.where(earlier, cosine, -1.0))
+    if beside is not None:
+        beside = jnp.maximum(beside, jnp.where(earlier, -1.0, cosine))
+    return below, beside
+
+
+def turned(line):
+    return jnp.max(jnp.transpose(line), axis=0, keepdims=True)
+
+
+def group_kernel(starts, last, *refs):
+    olds = len(starts) - 1
+    refs = list(refs)
+    row_ref, column_ref = refs[:2]
+    old_refs, new_ref = refs[2 : 2 + olds], refs[2 + olds]
+    rest = refs[3 + olds :]
+    best_in_ref = rest.pop(0) if olds else None
+    line_in_ref = rest.pop(0) if olds > 1 else None
+    best_ref = rest.pop(0)
+    line_ref = rest.pop(0) if olds else None
+    cosines_ref, turned_ref, all_ref = rest
+    new_start, fresh = starts[-1], new_ref.shape[0]
+    tiles = fresh // 128
+    for t in range(0, fresh, 128):
+        turned_ref[:, t : t + 128] = jnp.transpose(new_ref[t : t + 128].astype(F32)).astype(BF16)
+    for start, old_ref in zip(starts[:-1], old_refs, strict=True):
+        all_ref[start : start + old_ref.shape[0]] = old_ref[...]
+    key_rows = [row_ref[:, new_start + t * 128 : new_start + (t + 1) * 128] for t in range(tiles)]
+    label_rows = [key_row // RANK_SPAN for key_row in key_rows]
+
+    def products(rows, buffer):
+        cosines_ref[buffer, : rows.shape[0]] = jnp.dot(rows, turned_ref[...], preferred_element_type=F32)
+
+    def maxima(at, step, line_from, buffer, below, keep):
+        below = list(below)
+        for s in range(0, step, 8):
+            here = pl.ds(at + s, 8)
+            key_col = column_ref[here, :]
+            label_col = key_col // RANK_SPAN
+            beside = None
+            if keep:
+                beside = jnp.full((8, 128), -1.0, F32) if line_from is None else line_from[here, :]
+            for t in range(tiles):
+                cosine = cosines_ref[buffer, s : s + 8, t * 128 : (t + 1) * 128]
+                below[t], beside = best_of(
+                    cosine, key_col, label_col, key_rows[t], label_rows[t], below[t], beside
+                )
+            if keep:
+                line_ref[here, :] = beside
+        return tuple(below)
+
+    def sweep(rows_ref, lo, hi, shift, line_from, keep, below):
+        step = CHUNK
+        while (hi - lo) % (2 * step):
+            step //= 2
+
+        def two(i, below):
+            at = pl.multiple_of(lo + i * 2 * step, step)
+            products(rows_ref[pl.ds(at + step, step), :], 1)
+            below = maxima(at + shift, step, line_from, 0, below, keep)
+            after = pl.multiple_of(jnp.minimum(at + 2 * step, hi - step), step)
+            products(rows_ref[pl.ds(after, step), :], 0)
+            return maxima(at + step + shift, step, line_from, 1, below, keep)
+
+        products(rows_ref[lo : lo + step], 0)
+        return lax.fori_loop(0, (hi - lo) // (2 * step), two, below)
+
+    below = tuple(jnp.full((8, 128), -1.0, F32) for _ in range(tiles))
+    below = sweep(new_ref, 0, fresh, new_start, None, False, below)
+    known = starts[-2] if olds > 1 else 0
+    if known:
+        below = sweep(all_ref, 0, known, 0, line_in_ref, True, below)
+    if olds:
+        below = sweep(all_ref, known, new_start, 0, None, True, below)
+    best_ref[...] = jnp.full(best_ref.shape, -1.0, F32)
+    if olds:
+        best_ref[:, :new_start] = best_in_ref[:, :new_start]
+    for t in range(tiles):
+        here = slice(new_start + t * 128, new_start + (t + 1) * 128)
+        best_ref[:, here] = jnp.max(below[t], axis=0, keepdims=True)
+    if last:
+        for at in range(0, new_start, 128):
+            here = slice(at, at + 128)
+            best_ref[:, here] = jnp.maximum(best_ref[:, here], turned(line_ref[here]))
+
+
+def end_kernel(masks, starts, me_ref, best_in_ref, row_ref, column_ref, *refs):
+    *old_refs, new_ref, best_ref, line_ref, all_ref = refs
+    new_start, fresh = starts[-1], new_ref.shape[0]
+    slot = best_ref.shape[2]
+    new = new_ref[...]
+    line_ref[...] = jnp.full(line_ref.shape, -1.0, F32)
+    all_ref[...] = best_in_ref[...]
+    for start, old_ref in zip(starts, [*old_refs, new_ref], strict=True):
+        both = start < new_start
+        for at in range(0, old_ref.shape[0], CHUNK):
+            others = old_ref[at : at + CHUNK]
+            cosines = lax.dot_general(new, others, (((1,), (1,)), ((), ())), preferred_element_type=F32)
+            tiles = range(0, others.shape[0], 128)
+            key_rows = [row_ref[:, start + at + t : start + at + t + 128] for t in tiles]
+            label_rows = [key_row // RANK_SPAN for key_row in key_rows]
+            below = [jnp.full((8, 128), -1.0, F32)] * len(tiles)
+            for s in range(0, fresh, 8):
+                key_col = column_ref[new_start + s : new_start + s + 8]
+                label_col = key_col // RANK_SPAN
+                beside = line_ref[s : s + 8] if both else None
+                for n, t in enumerate(tiles):
+                    below[n], beside = best_of(
+                        cosines[s : s + 8, t : t + 128],
+                        key_col, label_col, key_rows[n], label_rows[n], below[n], beside,
+                    )
+                if both:
+                    line_ref[s : s + 8] = beside
+            for n, t in enumerate(tiles):
+                here = slice(start + at + t, start + at + t + 128)
+                all_ref[:, here] = jnp.maximum(all_ref[:, here], jnp.max(below[n], axis=0, keepdims=True))
+    for s in range(0, fresh, 128):
+        here = slice(new_start + s, new_start + s + 128)
+        all_ref[:, here] = jnp.maximum(all_ref[:, here], turned(line_ref[s : s + 128]))
+    for n, mask in enumerate(masks):
+        best_ref[me_ref[0] ^ mask] = all_ref[:, n * slot : (n + 1) * slot]
+
+
+def back_kernel(slot, place_ref, returned_ref, out_ref):
     peers = returned_ref.shape[0]
     place = place_ref[...]
     rows = place.shape[1]
-    values = returned_ref[...]
+    values = returned_ref[...].reshape(peers, slot)
     high = values.astype(BF16)
     rest = values - high.astype(F32)
     middle = rest.astype(BF16)
@@ -201,38 +280,53 @@
     peers = lax.axis_size("wide")
     me = lax.axis_index("wide").astype(jnp.int32).reshape(1)
     rows, depth = embeddings.shape
-    width = pca_basis.shape[1]
-    piece_rows = pca_basis.shape[0]
+    piece_rows, width = pca_basis.shape
     slot = 2 * rows // peers
+    total = peers * slot
     order = masks_of(peers)
     masks = [0, *order]
 
     place, keys = call(
         functools.partial(places_kernel, peers, slot),
-        (sds((1, rows), jnp.int32), sds((peers, slot), jnp.int32)),
+        (sds((1, rows), jnp.int32), sds((peers, 1, slot), jnp.int32)),
         (row_labels.reshape(1, rows), row_ranks.reshape(1, rows)),
         flops=2 * 3 * peers * rows * slot,
     )
-    got_keys = lax.all_to_all(keys, "wide", split_axis=0, concat_axis=0, tiled=True)
+    staged = pl.pallas_call(
+        stage_kernel,
+        out_shape=sds((rows, depth), BF16),
+        in_specs=[pl.BlockSpec(memory_space=pl.ANY)],
+        out_specs=VMEM,
+        scratch_shapes=[pltpu.SemaphoreType.DMA],
+        compiler_params=pltpu.CompilerParams(vmem_limit_bytes=VMEM_BYTES),
+        cost_estimate=pl.CostEstimate(flops=0, bytes_accessed=4 * rows * depth, transcendentals=0),
+    )(embeddings)
 
     cost = dict(flops=2 * rows * depth * width, moved=2 * rows * depth)
     if piece_rows % PIECE_TILE:
         basis = lax.all_gather(pca_basis, "wide", axis=0, tiled=True)
         center = lax.all_gather(pca_center, "wide", axis=0, tiled=True).reshape(1, depth)
-        units = call(project_whole_kernel, sds((rows, width), BF16), (embeddings, basis, center), **cost)
+        units = call(project_whole_kernel, sds((rows, width), BF16), (staged, basis, center), **cost)
     else:
-        tail = jnp.zeros((PIECE_TILE, width), BF16).at[0, :piece_rows].set(pca_center)
-        gathered = jnp.concatenate([pca_basis, tail], axis=0)
+        tail = jnp.pad(pca_center.reshape(1, piece_rows), ((0, PIECE_TILE - 1), (0, width - piece_rows)))
+        gathered = lax.optimization_barrier(jnp.concatenate([pca_basis, tail], axis=0))
         spots = [0]
         bit = peers // 2
+        beside = [(place, keys), (staged,)]
         while bit:
             gathered = jnp.concatenate([gathered, swap(gathered, bit, peers)], axis=0)
+            if beside:
+                gathered, *tied = lax.optimization_barrier((gathered, *beside.pop(0)))
+                if len(tied) == 2:
+                    place, keys = tied
+                else:
+                    (staged,) = tied
             spots = spots + [spot ^ bit for spot in spots]
             bit //= 2
         units = call(
             functools.partial(project_pieces_kernel, spots, piece_rows),
             sds((rows, width), BF16),
-            (me, embeddings, gathered),
+            (me, staged, gathered),
             scratch=[pltpu.VMEM((depth, width), BF16)],
             smem=(0,),
             **cost,
@@ -248,6 +342,8 @@
             smem=(0,),
             flops=2 * len(part) * slot * rows * width,
         )
+    keys, sent[-1] = lax.optimization_barrier((keys, sent[-1]))
+    got_keys = lax.all_to_all(keys, "wide", split_axis=0, concat_axis=0, tiled=True)
     blocks = [sent[-1]]
     for n, mask in enumerate(order):
         block = sent[n]
@@ -255,7 +351,6 @@
             block, blocks[n - IN_FLIGHT + 1] = lax.optimization_barrier((block, blocks[n - IN_FLIGHT + 1]))
         blocks.append(swap(block, mask, peers))
 
-    total = peers * slot
     key_row, key_column = call(
         functools.partial(keys_kernel, masks),
         (sds((1, total), jnp.int32), sds((total, 128), jnp.int32)),
@@ -264,24 +359,37 @@
     )
     quarter, end = peers // 4, peers // 16
     cuts = [0, quarter, 2 * quarter, 3 * quarter, peers - end, peers]
-    groups, starts = [], []
-    best = jnp.zeros((1, total), F32)
+    groups, starts, state = [], [], ()
     for lo, hi in zip(cuts[:-1], cuts[1:], strict=True):
-        groups.append(jnp.concatenate(blocks[lo:hi], axis=0) if hi - lo > 1 else blocks[lo])
+        group = jnp.concatenate(blocks[lo:hi], axis=0) if hi - lo > 1 else blocks[lo]
+        groups.append(group)
         starts.append(lo * slot)
-        best = call(
-            functools.partial(pairs_kernel, tuple(starts), lo == 0),
-            sds((1, total), F32),
-            (best, key_row, key_column, *groups),
-            scratch=[pltpu.VMEM((min(CHUNK, (hi - lo) * slot), 128), F32)],
-            flops=2 * (hi - lo) * slot * hi * slot * width,
-        )
-    best = best.reshape(peers, slot)
-    source = jnp.bitwise_xor(me[0], jnp.asarray(masks, jnp.int32))
-    best = jnp.zeros_like(best).at[source].set(best)
+        fresh = (hi - lo) * slot
+        flops = 2 * fresh * hi * slot * width
+        if hi < peers:
+            state = call(
+                functools.partial(group_kernel, tuple(starts), hi == peers - end),
+                (sds((1, total), F32), *([sds((lo * slot, 128), F32)] if lo else [])),
+                (key_row, key_column, *groups, *state),
+                scratch=[
+                    pltpu.VMEM((2, CHUNK, fresh), F32),
+                    pltpu.VMEM((width, fresh), BF16),
+                    pltpu.VMEM((max(lo * slot, 16), width), BF16),
+                ],
+                flops=flops,
+            )
+        else:
+            best = call(
+                functools.partial(end_kernel, masks, tuple(starts)),
+                sds((peers, 1, slot), F32),
+                (me, state[0], key_row, key_column, *groups),
+                scratch=[pltpu.VMEM((fresh, 128), F32), pltpu.VMEM((1, total), F32)],
+                smem=(0,),
+                flops=flops,
+            )
     returned = lax.all_to_all(best, "wide", split_axis=0, concat_axis=0, tiled=True)
     nearest = call(
-        functools.partial(back_kernel, masks, slot),
+        functools.partial(back_kernel, slot),
         sds((1, rows), F32),
         (place, returned),
         flops=2 * 3 * peers * rows * slot,

time: 126 us -> 105 us (0.83)
  Pallas kernels: 42.2 us -> 32.4 us
  waiting for transfers between devices: 27.3 us -> 21.5 us
  local copies, waits for them, and re-layouts: 6.7 us -> 1.56 us
    pallas_call x11, Pallas kernels: 42.2 us -> 30.5 us  [call(): pl.pallas_call(kernel, out_shape=outs, in_specs=[SMEM if i in smem else V...]
    ppermute x19, waiting for transfers between devices: 21.5 us -> 15 us  [swap(): return lax.ppermute(x, 'wide', [(i, i ^ mask) for i in range(peers)])]
    unnamed x23 -> x19, local copies, waits for them, and re-layouts: 4.81 us -> 1.52 us
    pallas_call x0 -> x1, Pallas kernels: none -> 1.9 us  [shards(): pl.pallas_call(stage_kernel, out_shape=sds((rows, depth), BF16), in_specs...]
  transfers between devices with their start and end apart: 20 -> 20, of which waited for: 9 -> 7; matrix products, arithmetic and copies ran while one was open for 1% -> 0% of each run, Pallas kernels for 28% -> 26%
where the time goes in v2:
time: 105 us; the launch traced here: 104 us
  starting transfers between devices  35.4 us (34%)
  Pallas kernels  32.4 us (31%)
  waiting for transfers between devices  21.5 us (20%)
  blocking collectives  10.5 us (10%)
  other arithmetic  2.48 us (2%)
  local copies, waits for them, and re-layouts  1.56 us (1%)
    pallas_call x11, Pallas kernels, call(): pl.pallas_call(kernel, out_shape=outs, in_specs=[SMEM if i in smem else V...  30.5 us
    ppermute x19, starting transfers between devices, swap(): return lax.ppermute(x, 'wide', [(i, i ^ mask) for i in range(peers)])  29.7 us
    ppermute x19, waiting for transfers between devices, swap(): return lax.ppermute(x, 'wide', [(i, i ^ mask) for i in range(peers)])  15 us
    all_to_all x1, blocking collectives, shards(): lax.all_to_all(best, 'wide', split_axis=0, concat_axis=0, tiled=True)  10.5 us
    all_to_all x1, waiting for transfers between devices, shards(): lax.all_to_all(keys, 'wide', split_axis=0, concat_axis=0, tiled=True)  6.47 us
    all_to_all x1, starting transfers between devices, shards(): lax.all_to_all(keys, 'wide', split_axis=0, concat_axis=0, tiled=True)  5.7 us
  transfers between devices with their start and end apart: 20, of which 7 were waited for; matrix products, arithmetic and copies ran while one was open for 0% of the time, Pallas kernels for 26%

profile of v2, /device:TPU:0, one launch (start us, length us, event | category | flops | bytes accessed | tf_op | source)
XLA Modules:
  0.0 104.1 jit_solution(4441563274426169496)
XLA Ops:
  0.8 4.0 %collective-permute-start = (bf16[64,256]{1,0:T(8,128)(2,1)S(1)}, bf16[64,256]{1,0:T(8,128)(2,1)S(1)}, u32[]{:S(2)}, u32[]{:S(2)}) collective-permute-start(bf16[64,256]{1,0:T(8,128)(2,1)S(1)} %fusion.1), channel_id=1, source_target_pairs={{0,8},{1,9},{2,10},{3,11},{4,12},{5,13},{6,14},{7,15},{8,0},{9,1},... | collective-permute-start | bytes 98312 | tf_op jit(solution)/shard_map/ppermute | solution.py:45
  7.5 1.6 %collective-permute-start.1 = (bf16[128,256]{1,0:T(8,128)(2,1)S(1)}, bf16[128,256]{1,0:T(8,128)(2,1)S(1)}, u32[]{:S(2)}, u32[]{:S(2)}) collective-permute-start(bf16[128,256]{1,0:T(8,128)(2,1)S(1)} %pad_maximum_fusion.3), channel_id=1, source_target_pairs={{0,4},{1,5},{2,6},{3,7},{4,0},{5,1},{6,2},{7,3},{8,12},{9,13},{10,... | collective-permute-start | bytes 196616 | tf_op jit(solution)/shard_map/ppermute | solution.py:45
  9.1 1.9 %shard_map.56.embeddings_ref = bf16[2048,768]{1,0:T(8,128)(2,1)S(1)} custom-call(bf16[2048,768]{1,0:T(8,128)(2,1)} %embeddings_ref.1), custom_call_target="tpu_custom_call" | custom-call | bytes 6291456 | tf_op jit(solution)/shard_map/pallas_call | solution.py:295
  11.8 1.6 %collective-permute-start.2 = (bf16[256,256]{1,0:T(8,128)(2,1)S(1)}, bf16[256,256]{1,0:T(8,128)(2,1)S(1)}, u32[]{:S(2)}, u32[]{:S(2)}) collective-permute-start(bf16[256,256]{1,0:T(8,128)(2,1)S(1)} %pad_maximum_fusion.2), channel_id=1, source_target_pairs={{0,2},{1,3},{2,0},{3,1},{4,6},{5,7},{6,4},{7,5},{8,10},{9,11},{10,... | collective-permute-start | bytes 393224 | tf_op jit(solution)/shard_map/ppermute | solution.py:45
  13.4 3.4 %collective-permute-done.2 = bf16[256,256]{1,0:T(8,128)(2,1)S(1)} collective-permute-done((bf16[256,256]{1,0:T(8,128)(2,1)S(1)}, bf16[256,256]{1,0:T(8,128)(2,1)S(1)}, u32[]{:S(2)}, u32[]{:S(2)}) %collective-permute-start.2) | collective-permute-done | bytes 131104 | tf_op jit(solution)/shard_map/ppermute | solution.py:45
  17.6 1.9 %collective-permute-done.3 = bf16[512,256]{1,0:T(8,128)(2,1)} collective-permute-done((bf16[512,256]{1,0:T(8,128)(2,1)}, bf16[512,256]{1,0:T(8,128)(2,1)}, u32[]{:S(2)}, u32[]{:S(2)}) %collective-permute-start.3) | collective-permute-done | bytes 262176 | tf_op jit(solution)/shard_map/ppermute | solution.py:45
  22.8 2.2 %collective-permute-start.4 = (bf16[256,256]{1,0:T(8,128)(2,1)S(1)}, bf16[256,256]{1,0:T(8,128)(2,1)S(1)}, u32[]{:S(2)}, u32[]{:S(2)}) collective-permute-start(bf16[256,256]{1,0:T(8,128)(2,1)S(1)} %get-tuple-element.72), channel_id=1, source_target_pairs={{0,8},{1,9},{2,10},{3,11},{4,12},{5,13},{6,14},{7,15},{8,0},{9,1},... | collective-permute-start | bytes 393224 | tf_op jit(solution)/shard_map/ppermute | solution.py:45
  25.0 1.8 %collective-permute-start.5 = (bf16[256,256]{1,0:T(8,128)(2,1)S(1)}, bf16[256,256]{1,0:T(8,128)(2,1)S(1)}, u32[]{:S(2)}, u32[]{:S(2)}) collective-permute-start(bf16[256,256]{1,0:T(8,128)(2,1)S(1)} %get-tuple-element.75), channel_id=1, source_target_pairs={{0,4},{1,5},{2,6},{3,7},{4,0},{5,1},{6,2},{7,3},{8,12},{9,13},{10,... | collective-permute-start | bytes 393224 | tf_op jit(solution)/shard_map/ppermute | solution.py:45
  27.6 3.4 %shard_map.58 = (bf16[256,256]{1,0:T(8,128)(2,1)S(1)}, bf16[256,256]{1,0:T(8,128)(2,1)S(1)}, bf16[256,256]{1,0:T(8,128)(2,1)S(1)}, bf16[256,256]{1,0:T(8,128)(2,...) custom-call(s32[1]{0:T(128)} %bitcast.3.me_ref, ...), custom_call_target="tpu_custom_call" | custom-call | flops 3221225472 | tf_op jit(solution)/shard_map/pallas_call | solution.py:24
  31.0 5.7 %all-to-all-start = ((s32[16,1,256]{2,1,0:T(1,128)}), s32[16,1,256]{2,1,0:T(1,128)S(1)}, u32[]{:S(2)}, u32[]{:S(2)}) async-start(s32[16,1,256]{2,1,0:T(1,128)} %get-tuple-element.67), calls=%async_computation | async-start | bytes 32768 | tf_op jit(solution)/shard_map/all_to_all | solution.py:346
  36.7 6.5 %all-to-all-done.keys_ref = s32[16,1,256]{2,1,0:T(1,128)S(1)} async-done(((s32[16,1,256]{2,1,0:T(1,128)}), s32[16,1,256]{2,1,0:T(1,128)S(1)}, u32[]{:S(2)}, u32[]{:S(2)}) %all-to-all-start) | async-done | bytes 16416 | tf_op jit(solution)/shard_map/all_to_all | solution.py:346
  47.1 3.3 %collective-permute-start.8 = (bf16[256,256]{1,0:T(8,128)(2,1)S(1)}, bf16[256,256]{1,0:T(8,128)(2,1)S(1)}, u32[]{:S(2)}, u32[]{:S(2)}) collective-permute-start(bf16[256,256]{1,0:T(8,128)(2,1)S(1)} %get-tuple-element.84), channel_id=1, source_target_pairs={{0,10},{1,11},{2,8},{3,9},{4,14},{5,15},{6,12},{7,13},{8,2},{9,3},... | collective-permute-start | bytes 393224 | tf_op jit(solution)/shard_map/ppermute | solution.py:45
  50.4 1.8 %shard_map.61.refs_4_ = f32[1,4096]{1,0:T(1,128)S(1)} custom-call(s32[1,4096]{1,0:T(1,128)S(1)} %get-tuple-element.68.refs_0_.row_ref, s32[4096,128]{1,0:T(8,128)S(1)} %get-tuple-element.69.refs_1_.column_ref, bf16[1024,256]{1,0:T(8,128)(2,1)S(1)} %constant_dynamic-update-slice_fusion.refs_2_.refs_0_), custom_call_target="tpu_custom_call" | custom-call | flops 536870912 | tf_op jit(solution)/shard_map/pallas_call | solution.py:24
  54.1 1.7 %collective-permute-start.14 = (bf16[256,256]{1,0:T(8,128)(2,1)S(1)}, bf16[256,256]{1,0:T(8,128)(2,1)S(1)}, u32[]{:S(2)}, u32[]{:S(2)}) collective-permute-start(bf16[256,256]{1,0:T(8,128)(2,1)S(1)} %get-tuple-element.102), channel_id=1, source_target_pairs={{0,13},{1,12},{2,15},{3,14},{4,9},{5,8},{6,11},{7,10},{8,5},{9,4},... | collective-permute-start | bytes 393224 | tf_op jit(solution)/shard_map/ppermute | solution.py:45
  55.8 2.9 %collective-permute-done.9 = bf16[256,256]{1,0:T(8,128)(2,1)S(1)} collective-permute-done((bf16[256,256]{1,0:T(8,128)(2,1)S(1)}, bf16[256,256]{1,0:T(8,128)(2,1)S(1)}, u32[]{:S(2)}, u32[]{:S(2)}) %collective-permute-start.9) | collective-permute-done | bytes 131104 | tf_op jit(solution)/shard_map/ppermute | solution.py:45
  58.8 4.7 %collective-permute-done.8 = bf16[256,256]{1,0:T(8,128)(2,1)S(1)} collective-permute-done((bf16[256,256]{1,0:T(8,128)(2,1)S(1)}, bf16[256,256]{1,0:T(8,128)(2,1)S(1)}, u32[]{:S(2)}, u32[]{:S(2)}) %collective-permute-start.8) | collective-permute-done | bytes 131104 | tf_op jit(solution)/shard_map/ppermute | solution.py:45
  64.7 3.7 %shard_map.62 = (f32[1,4096]{1,0:T(1,128)S(1)}, f32[1024,128]{1,0:T(8,128)S(1)}) custom-call(s32[1,4096]{1,0:T(1,128)S(1)} %get-tuple-element.68.refs_0_.row_ref, s32[4096,128]{1,0:T(8,128)S(1)} %get-tuple-element.69.refs_1_.column_ref, bf16[1024,256]{1,0:T(8,128)(2,1)S(1)} %constant_dynamic-update-slice_fusion.refs_2_.refs_0_, ...), custom_call_target="tpu_custom_call" | custom-call | flops 1073741824 | tf_op jit(solution)/shard_map/pallas_call | solution.py:24
  68.4 2.0 %collective-permute-start.18 = (bf16[256,256]{1,0:T(8,128)(2,1)S(1)}, bf16[256,256]{1,0:T(8,128)(2,1)S(1)}, u32[]{:S(2)}, u32[]{:S(2)}) collective-permute-start(bf16[256,256]{1,0:T(8,128)(2,1)S(1)} %get-tuple-element.112), channel_id=1, source_target_pairs={{0,15},{1,14},{2,13},{3,12},{4,11},{5,10},{6,9},{7,8},{8,7},{9,6},... | collective-permute-start | bytes 393224 | tf_op jit(solution)/shard_map/ppermute | solution.py:45
  70.4 1.9 %collective-permute-start.17 = (bf16[256,256]{1,0:T(8,128)(2,1)S(1)}, bf16[256,256]{1,0:T(8,128)(2,1)S(1)}, u32[]{:S(2)}, u32[]{:S(2)}) collective-permute-start(bf16[256,256]{1,0:T(8,128)(2,1)S(1)} %get-tuple-element.106), channel_id=1, source_target_pairs={{0,3},{1,2},{2,1},{3,0},{4,7},{5,6},{6,5},{7,4},{8,11},{9,10},{10,... | collective-permute-start | bytes 393224 | tf_op jit(solution)/shard_map/ppermute | solution.py:45
  72.4 3.8 %collective-permute-start.16 = (bf16[256,256]{1,0:T(8,128)(2,1)S(1)}, bf16[256,256]{1,0:T(8,128)(2,1)S(1)}, u32[]{:S(2)}, u32[]{:S(2)}) collective-permute-start(bf16[256,256]{1,0:T(8,128)(2,1)S(1)} %get-tuple-element.105), channel_id=1, source_target_pairs={{0,14},{1,15},{2,12},{3,13},{4,10},{5,11},{6,8},{7,9},{8,6},{9,7},... | collective-permute-start | bytes 393224 | tf_op jit(solution)/shard_map/ppermute | solution.py:45
  76.2 5.7 %shard_map.63 = (f32[1,4096]{1,0:T(1,128)S(1)}, f32[2048,128]{1,0:T(8,128)S(1)}) custom-call(s32[1,4096]{1,0:T(1,128)S(1)} %get-tuple-element.68.refs_0_.row_ref, s32[4096,128]{1,0:T(8,128)S(1)} %get-tuple-element.69.refs_1_.column_ref, bf16[1024,256]{1,0:T(8,128)(2,1)S(1)} %constant_dynamic-update-slice_fusion.refs_2_.refs_0_, ...), custom_call_target="tpu_custom_call" | custom-call | flops 1610612736 | tf_op jit(solution)/shard_map/pallas_call | solution.py:24
  82.0 8.6 %shard_map.64 = (f32[1,4096]{1,0:T(1,128)S(1)}, f32[3072,128]{1,0:T(8,128)}) custom-call(s32[1,4096]{1,0:T(1,128)S(1)} %get-tuple-element.68.refs_0_.row_ref, s32[4096,128]{1,0:T(8,128)} %copy-done, bf16[1024,256]{1,0:T(8,128)(2,1)S(1)} %constant_dynamic-update-slice_fusion.refs_2_.refs_0_, ...), custom_call_target="tpu_custom_call" | custom-call | flops 1509949440 | tf_op jit(solution)/shard_map/pallas_call | solution.py:24
  90.6 2.0 %shard_map.65 = f32[16,1,256]{2,1,0:T(1,128)S(1)} custom-call(s32[1]{0:T(128)} %bitcast.3.me_ref, f32[1,4096]{1,0:T(1,128)S(1)} %get-tuple-element.111.best_in_ref, s32[1,4096]{1,0:T(1,128)S(1)} %get-tuple-element.68.refs_0_.row_ref, s32[4096,128]{1,0:T(8,128)S(1)} %copy-done.1, bf16[1024,256]{1,0:T(8,128)(2,1)S(1)} %constant_dynamic-update-slice_fusion.refs_2_.refs_0_, ...), custom_call_target="tpu_custom_call" | custom-call | flops 536870912 | tf_op jit(solution)/shard_map/pallas_call | solution.py:24
  92.6 10.5 %all_to_all.10.returned_ref = f32[16,1,256]{2,1,0:T(1,128)S(1)} all-to-all(f32[16,1,256]{2,1,0:T(1,128)S(1)} %shard_map.65), channel_id=1, replica_groups=mesh['groups'=2,'wide'=16] {'wide'}, dimensions={0} | all-to-all | bytes 32768 | tf_op jit(solution)/shard_map/all_to_all | solution.py:390
  (57 shorter events, 17.2 us)
Async XLA Ops:
  0.8 6.7 %collective-permute-start = (bf16[64,256]{1,0:T(8,128)(2,1)S(1)}, bf16[64,256]{1,0:T(8,128)(2,1)S(1)}, u32[]{:S(2)}, u32[]{:S(2)}) collective-permute-start(bf16[64,256]{1,0:T(8,128)(2,1)S(1)} %fusion.1), channel_id=1, source_target_pairs={{0,8},{1,9},{2,10},{3,11},{4,12},{5,13},{6,14},{7,15},{8,0},{9,1},... | collective-permute-start | bytes 98312 | tf_op jit(solution)/shard_map/ppermute | solution.py:45
  4.8 0.7 copy-start.2
  5.5 0.7 copy-start.3
  7.5 4.3 %collective-permute-start.1 = (bf16[128,256]{1,0:T(8,128)(2,1)S(1)}, bf16[128,256]{1,0:T(8,128)(2,1)S(1)}, u32[]{:S(2)}, u32[]{:S(2)}) collective-permute-start(bf16[128,256]{1,0:T(8,128)(2,1)S(1)} %pad_maximum_fusion.3), channel_id=1, source_target_pairs={{0,4},{1,5},{2,6},{3,7},{4,0},{5,1},{6,2},{7,3},{8,12},{9,13},{10,... | collective-permute-start | bytes 196616 | tf_op jit(solution)/shard_map/ppermute | solution.py:45
  11.8 5.0 %collective-permute-start.2 = (bf16[256,256]{1,0:T(8,128)(2,1)S(1)}, bf16[256,256]{1,0:T(8,128)(2,1)S(1)}, u32[]{:S(2)}, u32[]{:S(2)}) collective-permute-start(bf16[256,256]{1,0:T(8,128)(2,1)S(1)} %pad_maximum_fusion.2), channel_id=1, source_target_pairs={{0,2},{1,3},{2,0},{3,1},{4,6},{5,7},{6,4},{7,5},{8,10},{9,11},{10,... | collective-permute-start | bytes 393224 | tf_op jit(solution)/shard_map/ppermute | solution.py:45
  17.6 1.9 %collective-permute-start.3 = (bf16[512,256]{1,0:T(8,128)(2,1)}, bf16[512,256]{1,0:T(8,128)(2,1)}, u32[]{:S(2)}, u32[]{:S(2)}) collective-permute-start(bf16[512,256]{1,0:T(8,128)(2,1)} %pad_maximum_fusion.1), channel_id=1, source_target_pairs={{0,1},{1,0},{2,3},{3,2},{4,5},{5,4},{6,7},{7,6},{8,9},{9,8},{10,11... | collective-permute-start | bytes 786440 | tf_op jit(solution)/shard_map/ppermute | solution.py:45
  22.8 21.0 %collective-permute-start.4 = (bf16[256,256]{1,0:T(8,128)(2,1)S(1)}, bf16[256,256]{1,0:T(8,128)(2,1)S(1)}, u32[]{:S(2)}, u32[]{:S(2)}) collective-permute-start(bf16[256,256]{1,0:T(8,128)(2,1)S(1)} %get-tuple-element.72), channel_id=1, source_target_pairs={{0,8},{1,9},{2,10},{3,11},{4,12},{5,13},{6,14},{7,15},{8,0},{9,1},... | collective-permute-start | bytes 393224 | tf_op jit(solution)/shard_map/ppermute | solution.py:45
  25.0 18.8 %collective-permute-start.5 = (bf16[256,256]{1,0:T(8,128)(2,1)S(1)}, bf16[256,256]{1,0:T(8,128)(2,1)S(1)}, u32[]{:S(2)}, u32[]{:S(2)}) collective-permute-start(bf16[256,256]{1,0:T(8,128)(2,1)S(1)} %get-tuple-element.75), channel_id=1, source_target_pairs={{0,4},{1,5},{2,6},{3,7},{4,0},{5,1},{6,2},{7,3},{8,12},{9,13},{10,... | collective-permute-start | bytes 393224 | tf_op jit(solution)/shard_map/ppermute | solution.py:45
  26.8 17.0 %collective-permute-start.6 = (bf16[256,256]{1,0:T(8,128)(2,1)S(1)}, bf16[256,256]{1,0:T(8,128)(2,1)S(1)}, u32[]{:S(2)}, u32[]{:S(2)}) collective-permute-start(bf16[256,256]{1,0:T(8,128)(2,1)S(1)} %get-tuple-element.78), channel_id=1, source_target_pairs={{0,9},{1,8},{2,11},{3,10},{4,13},{5,12},{6,15},{7,14},{8,1},{9,0},... | collective-permute-start | bytes 393224 | tf_op jit(solution)/shard_map/ppermute | solution.py:45
  26.8 17.0 %collective-permute-start.7 = (bf16[256,256]{1,0:T(8,128)(2,1)S(1)}, bf16[256,256]{1,0:T(8,128)(2,1)S(1)}, u32[]{:S(2)}, u32[]{:S(2)}) collective-permute-start(bf16[256,256]{1,0:T(8,128)(2,1)S(1)} %get-tuple-element.81), channel_id=1, source_target_pairs={{0,5},{1,4},{2,7},{3,6},{4,1},{5,0},{6,3},{7,2},{8,13},{9,12},{10,... | collective-permute-start | bytes 393224 | tf_op jit(solution)/shard_map/ppermute | solution.py:45
  31.0 12.2 %all-to-all-start = ((s32[16,1,256]{2,1,0:T(1,128)}), s32[16,1,256]{2,1,0:T(1,128)S(1)}, u32[]{:S(2)}, u32[]{:S(2)}) async-start(s32[16,1,256]{2,1,0:T(1,128)} %get-tuple-element.67), calls=%async_computation | async-start | bytes 32768 | tf_op jit(solution)/shard_map/all_to_all | solution.py:346
  43.8 32.4 %copy-start = (s32[4096,128]{1,0:T(8,128)}, s32[4096,128]{1,0:T(8,128)S(1)}, u32[]{:S(2)}) copy-start(s32[4096,128]{1,0:T(8,128)S(1)} %get-tuple-element.69.refs_1_.column_ref) | copy-start | bytes 6291460
  43.8 8.4 %collective-permute-start.11 = (bf16[256,256]{1,0:T(8,128)(2,1)S(1)}, bf16[256,256]{1,0:T(8,128)(2,1)S(1)}, u32[]{:S(2)}, u32[]{:S(2)}) collective-permute-start(bf16[256,256]{1,0:T(8,128)(2,1)S(1)} %get-tuple-element.93), channel_id=1, source_target_pairs={{0,7},{1,6},{2,5},{3,4},{4,3},{5,2},{6,1},{7,0},{8,15},{9,14},{10,... | collective-permute-start | bytes 393224 | tf_op jit(solution)/shard_map/ppermute | solution.py:45
  44.1 10.0 %collective-permute-start.10 = (bf16[256,256]{1,0:T(8,128)(2,1)S(1)}, bf16[256,256]{1,0:T(8,128)(2,1)S(1)}, u32[]{:S(2)}, u32[]{:S(2)}) collective-permute-start(bf16[256,256]{1,0:T(8,128)(2,1)S(1)} %get-tuple-element.90), channel_id=1, source_target_pairs={{0,11},{1,10},{2,9},{3,8},{4,15},{5,14},{6,13},{7,12},{8,3},{9,2},... | collective-permute-start | bytes 393224 | tf_op jit(solution)/shard_map/ppermute | solution.py:45
  45.6 13.1 %collective-permute-start.9 = (bf16[256,256]{1,0:T(8,128)(2,1)S(1)}, bf16[256,256]{1,0:T(8,128)(2,1)S(1)}, u32[]{:S(2)}, u32[]{:S(2)}) collective-permute-start(bf16[256,256]{1,0:T(8,128)(2,1)S(1)} %get-tuple-element.87), channel_id=1, source_target_pairs={{0,6},{1,7},{2,4},{3,5},{4,2},{5,3},{6,0},{7,1},{8,14},{9,15},{10,... | collective-permute-start | bytes 393224 | tf_op jit(solution)/shard_map/ppermute | solution.py:45
  47.1 16.4 %collective-permute-start.8 = (bf16[256,256]{1,0:T(8,128)(2,1)S(1)}, bf16[256,256]{1,0:T(8,128)(2,1)S(1)}, u32[]{:S(2)}, u32[]{:S(2)}) collective-permute-start(bf16[256,256]{1,0:T(8,128)(2,1)S(1)} %get-tuple-element.84), channel_id=1, source_target_pairs={{0,10},{1,11},{2,8},{3,9},{4,14},{5,15},{6,12},{7,13},{8,2},{9,3},... | collective-permute-start | bytes 393224 | tf_op jit(solution)/shard_map/ppermute | solution.py:45
  52.3 29.6 %collective-permute-start.15 = (bf16[256,256]{1,0:T(8,128)(2,1)S(1)}, bf16[256,256]{1,0:T(8,128)(2,1)S(1)}, u32[]{:S(2)}, u32[]{:S(2)}) collective-permute-start(bf16[256,256]{1,0:T(8,128)(2,1)S(1)} %get-tuple-element.104), channel_id=1, source_target_pairs={{0,2},{1,3},{2,0},{3,1},{4,6},{5,7},{6,4},{7,5},{8,10},{9,11},{10,... | collective-permute-start | bytes 393224 | tf_op jit(solution)/shard_map/ppermute | solution.py:45
  54.1 14.3 %collective-permute-start.14 = (bf16[256,256]{1,0:T(8,128)(2,1)S(1)}, bf16[256,256]{1,0:T(8,128)(2,1)S(1)}, u32[]{:S(2)}, u32[]{:S(2)}) collective-permute-start(bf16[256,256]{1,0:T(8,128)(2,1)S(1)} %get-tuple-element.102), channel_id=1, source_target_pairs={{0,13},{1,12},{2,15},{3,14},{4,9},{5,8},{6,11},{7,10},{8,5},{9,4},... | collective-permute-start | bytes 393224 | tf_op jit(solution)/shard_map/ppermute | solution.py:45
  58.7 11.8 %collective-permute-start.13 = (bf16[256,256]{1,0:T(8,128)(2,1)S(1)}, bf16[256,256]{1,0:T(8,128)(2,1)S(1)}, u32[]{:S(2)}, u32[]{:S(2)}) collective-permute-start(bf16[256,256]{1,0:T(8,128)(2,1)S(1)} %get-tuple-element.99), channel_id=1, source_target_pairs={{0,1},{1,0},{2,3},{3,2},{4,5},{5,4},{6,7},{7,6},{8,9},{9,8},{10,11... | collective-permute-start | bytes 393224 | tf_op jit(solution)/shard_map/ppermute | solution.py:45
  63.5 8.9 %collective-permute-start.12 = (bf16[256,256]{1,0:T(8,128)(2,1)S(1)}, bf16[256,256]{1,0:T(8,128)(2,1)S(1)}, u32[]{:S(2)}, u32[]{:S(2)}) collective-permute-start(bf16[256,256]{1,0:T(8,128)(2,1)S(1)} %get-tuple-element.96), channel_id=1, source_target_pairs={{0,12},{1,13},{2,14},{3,15},{4,8},{5,9},{6,10},{7,11},{8,4},{9,5},... | collective-permute-start | bytes 393224 | tf_op jit(solution)/shard_map/ppermute | solution.py:45
  68.4 22.2 %collective-permute-start.18 = (bf16[256,256]{1,0:T(8,128)(2,1)S(1)}, bf16[256,256]{1,0:T(8,128)(2,1)S(1)}, u32[]{:S(2)}, u32[]{:S(2)}) collective-permute-start(bf16[256,256]{1,0:T(8,128)(2,1)S(1)} %get-tuple-element.112), channel_id=1, source_target_pairs={{0,15},{1,14},{2,13},{3,12},{4,11},{5,10},{6,9},{7,8},{8,7},{9,6},... | collective-permute-start | bytes 393224 | tf_op jit(solution)/shard_map/ppermute | solution.py:45
  70.4 11.5 %collective-permute-start.17 = (bf16[256,256]{1,0:T(8,128)(2,1)S(1)}, bf16[256,256]{1,0:T(8,128)(2,1)S(1)}, u32[]{:S(2)}, u32[]{:S(2)}) collective-permute-start(bf16[256,256]{1,0:T(8,128)(2,1)S(1)} %get-tuple-element.106), channel_id=1, source_target_pairs={{0,3},{1,2},{2,1},{3,0},{4,7},{5,6},{6,5},{7,4},{8,11},{9,10},{10,... | collective-permute-start | bytes 393224 | tf_op jit(solution)/shard_map/ppermute | solution.py:45
  72.4 9.5 %collective-permute-start.16 = (bf16[256,256]{1,0:T(8,128)(2,1)S(1)}, bf16[256,256]{1,0:T(8,128)(2,1)S(1)}, u32[]{:S(2)}, u32[]{:S(2)}) collective-permute-start(bf16[256,256]{1,0:T(8,128)(2,1)S(1)} %get-tuple-element.105), channel_id=1, source_target_pairs={{0,14},{1,15},{2,12},{3,13},{4,10},{5,11},{6,8},{7,9},{8,6},{9,7},... | collective-permute-start | bytes 393224 | tf_op jit(solution)/shard_map/ppermute | solution.py:45
  81.9 8.7 %copy-start.1 = (s32[4096,128]{1,0:T(8,128)S(1)}, s32[4096,128]{1,0:T(8,128)}, u32[]{:S(2)}) copy-start(s32[4096,128]{1,0:T(8,128)} %copy-done) | copy-start | bytes 6291460

commit v3 on v1

v3 whole, which is shorter than its diff:
```python
import functools

import jax
import jax.numpy as jnp
from jax import lax
from jax.experimental import pallas as pl
from jax.experimental.pallas import tpu as pltpu
from jax.sharding import PartitionSpec as P

CL_DEV = 4
RANK_SPAN = 4096
KEY_LOW = 128
PIECE_TILE = 16
CHUNK = 256
LANES = 512
SLAB = 16
KEY_ROWS = 16
IN_FLIGHT = 5
VMEM_BYTES = 48 * 1024 * 1024
VMEM = pl.BlockSpec(memory_space=pltpu.VMEM)
SMEM = pl.BlockSpec(memory_space=pltpu.SMEM)
F32 = jnp.float32
BF16 = jnp.bfloat16


def call(kernel, outs, operands, scratch=(), smem=(), flops=0, moved=0):
    return pl.pallas_call(
        kernel,
        out_shape=outs,
        in_specs=[SMEM if i in smem else VMEM for i in range(len(operands))],
        out_specs=jax.tree.map(lambda _: VMEM, outs),
        scratch_shapes=list(scratch),
        compiler_params=pltpu.CompilerParams(vmem_limit_bytes=VMEM_BYTES),
        cost_estimate=pl.CostEstimate(flops=flops, bytes_accessed=moved, transcendentals=0),
    )(*operands)


def masks_of(peers):
    far = list(range(peers // 2, peers))
    near = list(range(peers // 4, peers // 2)) + list(range(1, peers // 4))
    order = []
    for i in range(len(near)):
        order += far[:-2][i : i + 1] + near[i : i + 1]
    return order + far[-2:]


def swap(x, mask, peers):
    return lax.ppermute(x, "wide", [(i, i ^ mask) for i in range(peers)])


def hits(owners, peers):
    return owners == lax.broadcasted_iota(jnp.int32, (peers, owners.shape[1]), 0)


def places_kernel(peers, slot, labels_ref, ranks_ref, place_ref, keys_ref):
    rows = labels_ref.shape[1]
    step = min(CHUNK, rows)
    labels = labels_ref[...]
    owners = labels // CL_DEV
    hit = hits(owners, peers)
    hit_f = jnp.where(hit, 1.0, 0.0)
    earlier = jnp.where(
        lax.broadcasted_iota(jnp.int32, (step, step), 0) < lax.broadcasted_iota(jnp.int32, (step, step), 1), 1.0, 0.0
    ).astype(BF16)
    seen = jnp.zeros((peers, 1), F32)
    within = []
    for b in range(rows // step):
        hit_b = hit_f[:, b * step : (b + 1) * step]
        counts = jnp.dot(hit_b.astype(BF16), earlier, preferred_element_type=F32) + seen
        within.append(jnp.sum(hit_b * counts, axis=0, keepdims=True))
        seen = seen + jnp.sum(hit_b, axis=1, keepdims=True)
    within = jnp.concatenate(within, axis=1).astype(jnp.int32)
    place_ref[...] = owners * slot + within
    keys = (labels % CL_DEV + 1) * RANK_SPAN + ranks_ref[...]
    high = (keys // KEY_LOW).astype(F32)
    low = (keys % KEY_LOW).astype(F32)
    spread = jnp.where(within == lax.broadcasted_iota(jnp.int32, (slot, rows), 0), 1.0, 0.0).astype(BF16)
    parts = jnp.concatenate([hit_f * high, hit_f * low], axis=0).astype(BF16)
    slots = lax.dot_general(parts, spread, (((1,), (1,)), ((), ())), preferred_element_type=F32)
    keys_ref[...] = (slots[:peers] * KEY_LOW + slots[peers:]).astype(jnp.int32).reshape(peers, 1, slot)


def stage_kernel(embeddings_ref, staged_ref, semaphore):
    copy = pltpu.make_async_copy(embeddings_ref, staged_ref, semaphore)
    copy.start()
    copy.wait()


def project(embeddings_ref, basis, offset, units_ref):
    rows = embeddings_ref.shape[0]
    step = min(CHUNK, rows)
    for b in range(rows // step):
        block = slice(b * step, (b + 1) * step)
        projected = jnp.dot(embeddings_ref[block], basis, preferred_element_type=F32) - offset
        scale_back = lax.rsqrt(jnp.sum(projected * projected, axis=1, keepdims=True) + 1e-06)
        units_ref[block] = (projected * scale_back).astype(BF16)


def fill_slots(masks, me_ref, place_ref, keys_ref, units_ref, out_refs):
    slot = keys_ref.shape[2]
    rows = place_ref.shape[1]
    units = units_ref[...]
    for mask, out_ref in zip(masks, out_refs, strict=True):
        owner = me_ref[0] ^ mask
        here = place_ref[...] - owner * slot
        spread = jnp.where(here == lax.broadcasted_iota(jnp.int32, (slot, rows), 0), 1.0, 0.0).astype(BF16)
        out_ref[:slot] = jnp.dot(spread, units, preferred_element_type=F32).astype(BF16)
        keys = keys_ref[owner]
        line = lax.broadcasted_iota(jnp.int32, (KEY_ROWS, slot), 0)
        parts = jnp.where(line == 0, keys // KEY_LOW, jnp.where(line == 1, keys % KEY_LOW, 0))
        out_ref[slot:, :slot] = parts.astype(F32).astype(BF16)


def slots_kernel(masks, me_ref, place_ref, keys_ref, units_ref, *out_refs):
    fill_slots(masks, me_ref, place_ref, keys_ref, units_ref, out_refs)


def project_whole_kernel(masks, me_ref, place_ref, keys_ref, embeddings_ref, basis_ref, center_ref, units_ref, *out_refs):
    basis = basis_ref[...]
    offset = jnp.dot(center_ref[...], basis, preferred_element_type=F32)
    project(embeddings_ref, basis, offset, units_ref)
    fill_slots(masks, me_ref, place_ref, keys_ref, units_ref, out_refs)


def project_pieces_kernel(masks, spots, piece_rows, me_ref, place_ref, keys_ref, embeddings_ref, *refs):
    *gathered_refs, units_ref = refs[: 3]
    out_refs, basis_ref = refs[3:-1], refs[-1]
    half = len(spots) // 2
    tile = gathered_refs[0].shape[0] // half
    offset = None
    for q, mask in enumerate(spots):
        gathered_ref, at = gathered_refs[q // half], q % half * tile
        piece = gathered_ref[at : at + piece_rows]
        start = pl.multiple_of((me_ref[0] ^ mask) * piece_rows, piece_rows)
        basis_ref[pl.ds(start, piece_rows), :] = piece
        center = gathered_ref[at + piece_rows : at + tile, :piece_rows]
        part = jnp.dot(center, piece, preferred_element_type=F32)
        offset = part if offset is None else offset + part
    project(embeddings_ref, basis_ref[...], offset[:1], units_ref)
    fill_slots(masks, me_ref, place_ref, keys_ref, units_ref, out_refs)


def best_of(cosine, key_col, label_col, key_row, label_row, below, beside):
    cosine = jnp.where(label_col == label_row, cosine, -1.0)
    earlier = key_col < key_row
    down = jnp.where(earlier, cosine, -1.0)
    down = jnp.max(down.reshape(-1, 8, 128), axis=0)
    below = jnp.maximum(below, down)
    if beside is not None:
        beside = jnp.maximum(beside, jnp.where(earlier, -1.0, cosine))
    return below, beside


def column_of(row):
    n = row.shape[1]
    same = lax.broadcasted_iota(jnp.int32, (n, n), 0) == lax.broadcasted_iota(jnp.int32, (n, n), 1)
    ones = jnp.ones((n, 128), BF16)
    parts = []
    for part in (row // KEY_LOW, row % KEY_LOW):
        spread = jnp.where(same, part.astype(F32), 0.0).astype(BF16)
        parts.append(jnp.dot(spread, ones, preferred_element_type=F32).astype(jnp.int32))
    return parts[0] * KEY_LOW + parts[1]


def pairs_kernel(fresh_blocks, masks, me_ref, *refs):
    refs = list(refs)
    state = (refs.pop(0), refs.pop(0)) if refs[0].shape[0] == 1 else None
    block_refs = refs[:-6]
    best_out_ref, row_out_ref, best_ref, line_ref, column_ref, all_ref = refs[-6:]
    width = all_ref.shape[1]
    slot = block_refs[0].shape[0] - KEY_ROWS
    start = (len(block_refs) - fresh_blocks) * slot
    fresh = fresh_blocks * slot
    end = start + fresh
    row_ref = row_out_ref
    best_ref[...] = jnp.full(best_ref.shape, -1.0, F32)
    if state is not None:
        row_ref[...] = state[1][...]
        best_ref[:, :start] = state[0][:, :start]
    else:
        row_ref[...] = jnp.zeros(row_ref.shape, jnp.int32)
    for n, block_ref in enumerate(block_refs):
        at = n * slot
        all_ref[at : at + slot] = block_ref[:slot]
        if at >= start:
            parts = block_ref[slot:].astype(F32)[:, :slot]
            row_ref[:, at : at + slot] = (parts[0:1] * KEY_LOW + parts[1:2]).astype(jnp.int32)
    step = min(CHUNK, fresh)
    for t in range(0, fresh, step):
        column_ref[t : t + step] = column_of(row_ref[:, start + t : start + t + step])
    line_ref[...] = jnp.full(line_ref.shape, -1.0, F32)

    def tile(t, lane, lanes, both):
        new = all_ref[start + t : start + t + step]
        others = all_ref[pl.ds(lane, lanes), :]
        cosines = lax.dot_general(new, others, (((1,), (1,)), ((), ())), preferred_element_type=F32)
        tiles = range(lanes // 128)
        heres = [pl.ds(lane + n * 128, 128) for n in tiles]
        key_rows = [row_ref[:, here] for here in heres]
        label_rows = [key_row // RANK_SPAN for key_row in key_rows]
        below = [jnp.full((8, 128), -1.0, F32)] * len(tiles)
        for s in range(0, step, SLAB):
            key_col = column_ref[t + s : t + s + SLAB]
            label_col = key_col // RANK_SPAN
            beside = line_ref[t + s : t + s + SLAB] if both else None
            for n in tiles:
                cosine = cosines[s : s + SLAB, n * 128 : (n + 1) * 128]
                below[n], beside = best_of(cosine, key_col, label_col, key_rows[n], label_rows[n], below[n], beside)
            if both:
                line_ref[t + s : t + s + SLAB] = beside
        for n, here in zip(tiles, heres, strict=True):
            best_ref[:, here] = jnp.maximum(best_ref[:, here], jnp.max(below[n], axis=0, keepdims=True))

    for t in range(0, fresh, step):
        tile(t, start + t, step, False)
        for lane in range(start, start + t, step):
            tile(t, lane, step, True)
    for lane in range(0, start, LANES):
        for t in range(0, fresh, step):
            tile(t, lane, min(LANES, start - lane), True)
    same = lax.broadcasted_iota(jnp.int32, (128, 128), 0) == lax.broadcasted_iota(jnp.int32, (128, 128), 1)
    for t in range(0, fresh, 128):
        here = slice(start + t, start + t + 128)
        column = jnp.max(line_ref[t : t + 128], axis=1, keepdims=True)
        turned = jnp.max(jnp.where(same, column, -1.0), axis=0, keepdims=True)
        best_ref[:, here] = jnp.maximum(best_ref[:, here], turned)
    if masks is None:
        best_out_ref[...] = best_ref[...]
    else:
        for n, mask in enumerate(masks):
            best_out_ref[me_ref[0] ^ mask] = best_ref[:, n * slot : (n + 1) * slot]


def back_kernel(slot, place_ref, returned_ref, out_ref):
    peers = returned_ref.shape[0]
    place = place_ref[...]
    rows = place.shape[1]
    values = returned_ref[...].reshape(peers, slot)
    high = values.astype(BF16)
    rest = values - high.astype(F32)
    middle = rest.astype(BF16)
    low = (rest - middle.astype(F32)).astype(BF16)
    parts = jnp.concatenate([high, middle, low], axis=0)
    spread = jnp.where(place % slot == lax.broadcasted_iota(jnp.int32, (slot, rows), 0), 1.0, 0.0).astype(BF16)
    found = jnp.dot(parts, spread, preferred_element_type=F32)
    found = (found[:peers] + found[peers : 2 * peers]) + found[2 * peers :]
    out_ref[...] = jnp.sum(jnp.where(hits(place // slot, peers), found, 0.0), axis=0, keepdims=True)


def sds(shape, dtype):
    return jax.ShapeDtypeStruct(shape, dtype)


def shards(embeddings, pca_basis, pca_center, row_labels, row_ranks):
    peers = lax.axis_size("wide")
    me = lax.axis_index("wide").astype(jnp.int32).reshape(1)
    rows, depth = embeddings.shape
    piece_rows, width = pca_basis.shape
    slot = 2 * rows // peers
    total = peers * slot
    order = masks_of(peers)
    masks = [0, *order]

    place, keys = call(
        functools.partial(places_kernel, peers, slot),
        (sds((1, rows), jnp.int32), sds((peers, 1, slot), jnp.int32)),
        (row_labels.reshape(1, rows), row_ranks.reshape(1, rows)),
        flops=2 * 3 * peers * rows * slot,
    )
    staged = pl.pallas_call(
        stage_kernel,
        out_shape=sds((rows, depth), BF16),
        in_specs=[pl.BlockSpec(memory_space=pl.ANY)],
        out_specs=VMEM,
        scratch_shapes=[pltpu.SemaphoreType.DMA],
        compiler_params=pltpu.CompilerParams(vmem_limit_bytes=VMEM_BYTES),
        cost_estimate=pl.CostEstimate(flops=0, bytes_accessed=4 * rows * depth, transcendentals=0),
    )(embeddings)

    leading = order[:1]
    followers = [order[1:3], order[3:IN_FLIGHT], [*order[IN_FLIGHT:], 0]]
    blocks_of = lambda part: tuple(sds((slot + KEY_ROWS, width), BF16) for _ in part)
    outs = (sds((rows, width), BF16), *blocks_of(leading))
    cost = dict(flops=2 * rows * width * (depth + len(leading) * slot), moved=2 * rows * depth)
    if piece_rows % PIECE_TILE:
        basis = lax.all_gather(pca_basis, "wide", axis=0, tiled=True)
        center = lax.all_gather(pca_center, "wide", axis=0, tiled=True).reshape(1, depth)
        kernel = functools.partial(project_whole_kernel, leading)
        units, *sent = call(kernel, outs, (me, place, keys, staged, basis, center), smem=(0,), **cost)
    else:
        tail = jnp.pad(pca_center.reshape(1, piece_rows), ((0, PIECE_TILE - 1), (0, width - piece_rows)))
        gathered = lax.optimization_barrier(jnp.concatenate([pca_basis, tail], axis=0))
        spots = [0]
        bit = peers // 2
        while bit:
            other = swap(gathered, bit, peers)
            spots = spots + [spot ^ bit for spot in spots]
            if len(spots) == 2:
                other, place, keys = lax.optimization_barrier((other, place, keys))
            elif len(spots) == 4:
                other, staged = lax.optimization_barrier((other, staged))
            if len(spots) < peers:
                gathered = lax.optimization_barrier(jnp.concatenate([gathered, other], axis=0))
            bit //= 2
        kernel = functools.partial(project_pieces_kernel, leading, spots, piece_rows)
        scratch = [pltpu.VMEM((depth, width), BF16)]
        operands = (me, place, keys, staged, gathered, other)
        units, *sent = call(kernel, outs, operands, scratch=scratch, smem=(0,), **cost)
    for part in followers:
        units, sent[-1] = lax.optimization_barrier((units, sent[-1]))
        sent += call(
            functools.partial(slots_kernel, part),
            blocks_of(part),
            (me, place, keys, units),
            smem=(0,),
            flops=2 * len(part) * slot * rows * width,
        )

    blocks = [sent[-1]]
    group, end = max(peers // 8, 1), max(peers // 16, 1)
    cuts = [*range(group, peers, group), peers - end, peers]
    state, done = (), 0

    def add_pairs(state, lo, hi):
        last = hi == peers
        fresh = (hi - lo) * slot
        return call(
            functools.partial(pairs_kernel, hi - lo, masks if last else None),
            (sds((peers, 1, slot) if last else (1, total), F32), sds((1, total), jnp.int32)),
            (me, *state, *blocks[:hi]),
            scratch=[
                pltpu.VMEM((1, total), F32),
                pltpu.VMEM((fresh, 128), F32),
                pltpu.VMEM((fresh, 128), jnp.int32),
                pltpu.VMEM((hi * slot, width), BF16),
            ],
            smem=(0,),
            flops=2 * fresh * hi * slot * width,
        )

    for n, mask in enumerate(order):
        block = sent[n]
        arrived = n + 1 - IN_FLIGHT
        if arrived > 0:
            while cuts[0] <= arrived + 1:
                state = add_pairs(state, done, cuts[0])
                done = cuts.pop(0)
            block, blocks[arrived], *state = lax.optimization_barrier((block, blocks[arrived], *state))
        blocks.append(swap(block, mask, peers))
    for cut in cuts:
        state = add_pairs(state, done, cut)
        done = cut
    best = state[0]
    returned = lax.all_to_all(best, "wide", split_axis=0, concat_axis=0, tiled=True)
    nearest = call(
        functools.partial(back_kernel, slot),
        sds((1, rows), F32),
        (place, returned),
        flops=2 * 3 * peers * rows * slot,
    )
    return nearest.reshape(-1)


def solution(mesh):
    return jax.shard_map(
        shards,
        mesh=mesh,
        in_specs=(
            P(("groups", "wide"), None),
            P("wide", None),
            P("wide"),
            P(("groups", "wide")),
            P(("groups", "wide")),
        ),
        out_specs=P(("groups", "wide")),
        check_vma=False,
    )
```

time: 126 us -> 91.5 us (0.73)
  Pallas kernels: 42.2 us -> 24.7 us
  waiting for transfers between devices: 27.3 us -> 14.5 us
  local copies, waits for them, and re-layouts: 6.7 us -> 1.39 us
  blocking collectives: 9.68 us -> 13.2 us
  other arithmetic: 3.57 us -> 0.79 us
    pallas_call x11 -> x15, Pallas kernels: 42.2 us -> 22.8 us  [call(): pl.pallas_call(kernel, out_shape=outs, in_specs=[SMEM if i in smem else V...]
    ppermute x19, waiting for transfers between devices: 21.5 us -> 14.5 us  [swap(): return lax.ppermute(x, 'wide', [(i, i ^ mask) for i in range(peers)])]
    ppermute x19, starting transfers between devices: 29.6 us -> 36.5 us  [swap(): return lax.ppermute(x, 'wide', [(i, i ^ mask) for i in range(peers)])]
    all_to_all x1 -> x0, starting transfers between devices: 6.26 us -> none  [shards(): lax.all_to_all(keys, 'wide', split_axis=0, concat_axis=0, tiled=True)]
    all_to_all x1 -> x0, waiting for transfers between devices: 5.83 us -> none  [shards(): lax.all_to_all(keys, 'wide', split_axis=0, concat_axis=0, tiled=True)]
    all_to_all x1, blocking collectives: 9.68 us -> 13.2 us  [shards(): lax.all_to_all(best, 'wide', split_axis=0, concat_axis=0, tiled=True)]
    unnamed x23 -> x4, local copies, waits for them, and re-layouts: 4.81 us -> 1.39 us
    pallas_call x0 -> x1, Pallas kernels: none -> 1.9 us  [shards(): pl.pallas_call(stage_kernel, out_shape=sds((rows, depth), BF16), in_specs...]
  transfers between devices with their start and end apart: 20 -> 19, of which waited for: 9 -> 8; matrix products, arithmetic and copies ran while one was open for 1% -> 0% of each run, Pallas kernels for 28% -> 21%
where the time goes in v3:
time: 91.5 us; the launch traced here: 91.1 us
  starting transfers between devices  36.5 us (40%)
  Pallas kernels  24.7 us (27%)
  waiting for transfers between devices  14.5 us (16%)
  blocking collectives  13.2 us (14%)
  local copies, waits for them, and re-layouts  1.39 us (2%)
    ppermute x19, starting transfers between devices, swap(): return lax.ppermute(x, 'wide', [(i, i ^ mask) for i in range(peers)])  36.5 us
    pallas_call x15, Pallas kernels, call(): pl.pallas_call(kernel, out_shape=outs, in_specs=[SMEM if i in smem else V...  22.8 us
    ppermute x19, waiting for transfers between devices, swap(): return lax.ppermute(x, 'wide', [(i, i ^ mask) for i in range(peers)])  14.5 us
    all_to_all x1, blocking collectives, shards(): lax.all_to_all(best, 'wide', split_axis=0, concat_axis=0, tiled=True)  13.2 us
    pallas_call x1, Pallas kernels, shards(): pl.pallas_call(stage_kernel, out_shape=sds((rows, depth), BF16), in_specs...  1.9 us
  transfers between devices with their start and end apart: 19, of which 8 were waited for; matrix products, arithmetic and copies ran while one was open for 0% of the time, Pallas kernels for 21%

profile of v3, /device:TPU:0, one launch (start us, length us, event | category | flops | bytes accessed | tf_op | source)
XLA Modules:
  0.0 91.1 jit_solution(7271585450362632579)
XLA Ops:
  0.8 4.0 %collective-permute-start = (bf16[64,256]{1,0:T(8,128)(2,1)S(1)}, bf16[64,256]{1,0:T(8,128)(2,1)S(1)}, u32[]{:S(2)}, u32[]{:S(2)}) collective-permute-start(bf16[64,256]{1,0:T(8,128)(2,1)S(1)} %fusion.1), channel_id=1, source_target_pairs={{0,8},{1,9},{2,10},{3,11},{4,12},{5,13},{6,14},{7,15},{8,0},{9,1},... | collective-permute-start | bytes 98312 | tf_op jit(solution)/shard_map/ppermute | solution.py:48
  7.0 1.6 %collective-permute-start.1 = (bf16[128,256]{1,0:T(8,128)(2,1)S(1)}, bf16[128,256]{1,0:T(8,128)(2,1)S(1)}, u32[]{:S(2)}, u32[]{:S(2)}) collective-permute-start(bf16[128,256]{1,0:T(8,128)(2,1)S(1)} %pad_maximum_fusion.2), channel_id=1, source_target_pairs={{0,4},{1,5},{2,6},{3,7},{4,0},{5,1},{6,2},{7,3},{8,12},{9,13},{10,... | collective-permute-start | bytes 196616 | tf_op jit(solution)/shard_map/ppermute | solution.py:48
  8.6 1.9 %shard_map.56.embeddings_ref = bf16[2048,768]{1,0:T(8,128)(2,1)S(1)} custom-call(bf16[2048,768]{1,0:T(8,128)(2,1)} %embeddings_ref.1), custom_call_target="tpu_custom_call" | custom-call | bytes 6291456 | tf_op jit(solution)/shard_map/pallas_call | solution.py:270
  11.3 1.8 %collective-permute-start.2 = (bf16[256,256]{1,0:T(8,128)(2,1)S(1)}, bf16[256,256]{1,0:T(8,128)(2,1)S(1)}, u32[]{:S(2)}, u32[]{:S(2)}) collective-permute-start(bf16[256,256]{1,0:T(8,128)(2,1)S(1)} %pad_maximum_fusion.1), channel_id=1, source_target_pairs={{0,2},{1,3},{2,0},{3,1},{4,6},{5,7},{6,4},{7,5},{8,10},{9,11},{10,... | collective-permute-start | bytes 393224 | tf_op jit(solution)/shard_map/ppermute | solution.py:48
  13.1 3.2 %collective-permute-done.2 = bf16[256,256]{1,0:T(8,128)(2,1)S(1)} collective-permute-done((bf16[256,256]{1,0:T(8,128)(2,1)S(1)}, bf16[256,256]{1,0:T(8,128)(2,1)S(1)}, u32[]{:S(2)}, u32[]{:S(2)}) %collective-permute-start.2) | collective-permute-done | bytes 131104 | tf_op jit(solution)/shard_map/ppermute | solution.py:48
  16.5 1.6 %collective-permute-done.3.refs_1_ = bf16[512,256]{1,0:T(8,128)(2,1)} collective-permute-done((bf16[512,256]{1,0:T(8,128)(2,1)S(1)}, bf16[512,256]{1,0:T(8,128)(2,1)}, u32[]{:S(2)}, u32[]{:S(2)}) %collective-permute-start.3) | collective-permute-done | bytes 262176 | tf_op jit(solution)/shard_map/ppermute | solution.py:48
  18.1 2.5 %shard_map.57 = (bf16[2048,256]{1,0:T(8,128)(2,1)S(1)}, bf16[272,256]{1,0:T(8,128)(2,1)S(1)}) custom-call(s32[1]{0:T(128)} %bitcast.3.me_ref, s32[1,2048]{1,0:T(1,128)S(1)} %get-tuple-element.92.place_ref, s32[16,1,256]{2,1,0:T(1,128)S(1)} %get-tuple-element.93.keys_ref, bf16[2048,768]{1,0:T(8,128)(2,1)S(1)} %shard_map.56.embeddings_ref, ...), custom_call_target="tpu_custom_call" | custom-call | flops 1073741824 | bytes 3145728 | tf_op jit(solution)/shard_map/pallas_call | solution.py:27
  20.7 2.7 %collective-permute-start.8 = (bf16[272,256]{1,0:T(8,128)(2,1)S(1)}, bf16[272,256]{1,0:T(8,128)(2,1)S(1)}, u32[]{:S(2)}, u32[]{:S(2)}) collective-permute-start(bf16[272,256]{1,0:T(8,128)(2,1)S(1)} %get-tuple-element.112), channel_id=1, source_target_pairs={{0,8},{1,9},{2,10},{3,11},{4,12},{5,13},{6,14},{7,15},{8,0},{9,1},... | collective-permute-start | bytes 417800 | tf_op jit(solution)/shard_map/ppermute | solution.py:48
  24.1 1.9 %collective-permute-start.7 = (bf16[272,256]{1,0:T(8,128)(2,1)S(1)}, bf16[272,256]{1,0:T(8,128)(2,1)S(1)}, u32[]{:S(2)}, u32[]{:S(2)}) collective-permute-start(bf16[272,256]{1,0:T(8,128)(2,1)S(1)} %get-tuple-element.110), channel_id=1, source_target_pairs={{0,4},{1,5},{2,6},{3,7},{4,0},{5,1},{6,2},{7,3},{8,12},{9,13},{10,... | collective-permute-start | bytes 417800 | tf_op jit(solution)/shard_map/ppermute | solution.py:48
  26.7 3.3 %collective-permute-start.4 = (bf16[272,256]{1,0:T(8,128)(2,1)S(1)}, bf16[272,256]{1,0:T(8,128)(2,1)S(1)}, u32[]{:S(2)}, u32[]{:S(2)}) collective-permute-start(bf16[272,256]{1,0:T(8,128)(2,1)S(1)} %get-tuple-element.104), channel_id=1, source_target_pairs={{0,10},{1,11},{2,8},{3,9},{4,14},{5,15},{6,12},{7,13},{8,2},{9,3},... | collective-permute-start | bytes 417800 | tf_op jit(solution)/shard_map/ppermute | solution.py:48
  30.0 3.1 %shard_map.60 = (bf16[272,256]{1,0:T(8,128)(2,1)S(1)}, bf16[272,256]{1,0:T(8,128)(2,1)S(1)}, bf16[272,256]{1,0:T(8,128)(2,1)S(1)}, bf16[272,256]{1,0:T(8,128)(2,...) custom-call(s32[1]{0:T(128)} %bitcast.3.me_ref, ...), custom_call_target="tpu_custom_call" | custom-call | flops 2952790016 | tf_op jit(solution)/shard_map/pallas_call | solution.py:27
  36.4 2.7 %collective-permute-start.12 = (bf16[272,256]{1,0:T(8,128)(2,1)S(1)}, bf16[272,256]{1,0:T(8,128)(2,1)S(1)}, u32[]{:S(2)}, u32[]{:S(2)}) collective-permute-start(bf16[272,256]{1,0:T(8,128)(2,1)S(1)} %get-tuple-element.138), channel_id=1, source_target_pairs={{0,11},{1,10},{2,9},{3,8},{4,15},{5,14},{6,13},{7,12},{8,3},{9,2},... | collective-permute-start | bytes 417800 | tf_op jit(solution)/shard_map/ppermute | solution.py:48
  40.0 1.6 %collective-permute-start.11 = (bf16[272,256]{1,0:T(8,128)(2,1)S(1)}, bf16[272,256]{1,0:T(8,128)(2,1)S(1)}, u32[]{:S(2)}, u32[]{:S(2)}) collective-permute-start(bf16[272,256]{1,0:T(8,128)(2,1)S(1)} %get-tuple-element.136), channel_id=1, source_target_pairs={{0,7},{1,6},{2,5},{3,4},{4,3},{5,2},{6,1},{7,0},{8,15},{9,14},{10,... | collective-permute-start | bytes 417800 | tf_op jit(solution)/shard_map/ppermute | solution.py:48
  41.6 2.3 %collective-permute-start.10 = (bf16[272,256]{1,0:T(8,128)(2,1)S(1)}, bf16[272,256]{1,0:T(8,128)(2,1)S(1)}, u32[]{:S(2)}, u32[]{:S(2)}) collective-permute-start(bf16[272,256]{1,0:T(8,128)(2,1)S(1)} %get-tuple-element.134), channel_id=1, source_target_pairs={{0,12},{1,13},{2,14},{3,15},{4,8},{5,9},{6,10},{7,11},{8,4},{9,5},... | collective-permute-start | bytes 417800 | tf_op jit(solution)/shard_map/ppermute | solution.py:48
  45.7 3.2 %collective-permute-done.13.refs_8_ = bf16[272,256]{1,0:T(8,128)(2,1)S(1)} collective-permute-done((bf16[272,256]{1,0:T(8,128)(2,1)S(1)}, bf16[272,256]{1,0:T(8,128)(2,1)S(1)}, u32[]{:S(2)}, u32[]{:S(2)}) %collective-permute-start.13) | collective-permute-done | bytes 139296 | tf_op jit(solution)/shard_map/ppermute | solution.py:48
  50.1 1.5 %shard_map.64 = (f32[1,4096]{1,0:T(1,128)S(1)}, s32[1,4096]{1,0:T(1,128)S(1)}) custom-call(s32[1]{0:T(128)} %bitcast.3.me_ref, f32[1,4096]{1,0:T(1,128)S(1)} %get-tuple-element.143.refs_0_, s32[1,4096]{1,0:T(1,128)S(1)} %get-tuple-element.144.refs_1_, bf16[272,256]{1,0:T(8,128)(2,1)S(1)} %get-tuple-element.113.refs_0_.refs_2_, ...), custom_call_target="tpu_custom_call" | custom-call | flops 536870912 | tf_op jit(solution)/shard_map/pallas_call | solution.py:27
  51.6 6.5 %collective-permute-start.16 = (bf16[272,256]{1,0:T(8,128)(2,1)S(1)}, bf16[272,256]{1,0:T(8,128)(2,1)S(1)}, u32[]{:S(2)}, u32[]{:S(2)}) collective-permute-start(bf16[272,256]{1,0:T(8,128)(2,1)S(1)} %get-tuple-element.167), channel_id=1, source_target_pairs={{0,3},{1,2},{2,1},{3,0},{4,7},{5,6},{6,5},{7,4},{8,11},{9,10},{10,... | collective-permute-start | bytes 417800 | tf_op jit(solution)/shard_map/ppermute | solution.py:48
  59.5 2.0 %shard_map.65 = (f32[1,4096]{1,0:T(1,128)S(1)}, s32[1,4096]{1,0:T(1,128)S(1)}) custom-call(s32[1]{0:T(128)} %bitcast.3.me_ref, f32[1,4096]{1,0:T(1,128)S(1)} %get-tuple-element.151.refs_0_, s32[1,4096]{1,0:T(1,128)S(1)} %get-tuple-element.152.refs_1_, bf16[272,256]{1,0:T(8,128)(2,1)S(1)} %get-tuple-element.113.refs_0_.refs_2_, ...), custom_call_target="tpu_custom_call" | custom-call | flops 671088640 | tf_op jit(solution)/shard_map/pallas_call | solution.py:27
  61.5 3.6 %collective-permute-start.18 = (bf16[272,256]{1,0:T(8,128)(2,1)S(1)}, bf16[272,256]{1,0:T(8,128)(2,1)S(1)}, u32[]{:S(2)}, u32[]{:S(2)}) collective-permute-start(bf16[272,256]{1,0:T(8,128)(2,1)S(1)} %get-tuple-element.173), channel_id=1, source_target_pairs={{0,15},{1,14},{2,13},{3,12},{4,11},{5,10},{6,9},{7,8},{8,7},{9,6},... | collective-permute-start | bytes 417800 | tf_op jit(solution)/shard_map/ppermute | solution.py:48
  65.5 2.1 %shard_map.66 = (f32[1,4096]{1,0:T(1,128)S(1)}, s32[1,4096]{1,0:T(1,128)S(1)}) custom-call(s32[1]{0:T(128)} %bitcast.3.me_ref, f32[1,4096]{1,0:T(1,128)S(1)} %get-tuple-element.159.refs_0_, s32[1,4096]{1,0:T(1,128)S(1)} %get-tuple-element.160.refs_1_, bf16[272,256]{1,0:T(8,128)(2,1)S(1)} %get-tuple-element.113.refs_0_.refs_2_, ...), custom_call_target="tpu_custom_call" | custom-call | flops 805306368 | tf_op jit(solution)/shard_map/pallas_call | solution.py:27
  67.6 2.4 %shard_map.67 = (f32[1,4096]{1,0:T(1,128)S(1)}, s32[1,4096]{1,0:T(1,128)S(1)}) custom-call(s32[1]{0:T(128)} %bitcast.3.me_ref, f32[1,4096]{1,0:T(1,128)S(1)} %get-tuple-element.164.refs_0_, s32[1,4096]{1,0:T(1,128)S(1)} %get-tuple-element.165.refs_1_, bf16[272,256]{1,0:T(8,128)(2,1)S(1)} %get-tuple-element.113.refs_0_.refs_2_, ...), custom_call_target="tpu_custom_call" | custom-call | flops 939524096 | tf_op jit(solution)/shard_map/pallas_call | solution.py:27
  70.1 3.8 %collective-permute-done.17.refs_16_ = bf16[272,256]{1,0:T(8,128)(2,1)S(1)} collective-permute-done((bf16[272,256]{1,0:T(8,128)(2,1)S(1)}, bf16[272,256]{1,0:T(8,128)(2,1)S(1)}, u32[]{:S(2)}, u32[]{:S(2)}) %collective-permute-start.17) | collective-permute-done | bytes 139296 | tf_op jit(solution)/shard_map/ppermute | solution.py:48
  75.4 1.6 %shard_map.69 = (f32[16,1,256]{2,1,0:T(1,128)S(1)}, s32[1,4096]{1,0:T(1,128)}) custom-call(s32[1]{0:T(128)} %bitcast.3.me_ref, f32[1,4096]{1,0:T(1,128)S(1)} %get-tuple-element.171.refs_0_, s32[1,4096]{1,0:T(1,128)S(1)} %get-tuple-element.172.refs_1_, bf16[272,256]{1,0:T(8,128)(2,1)S(1)} %get-tuple-element.113.refs_0_.refs_2_, ...), custom_call_target="tpu_custom_call" | custom-call | flops 536870912 | tf_op jit(solution)/shard_map/pallas_call | solution.py:27
  77.0 13.2 %all_to_all.5.returned_ref = f32[16,1,256]{2,1,0:T(1,128)S(1)} all-to-all(f32[16,1,256]{2,1,0:T(1,128)S(1)} %get-tuple-element.174), channel_id=1, replica_groups=mesh['groups'=2,'wide'=16] {'wide'}, dimensions={0} | all-to-all | bytes 32768 | tf_op jit(solution)/shard_map/all_to_all | solution.py:354
  (39 shorter events, 16.6 us)
Async XLA Ops:
  0.8 6.3 %collective-permute-start = (bf16[64,256]{1,0:T(8,128)(2,1)S(1)}, bf16[64,256]{1,0:T(8,128)(2,1)S(1)}, u32[]{:S(2)}, u32[]{:S(2)}) collective-permute-start(bf16[64,256]{1,0:T(8,128)(2,1)S(1)} %fusion.1), channel_id=1, source_target_pairs={{0,8},{1,9},{2,10},{3,11},{4,12},{5,13},{6,14},{7,15},{8,0},{9,1},... | collective-permute-start | bytes 98312 | tf_op jit(solution)/shard_map/ppermute | solution.py:48
  4.8 0.7 copy-start
  5.5 0.7 copy-start.1
  7.0 4.3 %collective-permute-start.1 = (bf16[128,256]{1,0:T(8,128)(2,1)S(1)}, bf16[128,256]{1,0:T(8,128)(2,1)S(1)}, u32[]{:S(2)}, u32[]{:S(2)}) collective-permute-start(bf16[128,256]{1,0:T(8,128)(2,1)S(1)} %pad_maximum_fusion.2), channel_id=1, source_target_pairs={{0,4},{1,5},{2,6},{3,7},{4,0},{5,1},{6,2},{7,3},{8,12},{9,13},{10,... | collective-permute-start | bytes 196616 | tf_op jit(solution)/shard_map/ppermute | solution.py:48
  11.3 5.0 %collective-permute-start.2 = (bf16[256,256]{1,0:T(8,128)(2,1)S(1)}, bf16[256,256]{1,0:T(8,128)(2,1)S(1)}, u32[]{:S(2)}, u32[]{:S(2)}) collective-permute-start(bf16[256,256]{1,0:T(8,128)(2,1)S(1)} %pad_maximum_fusion.1), channel_id=1, source_target_pairs={{0,2},{1,3},{2,0},{3,1},{4,6},{5,7},{6,4},{7,5},{8,10},{9,11},{10,... | collective-permute-start | bytes 393224 | tf_op jit(solution)/shard_map/ppermute | solution.py:48
  16.4 1.7 %collective-permute-start.3 = (bf16[512,256]{1,0:T(8,128)(2,1)S(1)}, bf16[512,256]{1,0:T(8,128)(2,1)}, u32[]{:S(2)}, u32[]{:S(2)}) collective-permute-start(bf16[512,256]{1,0:T(8,128)(2,1)S(1)} %pad_maximum_fusion.refs_0_), channel_id=1, source_target_pairs={{0,1},{1,0},{2,3},{3,2},{4,5},{5,4},{6,7},{7,6},{8,9},{9,8},{10,11... | collective-permute-start | bytes 786440 | tf_op jit(solution)/shard_map/ppermute | solution.py:48
  20.7 13.5 %collective-permute-start.8 = (bf16[272,256]{1,0:T(8,128)(2,1)S(1)}, bf16[272,256]{1,0:T(8,128)(2,1)S(1)}, u32[]{:S(2)}, u32[]{:S(2)}) collective-permute-start(bf16[272,256]{1,0:T(8,128)(2,1)S(1)} %get-tuple-element.112), channel_id=1, source_target_pairs={{0,8},{1,9},{2,10},{3,11},{4,12},{5,13},{6,14},{7,15},{8,0},{9,1},... | collective-permute-start | bytes 417800 | tf_op jit(solution)/shard_map/ppermute | solution.py:48
  24.0 15.1 %collective-permute-start.6 = (bf16[272,256]{1,0:T(8,128)(2,1)S(1)}, bf16[272,256]{1,0:T(8,128)(2,1)S(1)}, u32[]{:S(2)}, u32[]{:S(2)}) collective-permute-start(bf16[272,256]{1,0:T(8,128)(2,1)S(1)} %get-tuple-element.108), channel_id=1, source_target_pairs={{0,9},{1,8},{2,11},{3,10},{4,13},{5,12},{6,15},{7,14},{8,1},{9,0},... | collective-permute-start | bytes 417800 | tf_op jit(solution)/shard_map/ppermute | solution.py:48
  24.1 12.3 %collective-permute-start.7 = (bf16[272,256]{1,0:T(8,128)(2,1)S(1)}, bf16[272,256]{1,0:T(8,128)(2,1)S(1)}, u32[]{:S(2)}, u32[]{:S(2)}) collective-permute-start(bf16[272,256]{1,0:T(8,128)(2,1)S(1)} %get-tuple-element.110), channel_id=1, source_target_pairs={{0,4},{1,5},{2,6},{3,7},{4,0},{5,1},{6,2},{7,3},{8,12},{9,13},{10,... | collective-permute-start | bytes 417800 | tf_op jit(solution)/shard_map/ppermute | solution.py:48
  26.7 17.7 %collective-permute-start.4 = (bf16[272,256]{1,0:T(8,128)(2,1)S(1)}, bf16[272,256]{1,0:T(8,128)(2,1)S(1)}, u32[]{:S(2)}, u32[]{:S(2)}) collective-permute-start(bf16[272,256]{1,0:T(8,128)(2,1)S(1)} %get-tuple-element.104), channel_id=1, source_target_pairs={{0,10},{1,11},{2,8},{3,9},{4,14},{5,15},{6,12},{7,13},{8,2},{9,3},... | collective-permute-start | bytes 417800 | tf_op jit(solution)/shard_map/ppermute | solution.py:48
  30.0 11.6 %collective-permute-start.5 = (bf16[272,256]{1,0:T(8,128)(2,1)S(1)}, bf16[272,256]{1,0:T(8,128)(2,1)S(1)}, u32[]{:S(2)}, u32[]{:S(2)}) collective-permute-start(bf16[272,256]{1,0:T(8,128)(2,1)S(1)} %get-tuple-element.106), channel_id=1, source_target_pairs={{0,5},{1,4},{2,7},{3,6},{4,1},{5,0},{6,3},{7,2},{8,13},{9,12},{10,... | collective-permute-start | bytes 417800 | tf_op jit(solution)/shard_map/ppermute | solution.py:48
  34.9 14.0 %collective-permute-start.13 = (bf16[272,256]{1,0:T(8,128)(2,1)S(1)}, bf16[272,256]{1,0:T(8,128)(2,1)S(1)}, u32[]{:S(2)}, u32[]{:S(2)}) collective-permute-start(bf16[272,256]{1,0:T(8,128)(2,1)S(1)} %get-tuple-element.140), channel_id=1, source_target_pairs={{0,6},{1,7},{2,4},{3,5},{4,2},{5,3},{6,0},{7,1},{8,14},{9,15},{10,... | collective-permute-start | bytes 417800 | tf_op jit(solution)/shard_map/ppermute | solution.py:48
  36.4 13.7 %collective-permute-start.12 = (bf16[272,256]{1,0:T(8,128)(2,1)S(1)}, bf16[272,256]{1,0:T(8,128)(2,1)S(1)}, u32[]{:S(2)}, u32[]{:S(2)}) collective-permute-start(bf16[272,256]{1,0:T(8,128)(2,1)S(1)} %get-tuple-element.138), channel_id=1, source_target_pairs={{0,11},{1,10},{2,9},{3,8},{4,15},{5,14},{6,13},{7,12},{8,3},{9,2},... | collective-permute-start | bytes 417800 | tf_op jit(solution)/shard_map/ppermute | solution.py:48
  40.0 11.6 %collective-permute-start.11 = (bf16[272,256]{1,0:T(8,128)(2,1)S(1)}, bf16[272,256]{1,0:T(8,128)(2,1)S(1)}, u32[]{:S(2)}, u32[]{:S(2)}) collective-permute-start(bf16[272,256]{1,0:T(8,128)(2,1)S(1)} %get-tuple-element.136), channel_id=1, source_target_pairs={{0,7},{1,6},{2,5},{3,4},{4,3},{5,2},{6,1},{7,0},{8,15},{9,14},{10,... | collective-permute-start | bytes 417800 | tf_op jit(solution)/shard_map/ppermute | solution.py:48
  41.6 17.9 %collective-permute-start.10 = (bf16[272,256]{1,0:T(8,128)(2,1)S(1)}, bf16[272,256]{1,0:T(8,128)(2,1)S(1)}, u32[]{:S(2)}, u32[]{:S(2)}) collective-permute-start(bf16[272,256]{1,0:T(8,128)(2,1)S(1)} %get-tuple-element.134), channel_id=1, source_target_pairs={{0,12},{1,13},{2,14},{3,15},{4,8},{5,9},{6,10},{7,11},{8,4},{9,5},... | collective-permute-start | bytes 417800 | tf_op jit(solution)/shard_map/ppermute | solution.py:48
  45.6 15.9 %collective-permute-start.9 = (bf16[272,256]{1,0:T(8,128)(2,1)S(1)}, bf16[272,256]{1,0:T(8,128)(2,1)S(1)}, u32[]{:S(2)}, u32[]{:S(2)}) collective-permute-start(bf16[272,256]{1,0:T(8,128)(2,1)S(1)} %get-tuple-element.132), channel_id=1, source_target_pairs={{0,1},{1,0},{2,3},{3,2},{4,5},{5,4},{6,7},{7,6},{8,9},{9,8},{10,11... | collective-permute-start | bytes 417800 | tf_op jit(solution)/shard_map/ppermute | solution.py:48
  48.9 16.6 %collective-permute-start.14 = (bf16[272,256]{1,0:T(8,128)(2,1)S(1)}, bf16[272,256]{1,0:T(8,128)(2,1)S(1)}, u32[]{:S(2)}, u32[]{:S(2)}) collective-permute-start(bf16[272,256]{1,0:T(8,128)(2,1)S(1)} %get-tuple-element.163), channel_id=1, source_target_pairs={{0,13},{1,12},{2,15},{3,14},{4,9},{5,8},{6,11},{7,10},{8,5},{9,4},... | collective-permute-start | bytes 417800 | tf_op jit(solution)/shard_map/ppermute | solution.py:48
  51.6 16.0 %collective-permute-start.16 = (bf16[272,256]{1,0:T(8,128)(2,1)S(1)}, bf16[272,256]{1,0:T(8,128)(2,1)S(1)}, u32[]{:S(2)}, u32[]{:S(2)}) collective-permute-start(bf16[272,256]{1,0:T(8,128)(2,1)S(1)} %get-tuple-element.167), channel_id=1, source_target_pairs={{0,3},{1,2},{2,1},{3,0},{4,7},{5,6},{6,5},{7,4},{8,11},{9,10},{10,... | collective-permute-start | bytes 417800 | tf_op jit(solution)/shard_map/ppermute | solution.py:48
  58.2 9.5 %collective-permute-start.15 = (bf16[272,256]{1,0:T(8,128)(2,1)S(1)}, bf16[272,256]{1,0:T(8,128)(2,1)S(1)}, u32[]{:S(2)}, u32[]{:S(2)}) collective-permute-start(bf16[272,256]{1,0:T(8,128)(2,1)S(1)} %get-tuple-element.166), channel_id=1, source_target_pairs={{0,2},{1,3},{2,0},{3,1},{4,6},{5,7},{6,4},{7,5},{8,10},{9,11},{10,... | collective-permute-start | bytes 417800 | tf_op jit(solution)/shard_map/ppermute | solution.py:48
  61.5 13.8 %collective-permute-start.18 = (bf16[272,256]{1,0:T(8,128)(2,1)S(1)}, bf16[272,256]{1,0:T(8,128)(2,1)S(1)}, u32[]{:S(2)}, u32[]{:S(2)}) collective-permute-start(bf16[272,256]{1,0:T(8,128)(2,1)S(1)} %get-tuple-element.173), channel_id=1, source_target_pairs={{0,15},{1,14},{2,13},{3,12},{4,11},{5,10},{6,9},{7,8},{8,7},{9,6},... | collective-permute-start | bytes 417800 | tf_op jit(solution)/shard_map/ppermute | solution.py:48
  65.1 8.7 %collective-permute-start.17 = (bf16[272,256]{1,0:T(8,128)(2,1)S(1)}, bf16[272,256]{1,0:T(8,128)(2,1)S(1)}, u32[]{:S(2)}, u32[]{:S(2)}) collective-permute-start(bf16[272,256]{1,0:T(8,128)(2,1)S(1)} %get-tuple-element.170), channel_id=1, source_target_pairs={{0,14},{1,15},{2,12},{3,13},{4,10},{5,11},{6,8},{7,9},{8,6},{9,7},... | collective-permute-start | bytes 417800 | tf_op jit(solution)/shard_map/ppermute | solution.py:48

commit v4 on v3

--- a/solution.py
+++ b/solution.py
@@ -14,8 +14,8 @@
 CHUNK = 256
 LANES = 512
 SLAB = 16
-KEY_ROWS = 16
-IN_FLIGHT = 5
+KEY_ROWS = 8
+IN_FLIGHT = 4
 VMEM_BYTES = 48 * 1024 * 1024
 VMEM = pl.BlockSpec(memory_space=pltpu.VMEM)
 SMEM = pl.BlockSpec(memory_space=pltpu.SMEM)
@@ -37,11 +37,11 @@
 
 def masks_of(peers):
     far = list(range(peers // 2, peers))
-    near = list(range(peers // 4, peers // 2)) + list(range(1, peers // 4))
+    near = list(range(1, peers // 2))
     order = []
-    for i in range(len(near)):
-        order += far[:-2][i : i + 1] + near[i : i + 1]
-    return order + far[-2:]
+    for i in range(len(far)):
+        order += far[i : i + 1] + near[i : i + 1]
+    return order
 
 
 def swap(x, mask, peers):
@@ -278,7 +278,7 @@
     )(embeddings)
 
     leading = order[:1]
-    followers = [order[1:3], order[3:IN_FLIGHT], [*order[IN_FLIGHT:], 0]]
+    followers = [order[1:3], order[3:5], [*order[5:], 0]]
     blocks_of = lambda part: tuple(sds((slot + KEY_ROWS, width), BF16) for _ in part)
     outs = (sds((rows, width), BF16), *blocks_of(leading))
     cost = dict(flops=2 * rows * width * (depth + len(leading) * slot), moved=2 * rows * depth)
@@ -317,8 +317,8 @@
         )
 
     blocks = [sent[-1]]
-    group, end = max(peers // 8, 1), max(peers // 16, 1)
-    cuts = [*range(group, peers, group), peers - end, peers]
+    step = max(peers // 16, 1)
+    cuts = [*range(2 * step, peers, step), peers]
     state, done = (), 0
 
     def add_pairs(state, lo, hi):
@@ -340,12 +340,11 @@
 
     for n, mask in enumerate(order):
         block = sent[n]
-        arrived = n + 1 - IN_FLIGHT
-        if arrived > 0:
-            while cuts[0] <= arrived + 1:
+        if n >= IN_FLIGHT:
+            if cuts[0] <= n + 2 - IN_FLIGHT:
                 state = add_pairs(state, done, cuts[0])
                 done = cuts.pop(0)
-            block, blocks[arrived], *state = lax.optimization_barrier((block, blocks[arrived], *state))
+            block, *state = lax.optimization_barrier((block, *state))
         blocks.append(swap(block, mask, peers))
     for cut in cuts:
         state = add_pairs(state, done, cut)

time: 91.5 us -> 86 us (0.940)
  starting transfers between devices: 36.5 us -> 32.8 us
  waiting for transfers between devices: 14.5 us -> 12.2 us
  Pallas kernels: 24.7 us -> 26 us
    ppermute x19, starting transfers between devices: 36.5 us -> 32.8 us  [swap(): return lax.ppermute(x, 'wide', [(i, i ^ mask) for i in range(peers)])]
    ppermute x19, waiting for transfers between devices: 14.5 us -> 12.2 us  [swap(): return lax.ppermute(x, 'wide', [(i, i ^ mask) for i in range(peers)])]
    pallas_call x15 -> x21, Pallas kernels: 22.8 us -> 24.1 us  [call(): pl.pallas_call(kernel, out_shape=outs, in_specs=[SMEM if i in smem else V...]
  transfers between devices with their start and end apart: 19 -> 19, of which waited for: 8 -> 9; matrix products, arithmetic and copies ran while one was open for 0% -> 0% of each run, Pallas kernels for 21% -> 24%
where the time goes in v4:
time: 86 us; the launch traced here: 85.6 us
  starting transfers between devices  32.8 us (38%)
  Pallas kernels  26 us (30%)
  blocking collectives  12.3 us (14%)
  waiting for transfers between devices  12.2 us (14%)
  local copies, waits for them, and re-layouts  1.39 us (2%)
    ppermute x19, starting transfers between devices, swap(): return lax.ppermute(x, 'wide', [(i, i ^ mask) for i in range(peers)])  32.8 us
    pallas_call x21, Pallas kernels, call(): pl.pallas_call(kernel, out_shape=outs, in_specs=[SMEM if i in smem else V...  24.1 us
    all_to_all x1, blocking collectives, shards(): lax.all_to_all(best, 'wide', split_axis=0, concat_axis=0, tiled=True)  12.3 us
    ppermute x19, waiting for transfers between devices, swap(): return lax.ppermute(x, 'wide', [(i, i ^ mask) for i in range(peers)])  12.2 us
    pallas_call x1, Pallas kernels, shards(): pl.pallas_call(stage_kernel, out_shape=sds((rows, depth), BF16), in_specs...  1.9 us
  transfers between devices with their start and end apart: 19, of which 9 were waited for; matrix products, arithmetic and copies ran while one was open for 0% of the time, Pallas kernels for 24%

profile of v4, /device:TPU:0, one launch (start us, length us, event | category | flops | bytes accessed | tf_op | source)
XLA Modules:
  0.0 85.6 jit_solution(15405780044596924467)
XLA Ops:
  0.8 4.0 %collective-permute-start = (bf16[64,256]{1,0:T(8,128)(2,1)S(1)}, bf16[64,256]{1,0:T(8,128)(2,1)S(1)}, u32[]{:S(2)}, u32[]{:S(2)}) collective-permute-start(bf16[64,256]{1,0:T(8,128)(2,1)S(1)} %fusion.1), channel_id=1, source_target_pairs={{0,8},{1,9},{2,10},{3,11},{4,12},{5,13},{6,14},{7,15},{8,0},{9,1},... | collective-permute-start | bytes 98312 | tf_op jit(solution)/shard_map/ppermute | solution.py:48
  7.0 1.6 %collective-permute-start.1 = (bf16[128,256]{1,0:T(8,128)(2,1)S(1)}, bf16[128,256]{1,0:T(8,128)(2,1)S(1)}, u32[]{:S(2)}, u32[]{:S(2)}) collective-permute-start(bf16[128,256]{1,0:T(8,128)(2,1)S(1)} %pad_maximum_fusion.2), channel_id=1, source_target_pairs={{0,4},{1,5},{2,6},{3,7},{4,0},{5,1},{6,2},{7,3},{8,12},{9,13},{10,... | collective-permute-start | bytes 196616 | tf_op jit(solution)/shard_map/ppermute | solution.py:48
  8.6 1.9 %shard_map.56.embeddings_ref = bf16[2048,768]{1,0:T(8,128)(2,1)S(1)} custom-call(bf16[2048,768]{1,0:T(8,128)(2,1)} %embeddings_ref.1), custom_call_target="tpu_custom_call" | custom-call | bytes 6291456 | tf_op jit(solution)/shard_map/pallas_call | solution.py:270
  11.3 1.8 %collective-permute-start.2 = (bf16[256,256]{1,0:T(8,128)(2,1)S(1)}, bf16[256,256]{1,0:T(8,128)(2,1)S(1)}, u32[]{:S(2)}, u32[]{:S(2)}) collective-permute-start(bf16[256,256]{1,0:T(8,128)(2,1)S(1)} %pad_maximum_fusion.1), channel_id=1, source_target_pairs={{0,2},{1,3},{2,0},{3,1},{4,6},{5,7},{6,4},{7,5},{8,10},{9,11},{10,... | collective-permute-start | bytes 393224 | tf_op jit(solution)/shard_map/ppermute | solution.py:48
  13.1 3.2 %collective-permute-done.2 = bf16[256,256]{1,0:T(8,128)(2,1)S(1)} collective-permute-done((bf16[256,256]{1,0:T(8,128)(2,1)S(1)}, bf16[256,256]{1,0:T(8,128)(2,1)S(1)}, u32[]{:S(2)}, u32[]{:S(2)}) %collective-permute-start.2) | collective-permute-done | bytes 131104 | tf_op jit(solution)/shard_map/ppermute | solution.py:48
  16.5 1.6 %collective-permute-done.3.refs_1_ = bf16[512,256]{1,0:T(8,128)(2,1)} collective-permute-done((bf16[512,256]{1,0:T(8,128)(2,1)S(1)}, bf16[512,256]{1,0:T(8,128)(2,1)}, u32[]{:S(2)}, u32[]{:S(2)}) %collective-permute-start.3) | collective-permute-done | bytes 262176 | tf_op jit(solution)/shard_map/ppermute | solution.py:48
  18.1 2.5 %shard_map.57 = (bf16[2048,256]{1,0:T(8,128)(2,1)S(1)}, bf16[264,256]{1,0:T(8,128)(2,1)S(1)}) custom-call(s32[1]{0:T(128)} %bitcast.3.me_ref, s32[1,2048]{1,0:T(1,128)S(1)} %get-tuple-element.97.place_ref, s32[16,1,256]{2,1,0:T(1,128)S(1)} %get-tuple-element.98.keys_ref, bf16[2048,768]{1,0:T(8,128)(2,1)S(1)} %shard_map.56.embeddings_ref, ...), custom_call_target="tpu_custom_call" | custom-call | flops 1073741824 | bytes 3145728 | tf_op jit(solution)/shard_map/pallas_call | solution.py:27
  20.7 2.7 %collective-permute-start.4 = (bf16[264,256]{1,0:T(8,128)(2,1)S(1)}, bf16[264,256]{1,0:T(8,128)(2,1)S(1)}, u32[]{:S(2)}, u32[]{:S(2)}) collective-permute-start(bf16[264,256]{1,0:T(8,128)(2,1)S(1)} %get-tuple-element.119), channel_id=1, source_target_pairs={{0,8},{1,9},{2,10},{3,11},{4,12},{5,13},{6,14},{7,15},{8,0},{9,1},... | collective-permute-start | bytes 405512 | tf_op jit(solution)/shard_map/ppermute | solution.py:48
  25.2 1.8 %collective-permute-start.7 = (bf16[264,256]{1,0:T(8,128)(2,1)S(1)}, bf16[264,256]{1,0:T(8,128)(2,1)S(1)}, u32[]{:S(2)}, u32[]{:S(2)}) collective-permute-start(bf16[264,256]{1,0:T(8,128)(2,1)S(1)} %get-tuple-element.134), channel_id=1, source_target_pairs={{0,2},{1,3},{2,0},{3,1},{4,6},{5,7},{6,4},{7,5},{8,10},{9,11},{10,... | collective-permute-start | bytes 405512 | tf_op jit(solution)/shard_map/ppermute | solution.py:48
  27.0 3.1 %shard_map.60 = (bf16[264,256]{1,0:T(8,128)(2,1)S(1)}, bf16[264,256]{1,0:T(8,128)(2,1)S(1)}, bf16[264,256]{1,0:T(8,128)(2,1)S(1)}, bf16[264,256]{1,0:T(8,128)(2,...) custom-call(s32[1]{0:T(128)} %bitcast.3.me_ref, ...), custom_call_target="tpu_custom_call" | custom-call | flops 2952790016 | tf_op jit(solution)/shard_map/pallas_call | solution.py:27
  30.2 3.7 %collective-permute-done.4.refs_1_.refs_3_ = bf16[264,256]{1,0:T(8,128)(2,1)S(1)} collective-permute-done((bf16[264,256]{1,0:T(8,128)(2,1)S(1)}, bf16[264,256]{1,0:T(8,128)(2,1)S(1)}, u32[]{:S(2)}, u32[]{:S(2)}) %collective-permute-start.4) | collective-permute-done | bytes 135200 | tf_op jit(solution)/shard_map/ppermute | solution.py:48
  36.5 4.6 %collective-permute-start.10 = (bf16[264,256]{1,0:T(8,128)(2,1)S(1)}, bf16[264,256]{1,0:T(8,128)(2,1)S(1)}, u32[]{:S(2)}, u32[]{:S(2)}) collective-permute-start(bf16[264,256]{1,0:T(8,128)(2,1)S(1)} %get-tuple-element.149), channel_id=1, source_target_pairs={{0,11},{1,10},{2,9},{3,8},{4,15},{5,14},{6,13},{7,12},{8,3},{9,2},... | collective-permute-start | bytes 405512 | tf_op jit(solution)/shard_map/ppermute | solution.py:48
  41.8 3.1 %collective-permute-start.11 = (bf16[264,256]{1,0:T(8,128)(2,1)S(1)}, bf16[264,256]{1,0:T(8,128)(2,1)S(1)}, u32[]{:S(2)}, u32[]{:S(2)}) collective-permute-start(bf16[264,256]{1,0:T(8,128)(2,1)S(1)} %get-tuple-element.154), channel_id=1, source_target_pairs={{0,4},{1,5},{2,6},{3,7},{4,0},{5,1},{6,2},{7,3},{8,12},{9,13},{10,... | collective-permute-start | bytes 405512 | tf_op jit(solution)/shard_map/ppermute | solution.py:48
  45.6 4.4 %collective-permute-start.12 = (bf16[264,256]{1,0:T(8,128)(2,1)S(1)}, bf16[264,256]{1,0:T(8,128)(2,1)S(1)}, u32[]{:S(2)}, u32[]{:S(2)}) collective-permute-start(bf16[264,256]{1,0:T(8,128)(2,1)S(1)} %get-tuple-element.159), channel_id=1, source_target_pairs={{0,12},{1,13},{2,14},{3,15},{4,8},{5,9},{6,10},{7,11},{8,4},{9,5},... | collective-permute-start | bytes 405512 | tf_op jit(solution)/shard_map/ppermute | solution.py:48
  54.5 1.2 %shard_map.69 = (f32[1,4096]{1,0:T(1,128)S(1)}, s32[1,4096]{1,0:T(1,128)S(1)}) custom-call(s32[1]{0:T(128)} %bitcast.3.me_ref, f32[1,4096]{1,0:T(1,128)S(1)} %get-tuple-element.157.refs_0_, s32[1,4096]{1,0:T(1,128)S(1)} %get-tuple-element.158.refs_1_, bf16[264,256]{1,0:T(8,128)(2,1)S(1)} %get-tuple-element.118.refs_0_.refs_2_, ...), custom_call_target="tpu_custom_call" | custom-call | flops 335544320 | tf_op jit(solution)/shard_map/pallas_call | solution.py:27
  55.7 4.1 %collective-permute-start.16 = (bf16[264,256]{1,0:T(8,128)(2,1)S(1)}, bf16[264,256]{1,0:T(8,128)(2,1)S(1)}, u32[]{:S(2)}, u32[]{:S(2)}) collective-permute-start(bf16[264,256]{1,0:T(8,128)(2,1)S(1)} %get-tuple-element.177), channel_id=1, source_target_pairs={{0,14},{1,15},{2,12},{3,13},{4,10},{5,11},{6,8},{7,9},{8,6},{9,7},... | collective-permute-start | bytes 405512 | tf_op jit(solution)/shard_map/ppermute | solution.py:48
  61.3 1.2 %shard_map.71 = (f32[1,4096]{1,0:T(1,128)S(1)}, s32[1,4096]{1,0:T(1,128)S(1)}) custom-call(s32[1]{0:T(128)} %bitcast.3.me_ref, f32[1,4096]{1,0:T(1,128)S(1)} %get-tuple-element.167.refs_0_, s32[1,4096]{1,0:T(1,128)S(1)} %get-tuple-element.168.refs_1_, bf16[264,256]{1,0:T(8,128)(2,1)S(1)} %get-tuple-element.118.refs_0_.refs_2_, ...), custom_call_target="tpu_custom_call" | custom-call | flops 402653184 | tf_op jit(solution)/shard_map/pallas_call | solution.py:27
  62.5 2.4 %collective-permute-start.18 = (bf16[264,256]{1,0:T(8,128)(2,1)S(1)}, bf16[264,256]{1,0:T(8,128)(2,1)S(1)}, u32[]{:S(2)}, u32[]{:S(2)}) collective-permute-start(bf16[264,256]{1,0:T(8,128)(2,1)S(1)} %get-tuple-element.183), channel_id=1, source_target_pairs={{0,15},{1,14},{2,13},{3,12},{4,11},{5,10},{6,9},{7,8},{8,7},{9,6},... | collective-permute-start | bytes 405512 | tf_op jit(solution)/shard_map/ppermute | solution.py:48
  64.9 1.3 %shard_map.72 = (f32[1,4096]{1,0:T(1,128)S(1)}, s32[1,4096]{1,0:T(1,128)S(1)}) custom-call(s32[1]{0:T(128)} %bitcast.3.me_ref, f32[1,4096]{1,0:T(1,128)S(1)} %get-tuple-element.172.refs_0_, s32[1,4096]{1,0:T(1,128)S(1)} %get-tuple-element.173.refs_1_, bf16[264,256]{1,0:T(8,128)(2,1)S(1)} %get-tuple-element.118.refs_0_.refs_2_, ...), custom_call_target="tpu_custom_call" | custom-call | flops 436207616 | tf_op jit(solution)/shard_map/pallas_call | solution.py:27
  66.2 1.4 %shard_map.73 = (f32[1,4096]{1,0:T(1,128)S(1)}, s32[1,4096]{1,0:T(1,128)S(1)}) custom-call(s32[1]{0:T(128)} %bitcast.3.me_ref, f32[1,4096]{1,0:T(1,128)S(1)} %get-tuple-element.175.refs_0_, s32[1,4096]{1,0:T(1,128)S(1)} %get-tuple-element.176.refs_1_, bf16[264,256]{1,0:T(8,128)(2,1)S(1)} %get-tuple-element.118.refs_0_.refs_2_, ...), custom_call_target="tpu_custom_call" | custom-call | flops 469762048 | tf_op jit(solution)/shard_map/pallas_call | solution.py:27
  67.6 1.3 %collective-permute-done.17.refs_16_ = bf16[264,256]{1,0:T(8,128)(2,1)S(1)} collective-permute-done((bf16[264,256]{1,0:T(8,128)(2,1)S(1)}, bf16[264,256]{1,0:T(8,128)(2,1)S(1)}, u32[]{:S(2)}, u32[]{:S(2)}) %collective-permute-start.17) | collective-permute-done | bytes 135200 | tf_op jit(solution)/shard_map/ppermute | solution.py:48
  68.9 1.5 %shard_map.74 = (f32[1,4096]{1,0:T(1,128)S(1)}, s32[1,4096]{1,0:T(1,128)S(1)}) custom-call(s32[1]{0:T(128)} %bitcast.3.me_ref, f32[1,4096]{1,0:T(1,128)S(1)} %get-tuple-element.178.refs_0_, s32[1,4096]{1,0:T(1,128)S(1)} %get-tuple-element.179.refs_1_, bf16[264,256]{1,0:T(8,128)(2,1)S(1)} %get-tuple-element.118.refs_0_.refs_2_, ...), custom_call_target="tpu_custom_call" | custom-call | flops 503316480 | tf_op jit(solution)/shard_map/pallas_call | solution.py:27
  70.7 1.6 %shard_map.75 = (f32[16,1,256]{2,1,0:T(1,128)S(1)}, s32[1,4096]{1,0:T(1,128)}) custom-call(s32[1]{0:T(128)} %bitcast.3.me_ref, f32[1,4096]{1,0:T(1,128)S(1)} %get-tuple-element.181.refs_0_, s32[1,4096]{1,0:T(1,128)S(1)} %get-tuple-element.182.refs_1_, bf16[264,256]{1,0:T(8,128)(2,1)S(1)} %get-tuple-element.118.refs_0_.refs_2_, ...), custom_call_target="tpu_custom_call" | custom-call | flops 536870912 | tf_op jit(solution)/shard_map/pallas_call | solution.py:27
  72.3 12.3 %all_to_all.5.returned_ref = f32[16,1,256]{2,1,0:T(1,128)S(1)} all-to-all(f32[16,1,256]{2,1,0:T(1,128)S(1)} %get-tuple-element.184), channel_id=1, replica_groups=mesh['groups'=2,'wide'=16] {'wide'}, dimensions={0} | all-to-all | bytes 32768 | tf_op jit(solution)/shard_map/all_to_all | solution.py:353
  (45 shorter events, 17.1 us)
Async XLA Ops:
  0.8 6.3 %collective-permute-start = (bf16[64,256]{1,0:T(8,128)(2,1)S(1)}, bf16[64,256]{1,0:T(8,128)(2,1)S(1)}, u32[]{:S(2)}, u32[]{:S(2)}) collective-permute-start(bf16[64,256]{1,0:T(8,128)(2,1)S(1)} %fusion.1), channel_id=1, source_target_pairs={{0,8},{1,9},{2,10},{3,11},{4,12},{5,13},{6,14},{7,15},{8,0},{9,1},... | collective-permute-start | bytes 98312 | tf_op jit(solution)/shard_map/ppermute | solution.py:48
  4.8 0.7 copy-start
  5.5 0.7 copy-start.1
  7.0 4.3 %collective-permute-start.1 = (bf16[128,256]{1,0:T(8,128)(2,1)S(1)}, bf16[128,256]{1,0:T(8,128)(2,1)S(1)}, u32[]{:S(2)}, u32[]{:S(2)}) collective-permute-start(bf16[128,256]{1,0:T(8,128)(2,1)S(1)} %pad_maximum_fusion.2), channel_id=1, source_target_pairs={{0,4},{1,5},{2,6},{3,7},{4,0},{5,1},{6,2},{7,3},{8,12},{9,13},{10,... | collective-permute-start | bytes 196616 | tf_op jit(solution)/shard_map/ppermute | solution.py:48
  11.3 5.0 %collective-permute-start.2 = (bf16[256,256]{1,0:T(8,128)(2,1)S(1)}, bf16[256,256]{1,0:T(8,128)(2,1)S(1)}, u32[]{:S(2)}, u32[]{:S(2)}) collective-permute-start(bf16[256,256]{1,0:T(8,128)(2,1)S(1)} %pad_maximum_fusion.1), channel_id=1, source_target_pairs={{0,2},{1,3},{2,0},{3,1},{4,6},{5,7},{6,4},{7,5},{8,10},{9,11},{10,... | collective-permute-start | bytes 393224 | tf_op jit(solution)/shard_map/ppermute | solution.py:48
  16.4 1.7 %collective-permute-start.3 = (bf16[512,256]{1,0:T(8,128)(2,1)S(1)}, bf16[512,256]{1,0:T(8,128)(2,1)}, u32[]{:S(2)}, u32[]{:S(2)}) collective-permute-start(bf16[512,256]{1,0:T(8,128)(2,1)S(1)} %pad_maximum_fusion.refs_0_), channel_id=1, source_target_pairs={{0,1},{1,0},{2,3},{3,2},{4,5},{5,4},{6,7},{7,6},{8,9},{9,8},{10,11... | collective-permute-start | bytes 786440 | tf_op jit(solution)/shard_map/ppermute | solution.py:48
  20.7 13.2 %collective-permute-start.4 = (bf16[264,256]{1,0:T(8,128)(2,1)S(1)}, bf16[264,256]{1,0:T(8,128)(2,1)S(1)}, u32[]{:S(2)}, u32[]{:S(2)}) collective-permute-start(bf16[264,256]{1,0:T(8,128)(2,1)S(1)} %get-tuple-element.119), channel_id=1, source_target_pairs={{0,8},{1,9},{2,10},{3,11},{4,12},{5,13},{6,14},{7,15},{8,0},{9,1},... | collective-permute-start | bytes 405512 | tf_op jit(solution)/shard_map/ppermute | solution.py:48
  24.0 11.9 %collective-permute-start.6 = (bf16[264,256]{1,0:T(8,128)(2,1)S(1)}, bf16[264,256]{1,0:T(8,128)(2,1)S(1)}, u32[]{:S(2)}, u32[]{:S(2)}) collective-permute-start(bf16[264,256]{1,0:T(8,128)(2,1)S(1)} %get-tuple-element.129), channel_id=1, source_target_pairs={{0,9},{1,8},{2,11},{3,10},{4,13},{5,12},{6,15},{7,14},{8,1},{9,0},... | collective-permute-start | bytes 405512 | tf_op jit(solution)/shard_map/ppermute | solution.py:48
  24.1 11.2 %collective-permute-start.5 = (bf16[264,256]{1,0:T(8,128)(2,1)S(1)}, bf16[264,256]{1,0:T(8,128)(2,1)S(1)}, u32[]{:S(2)}, u32[]{:S(2)}) collective-permute-start(bf16[264,256]{1,0:T(8,128)(2,1)S(1)} %get-tuple-element.124), channel_id=1, source_target_pairs={{0,1},{1,0},{2,3},{3,2},{4,5},{5,4},{6,7},{7,6},{8,9},{9,8},{10,11... | collective-permute-start | bytes 405512 | tf_op jit(solution)/shard_map/ppermute | solution.py:48
  25.2 15.9 %collective-permute-start.7 = (bf16[264,256]{1,0:T(8,128)(2,1)S(1)}, bf16[264,256]{1,0:T(8,128)(2,1)S(1)}, u32[]{:S(2)}, u32[]{:S(2)}) collective-permute-start(bf16[264,256]{1,0:T(8,128)(2,1)S(1)} %get-tuple-element.134), channel_id=1, source_target_pairs={{0,2},{1,3},{2,0},{3,1},{4,6},{5,7},{6,4},{7,5},{8,10},{9,11},{10,... | collective-permute-start | bytes 405512 | tf_op jit(solution)/shard_map/ppermute | solution.py:48
  34.5 10.4 %collective-permute-start.8 = (bf16[264,256]{1,0:T(8,128)(2,1)S(1)}, bf16[264,256]{1,0:T(8,128)(2,1)S(1)}, u32[]{:S(2)}, u32[]{:S(2)}) collective-permute-start(bf16[264,256]{1,0:T(8,128)(2,1)S(1)} %get-tuple-element.139), channel_id=1, source_target_pairs={{0,10},{1,11},{2,8},{3,9},{4,14},{5,15},{6,12},{7,13},{8,2},{9,3},... | collective-permute-start | bytes 405512 | tf_op jit(solution)/shard_map/ppermute | solution.py:48
  35.8 14.2 %collective-permute-start.9 = (bf16[264,256]{1,0:T(8,128)(2,1)S(1)}, bf16[264,256]{1,0:T(8,128)(2,1)S(1)}, u32[]{:S(2)}, u32[]{:S(2)}) collective-permute-start(bf16[264,256]{1,0:T(8,128)(2,1)S(1)} %get-tuple-element.144), channel_id=1, source_target_pairs={{0,3},{1,2},{2,1},{3,0},{4,7},{5,6},{6,5},{7,4},{8,11},{9,10},{10,... | collective-permute-start | bytes 405512 | tf_op jit(solution)/shard_map/ppermute | solution.py:48
  36.5 14.4 %collective-permute-start.10 = (bf16[264,256]{1,0:T(8,128)(2,1)S(1)}, bf16[264,256]{1,0:T(8,128)(2,1)S(1)}, u32[]{:S(2)}, u32[]{:S(2)}) collective-permute-start(bf16[264,256]{1,0:T(8,128)(2,1)S(1)} %get-tuple-element.149), channel_id=1, source_target_pairs={{0,11},{1,10},{2,9},{3,8},{4,15},{5,14},{6,13},{7,12},{8,3},{9,2},... | collective-permute-start | bytes 405512 | tf_op jit(solution)/shard_map/ppermute | solution.py:48
  41.8 10.8 %collective-permute-start.11 = (bf16[264,256]{1,0:T(8,128)(2,1)S(1)}, bf16[264,256]{1,0:T(8,128)(2,1)S(1)}, u32[]{:S(2)}, u32[]{:S(2)}) collective-permute-start(bf16[264,256]{1,0:T(8,128)(2,1)S(1)} %get-tuple-element.154), channel_id=1, source_target_pairs={{0,4},{1,5},{2,6},{3,7},{4,0},{5,1},{6,2},{7,3},{8,12},{9,13},{10,... | collective-permute-start | bytes 405512 | tf_op jit(solution)/shard_map/ppermute | solution.py:48
  45.6 8.9 %collective-permute-start.12 = (bf16[264,256]{1,0:T(8,128)(2,1)S(1)}, bf16[264,256]{1,0:T(8,128)(2,1)S(1)}, u32[]{:S(2)}, u32[]{:S(2)}) collective-permute-start(bf16[264,256]{1,0:T(8,128)(2,1)S(1)} %get-tuple-element.159), channel_id=1, source_target_pairs={{0,12},{1,13},{2,14},{3,15},{4,8},{5,9},{6,10},{7,11},{8,4},{9,5},... | collective-permute-start | bytes 405512 | tf_op jit(solution)/shard_map/ppermute | solution.py:48
  50.9 9.1 %collective-permute-start.13 = (bf16[264,256]{1,0:T(8,128)(2,1)S(1)}, bf16[264,256]{1,0:T(8,128)(2,1)S(1)}, u32[]{:S(2)}, u32[]{:S(2)}) collective-permute-start(bf16[264,256]{1,0:T(8,128)(2,1)S(1)} %get-tuple-element.164), channel_id=1, source_target_pairs={{0,5},{1,4},{2,7},{3,6},{4,1},{5,0},{6,3},{7,2},{8,13},{9,12},{10,... | collective-permute-start | bytes 405512 | tf_op jit(solution)/shard_map/ppermute | solution.py:48
  51.9 9.4 %collective-permute-start.14 = (bf16[264,256]{1,0:T(8,128)(2,1)S(1)}, bf16[264,256]{1,0:T(8,128)(2,1)S(1)}, u32[]{:S(2)}, u32[]{:S(2)}) collective-permute-start(bf16[264,256]{1,0:T(8,128)(2,1)S(1)} %get-tuple-element.169), channel_id=1, source_target_pairs={{0,13},{1,12},{2,15},{3,14},{4,9},{5,8},{6,11},{7,10},{8,5},{9,4},... | collective-permute-start | bytes 405512 | tf_op jit(solution)/shard_map/ppermute | solution.py:48
  53.6 11.3 %collective-permute-start.15 = (bf16[264,256]{1,0:T(8,128)(2,1)S(1)}, bf16[264,256]{1,0:T(8,128)(2,1)S(1)}, u32[]{:S(2)}, u32[]{:S(2)}) collective-permute-start(bf16[264,256]{1,0:T(8,128)(2,1)S(1)} %get-tuple-element.174), channel_id=1, source_target_pairs={{0,6},{1,7},{2,4},{3,5},{4,2},{5,3},{6,0},{7,1},{8,14},{9,15},{10,... | collective-permute-start | bytes 405512 | tf_op jit(solution)/shard_map/ppermute | solution.py:48
  55.7 10.5 %collective-permute-start.16 = (bf16[264,256]{1,0:T(8,128)(2,1)S(1)}, bf16[264,256]{1,0:T(8,128)(2,1)S(1)}, u32[]{:S(2)}, u32[]{:S(2)}) collective-permute-start(bf16[264,256]{1,0:T(8,128)(2,1)S(1)} %get-tuple-element.177), channel_id=1, source_target_pairs={{0,14},{1,15},{2,12},{3,13},{4,10},{5,11},{6,8},{7,9},{8,6},{9,7},... | collective-permute-start | bytes 405512 | tf_op jit(solution)/shard_map/ppermute | solution.py:48
  61.2 7.7 %collective-permute-start.17 = (bf16[264,256]{1,0:T(8,128)(2,1)S(1)}, bf16[264,256]{1,0:T(8,128)(2,1)S(1)}, u32[]{:S(2)}, u32[]{:S(2)}) collective-permute-start(bf16[264,256]{1,0:T(8,128)(2,1)S(1)} %get-tuple-element.180), channel_id=1, source_target_pairs={{0,7},{1,6},{2,5},{3,4},{4,3},{5,2},{6,1},{7,0},{8,15},{9,14},{10,... | collective-permute-start | bytes 405512 | tf_op jit(solution)/shard_map/ppermute | solution.py:48
  62.5 8.2 %collective-permute-start.18 = (bf16[264,256]{1,0:T(8,128)(2,1)S(1)}, bf16[264,256]{1,0:T(8,128)(2,1)S(1)}, u32[]{:S(2)}, u32[]{:S(2)}) collective-permute-start(bf16[264,256]{1,0:T(8,128)(2,1)S(1)} %get-tuple-element.183), channel_id=1, source_target_pairs={{0,15},{1,14},{2,13},{3,12},{4,11},{5,10},{6,9},{7,8},{8,7},{9,6},... | collective-permute-start | bytes 405512 | tf_op jit(solution)/shard_map/ppermute | solution.py:48

commit v5 on v4

--- a/solution.py
+++ b/solution.py
@@ -16,6 +16,8 @@
 SLAB = 16
 KEY_ROWS = 8
 IN_FLIGHT = 4
+LEADING = 3
+FIRST = 5
 VMEM_BYTES = 48 * 1024 * 1024
 VMEM = pl.BlockSpec(memory_space=pltpu.VMEM)
 SMEM = pl.BlockSpec(memory_space=pltpu.SMEM)
@@ -86,45 +88,48 @@
     copy.wait()
 
 
-def project(embeddings_ref, basis, offset, units_ref):
-    rows = embeddings_ref.shape[0]
-    step = min(CHUNK, rows)
-    for b in range(rows // step):
-        block = slice(b * step, (b + 1) * step)
-        projected = jnp.dot(embeddings_ref[block], basis, preferred_element_type=F32) - offset
-        scale_back = lax.rsqrt(jnp.sum(projected * projected, axis=1, keepdims=True) + 1e-06)
-        units_ref[block] = (projected * scale_back).astype(BF16)
-
-
-def fill_slots(masks, me_ref, place_ref, keys_ref, units_ref, out_refs):
+def spread_of(place_ref, owner, slot):
+    here = place_ref[...] - owner * slot
+    line = lax.broadcasted_iota(jnp.int32, (slot, place_ref.shape[1]), 0)
+    return jnp.where(here == line, 1.0, 0.0).astype(BF16)
+
+
+def lead_kernel(masks, slot, me_ref, place_ref, embeddings_ref, lead_ref):
+    for n, mask in enumerate(masks):
+        spread = spread_of(place_ref, me_ref[0] ^ mask, slot)
+        rows = jnp.dot(spread, embeddings_ref[...], preferred_element_type=F32)
+        lead_ref[n * slot : (n + 1) * slot] = rows.astype(BF16)
+
+
+def project(rows, basis, offset):
+    projected = jnp.dot(rows, basis, preferred_element_type=F32) - offset
+    scale_back = lax.rsqrt(jnp.sum(projected * projected, axis=1, keepdims=True) + 1e-06)
+    return (projected * scale_back).astype(BF16)
+
+
+def fill_keys(owner, keys_ref, out_ref):
     slot = keys_ref.shape[2]
-    rows = place_ref.shape[1]
-    units = units_ref[...]
-    for mask, out_ref in zip(masks, out_refs, strict=True):
-        owner = me_ref[0] ^ mask
-        here = place_ref[...] - owner * slot
-        spread = jnp.where(here == lax.broadcasted_iota(jnp.int32, (slot, rows), 0), 1.0, 0.0).astype(BF16)
-        out_ref[:slot] = jnp.dot(spread, units, preferred_element_type=F32).astype(BF16)
-        keys = keys_ref[owner]
-        line = lax.broadcasted_iota(jnp.int32, (KEY_ROWS, slot), 0)
-        parts = jnp.where(line == 0, keys // KEY_LOW, jnp.where(line == 1, keys % KEY_LOW, 0))
-        out_ref[slot:, :slot] = parts.astype(F32).astype(BF16)
-
-
-def slots_kernel(masks, me_ref, place_ref, keys_ref, units_ref, *out_refs):
-    fill_slots(masks, me_ref, place_ref, keys_ref, units_ref, out_refs)
-
-
-def project_whole_kernel(masks, me_ref, place_ref, keys_ref, embeddings_ref, basis_ref, center_ref, units_ref, *out_refs):
-    basis = basis_ref[...]
-    offset = jnp.dot(center_ref[...], basis, preferred_element_type=F32)
-    project(embeddings_ref, basis, offset, units_ref)
-    fill_slots(masks, me_ref, place_ref, keys_ref, units_ref, out_refs)
-
-
-def project_pieces_kernel(masks, spots, piece_rows, me_ref, place_ref, keys_ref, embeddings_ref, *refs):
-    *gathered_refs, units_ref = refs[: 3]
-    out_refs, basis_ref = refs[3:-1], refs[-1]
+    keys = keys_ref[owner]
+    line = lax.broadcasted_iota(jnp.int32, (KEY_ROWS, slot), 0)
+    parts = jnp.where(line == 0, keys // KEY_LOW, jnp.where(line == 1, keys % KEY_LOW, 0))
+    out_ref[slot:, :slot] = parts.astype(F32).astype(BF16)
+
+
+def fill_lead(masks, me_ref, keys_ref, lead_ref, basis, offset, out_refs):
+    slot = keys_ref.shape[2]
+    for n, (mask, out_ref) in enumerate(zip(masks, out_refs, strict=True)):
+        out_ref[:slot] = project(lead_ref[n * slot : (n + 1) * slot], basis, offset)
+        fill_keys(me_ref[0] ^ mask, keys_ref, out_ref)
+
+
+def first_whole_kernel(masks, me_ref, keys_ref, lead_ref, gathered_ref, center_ref, basis_ref, offset_ref, *out_refs):
+    basis_ref[...] = gathered_ref[...]
+    offset_ref[...] = jnp.dot(center_ref[...], basis_ref[...], preferred_element_type=F32)
+    fill_lead(masks, me_ref, keys_ref, lead_ref, basis_ref[...], offset_ref[...], out_refs)
+
+
+def first_pieces_kernel(masks, spots, piece_rows, me_ref, keys_ref, lead_ref, *refs):
+    *gathered_refs, basis_ref, offset_ref = refs[:4]
     half = len(spots) // 2
     tile = gathered_refs[0].shape[0] // half
     offset = None
@@ -136,7 +141,29 @@
         center = gathered_ref[at + piece_rows : at + tile, :piece_rows]
         part = jnp.dot(center, piece, preferred_element_type=F32)
         offset = part if offset is None else offset + part
-    project(embeddings_ref, basis_ref[...], offset[:1], units_ref)
+    offset_ref[...] = offset[:1]
+    fill_lead(masks, me_ref, keys_ref, lead_ref, basis_ref[...], offset[:1], refs[4:])
+
+
+def fill_slots(masks, me_ref, place_ref, keys_ref, units_ref, out_refs):
+    slot = keys_ref.shape[2]
+    units = units_ref[...]
+    for mask, out_ref in zip(masks, out_refs, strict=True):
+        owner = me_ref[0] ^ mask
+        spread = spread_of(place_ref, owner, slot)
+        out_ref[:slot] = jnp.dot(spread, units, preferred_element_type=F32).astype(BF16)
+        fill_keys(owner, keys_ref, out_ref)
+
+
+def units_kernel(masks, me_ref, place_ref, keys_ref, embeddings_ref, basis_ref, offset_ref, units_ref, *out_refs):
+    rows = embeddings_ref.shape[0]
+    step = min(CHUNK, rows)
+    for b in range(0, rows, step):
+        units_ref[b : b + step] = project(embeddings_ref[b : b + step], basis_ref[...], offset_ref[...])
+    fill_slots(masks, me_ref, place_ref, keys_ref, units_ref, out_refs)
+
+
+def slots_kernel(masks, me_ref, place_ref, keys_ref, units_ref, *out_refs):
     fill_slots(masks, me_ref, place_ref, keys_ref, units_ref, out_refs)
 
 
@@ -164,53 +191,58 @@
 
 def pairs_kernel(fresh_blocks, masks, me_ref, *refs):
     refs = list(refs)
-    state = (refs.pop(0), refs.pop(0)) if refs[0].shape[0] == 1 else None
-    block_refs = refs[:-6]
-    best_out_ref, row_out_ref, best_ref, line_ref, column_ref, all_ref = refs[-6:]
-    width = all_ref.shape[1]
+    best_in_ref = refs.pop(0) if refs[0].shape[0] == 1 else None
+    *block_refs, best_out_ref, best_ref, line_ref, column_ref = refs
     slot = block_refs[0].shape[0] - KEY_ROWS
     start = (len(block_refs) - fresh_blocks) * slot
     fresh = fresh_blocks * slot
-    end = start + fresh
-    row_ref = row_out_ref
-    best_ref[...] = jnp.full(best_ref.shape, -1.0, F32)
-    if state is not None:
-        row_ref[...] = state[1][...]
-        best_ref[:, :start] = state[0][:, :start]
-    else:
-        row_ref[...] = jnp.zeros(row_ref.shape, jnp.int32)
-    for n, block_ref in enumerate(block_refs):
-        at = n * slot
-        all_ref[at : at + slot] = block_ref[:slot]
-        if at >= start:
+    step = min(CHUNK, fresh)
+    if masks is None:
+        best_ref = best_out_ref
+    best_ref[:, start:] = jnp.full((1, best_ref.shape[1] - start), -1.0, F32)
+    if start:
+        best_ref[:, :start] = best_in_ref[:, :start]
+
+    def units_of(at, count):
+        pieces = [block_ref[:slot] for block_ref in block_refs[at // slot : (at + count) // slot]]
+        return pieces[0] if len(pieces) == 1 else jnp.concatenate(pieces, axis=0)
+
+    def keys_of(at, count):
+        pieces = []
+        for block_ref in block_refs[at // slot : (at + count) // slot]:
             parts = block_ref[slot:].astype(F32)[:, :slot]
-            row_ref[:, at : at + slot] = (parts[0:1] * KEY_LOW + parts[1:2]).astype(jnp.int32)
-    step = min(CHUNK, fresh)
+            pieces.append((parts[0:1] * KEY_LOW + parts[1:2]).astype(jnp.int32))
+        return pieces[0] if len(pieces) == 1 else jnp.concatenate(pieces, axis=1)
+
     for t in range(0, fresh, step):
-        column_ref[t : t + step] = column_of(row_ref[:, start + t : start + t + step])
-    line_ref[...] = jnp.full(line_ref.shape, -1.0, F32)
+        column_ref[t : t + step] = column_of(keys_of(start + t, step))
 
     def tile(t, lane, lanes, both):
-        new = all_ref[start + t : start + t + step]
-        others = all_ref[pl.ds(lane, lanes), :]
+        new, others = units_of(start + t, step), units_of(lane, lanes)
         cosines = lax.dot_general(new, others, (((1,), (1,)), ((), ())), preferred_element_type=F32)
+        keys = keys_of(lane, lanes)
         tiles = range(lanes // 128)
-        heres = [pl.ds(lane + n * 128, 128) for n in tiles]
-        key_rows = [row_ref[:, here] for here in heres]
+        key_rows = [keys[:, n * 128 : (n + 1) * 128] for n in tiles]
         label_rows = [key_row // RANK_SPAN for key_row in key_rows]
         below = [jnp.full((8, 128), -1.0, F32)] * len(tiles)
         for s in range(0, step, SLAB):
             key_col = column_ref[t + s : t + s + SLAB]
             label_col = key_col // RANK_SPAN
-            beside = line_ref[t + s : t + s + SLAB] if both else None
+            beside = None
+            if both:
+                beside = jnp.full((SLAB, 128), -1.0, F32) if fresh_line[t] else line_ref[t + s : t + s + SLAB]
             for n in tiles:
                 cosine = cosines[s : s + SLAB, n * 128 : (n + 1) * 128]
                 below[n], beside = best_of(cosine, key_col, label_col, key_rows[n], label_rows[n], below[n], beside)
             if both:
                 line_ref[t + s : t + s + SLAB] = beside
-        for n, here in zip(tiles, heres, strict=True):
+        if both:
+            fresh_line[t] = False
+        for n in tiles:
+            here = slice(lane + n * 128, lane + (n + 1) * 128)
             best_ref[:, here] = jnp.maximum(best_ref[:, here], jnp.max(below[n], axis=0, keepdims=True))
 
+    fresh_line = {t: True for t in range(0, fresh, step)}
     for t in range(0, fresh, step):
         tile(t, start + t, step, False)
         for lane in range(start, start + t, step):
@@ -220,13 +252,12 @@
             tile(t, lane, min(LANES, start - lane), True)
     same = lax.broadcasted_iota(jnp.int32, (128, 128), 0) == lax.broadcasted_iota(jnp.int32, (128, 128), 1)
     for t in range(0, fresh, 128):
-        here = slice(start + t, start + t + 128)
-        column = jnp.max(line_ref[t : t + 128], axis=1, keepdims=True)
-        turned = jnp.max(jnp.where(same, column, -1.0), axis=0, keepdims=True)
-        best_ref[:, here] = jnp.maximum(best_ref[:, here], turned)
-    if masks is None:
-        best_out_ref[...] = best_ref[...]
-    else:
+        if not fresh_line[t // step * step]:
+            here = slice(start + t, start + t + 128)
+            column = jnp.max(line_ref[t : t + 128], axis=1, keepdims=True)
+            turned = jnp.max(jnp.where(same, column, -1.0), axis=0, keepdims=True)
+            best_ref[:, here] = jnp.maximum(best_ref[:, here], turned)
+    if masks is not None:
         for n, mask in enumerate(masks):
             best_out_ref[me_ref[0] ^ mask] = best_ref[:, n * slot : (n + 1) * slot]
 
@@ -277,18 +308,23 @@
         cost_estimate=pl.CostEstimate(flops=0, bytes_accessed=4 * rows * depth, transcendentals=0),
     )(embeddings)
 
-    leading = order[:1]
-    followers = [order[1:3], order[3:5], [*order[5:], 0]]
-    blocks_of = lambda part: tuple(sds((slot + KEY_ROWS, width), BF16) for _ in part)
-    outs = (sds((rows, width), BF16), *blocks_of(leading))
-    cost = dict(flops=2 * rows * width * (depth + len(leading) * slot), moved=2 * rows * depth)
+    first, second, third = order[:LEADING], order[LEADING:FIRST], [*order[FIRST:], 0]
+    lead = call(
+        functools.partial(lead_kernel, first, slot),
+        sds((len(first) * slot, depth), BF16),
+        (me, place, staged),
+        smem=(0,),
+    )
+
+    blocks_of = lambda part: [sds((slot + KEY_ROWS, width), BF16) for _ in part]
+    outs = [sds((depth, width), BF16), sds((1, width), F32), *blocks_of(first)]
     if piece_rows % PIECE_TILE:
         basis = lax.all_gather(pca_basis, "wide", axis=0, tiled=True)
         center = lax.all_gather(pca_center, "wide", axis=0, tiled=True).reshape(1, depth)
-        kernel = functools.partial(project_whole_kernel, leading)
-        units, *sent = call(kernel, outs, (me, place, keys, staged, basis, center), smem=(0,), **cost)
+        kernel = functools.partial(first_whole_kernel, first)
+        basis, offset, *sent = call(kernel, outs, (me, keys, lead, basis, center), smem=(0,))
     else:
-        tail = jnp.pad(pca_center.reshape(1, piece_rows), ((0, PIECE_TILE - 1), (0, width - piece_rows)))
+        tail = jnp.pad(pca_center.reshape(1, piece_rows), ((0, KEY_ROWS - 1), (0, width - piece_rows)))
         gathered = lax.optimization_barrier(jnp.concatenate([pca_basis, tail], axis=0))
         spots = [0]
         bit = peers // 2
@@ -299,22 +335,31 @@
                 other, place, keys = lax.optimization_barrier((other, place, keys))
             elif len(spots) == 4:
                 other, staged = lax.optimization_barrier((other, staged))
+            elif len(spots) == 8:
+                other, lead = lax.optimization_barrier((other, lead))
             if len(spots) < peers:
                 gathered = lax.optimization_barrier(jnp.concatenate([gathered, other], axis=0))
             bit //= 2
-        kernel = functools.partial(project_pieces_kernel, leading, spots, piece_rows)
-        scratch = [pltpu.VMEM((depth, width), BF16)]
-        operands = (me, place, keys, staged, gathered, other)
-        units, *sent = call(kernel, outs, operands, scratch=scratch, smem=(0,), **cost)
-    for part in followers:
-        units, sent[-1] = lax.optimization_barrier((units, sent[-1]))
-        sent += call(
-            functools.partial(slots_kernel, part),
-            blocks_of(part),
-            (me, place, keys, units),
-            smem=(0,),
-            flops=2 * len(part) * slot * rows * width,
-        )
+        kernel = functools.partial(first_pieces_kernel, first, spots, piece_rows)
+        basis, offset, *sent = call(kernel, outs, (me, keys, lead, gathered, other), smem=(0,))
+    ahead = swap(sent[1], order[1], peers)
+    staged, ahead = lax.optimization_barrier((staged, ahead))
+    units, *made = call(
+        functools.partial(units_kernel, second),
+        [sds((rows, width), BF16), *blocks_of(second)],
+        (me, place, keys, staged, basis, offset),
+        smem=(0,),
+        flops=2 * rows * width * depth,
+    )
+    sent += made
+    units, sent[-1] = lax.optimization_barrier((units, sent[-1]))
+    sent += call(
+        functools.partial(slots_kernel, third),
+        blocks_of(third),
+        (me, place, keys, units),
+        smem=(0,),
+        flops=2 * len(third) * slot * rows * width,
+    )
 
     blocks = [sent[-1]]
     step = max(peers // 16, 1)
@@ -326,13 +371,12 @@
         fresh = (hi - lo) * slot
         return call(
             functools.partial(pairs_kernel, hi - lo, masks if last else None),
-            (sds((peers, 1, slot) if last else (1, total), F32), sds((1, total), jnp.int32)),
+            (sds((peers, 1, slot) if last else (1, total), F32),),
             (me, *state, *blocks[:hi]),
             scratch=[
                 pltpu.VMEM((1, total), F32),
                 pltpu.VMEM((fresh, 128), F32),
                 pltpu.VMEM((fresh, 128), jnp.int32),
-                pltpu.VMEM((hi * slot, width), BF16),
             ],
             smem=(0,),
             flops=2 * fresh * hi * slot * width,
@@ -340,12 +384,12 @@
 
     for n, mask in enumerate(order):
         block = sent[n]
-        if n >= IN_FLIGHT:
+        if n >= FIRST:
             if cuts[0] <= n + 2 - IN_FLIGHT:
                 state = add_pairs(state, done, cuts[0])
                 done = cuts.pop(0)
             block, *state = lax.optimization_barrier((block, *state))
-        blocks.append(swap(block, mask, peers))
+        blocks.append(ahead if n == 1 else swap(block, mask, peers))
     for cut in cuts:
         state = add_pairs(state, done, cut)
         done = cut

time: 86 us -> 84.4 us (0.981)
  waiting for transfers between devices: 12.2 us -> 7.45 us
  starting transfers between devices: 32.8 us -> 36.9 us
  blocking collectives: 12.3 us -> 10.9 us
    ppermute x19, waiting for transfers between devices: 12.2 us -> 7.45 us  [swap(): return lax.ppermute(x, 'wide', [(i, i ^ mask) for i in range(peers)])]
    ppermute x19, starting transfers between devices: 32.8 us -> 36.9 us  [swap(): return lax.ppermute(x, 'wide', [(i, i ^ mask) for i in range(peers)])]
    all_to_all x1, blocking collectives: 12.3 us -> 10.9 us  [shards(): lax.all_to_all(best, 'wide', split_axis=0, concat_axis=0, tiled=True)]
  transfers between devices with their start and end apart: 19 -> 19, of which waited for: 9 -> 5; matrix products, arithmetic and copies ran while one was open for 0% -> 0% of each run, Pallas kernels for 24% -> 28%
where the time goes in v5:
time: 84.4 us; the launch traced here: 84.1 us
  starting transfers between devices  36.9 us (44%)
  Pallas kernels  26.5 us (31%)
  blocking collectives  10.9 us (13%)
  waiting for transfers between devices  7.45 us (9%)
  local copies, waits for them, and re-layouts  1.39 us (2%)
    ppermute x19, starting transfers between devices, swap(): return lax.ppermute(x, 'wide', [(i, i ^ mask) for i in range(peers)])  36.9 us
    pallas_call x21, Pallas kernels, call(): pl.pallas_call(kernel, out_shape=outs, in_specs=[SMEM if i in smem else V...  24.6 us
    all_to_all x1, blocking collectives, shards(): lax.all_to_all(best, 'wide', split_axis=0, concat_axis=0, tiled=True)  10.9 us
    ppermute x19, waiting for transfers between devices, swap(): return lax.ppermute(x, 'wide', [(i, i ^ mask) for i in range(peers)])  7.45 us
    pallas_call x1, Pallas kernels, shards(): pl.pallas_call(stage_kernel, out_shape=sds((rows, depth), BF16), in_specs...  1.9 us
  transfers between devices with their start and end apart: 19, of which 5 were waited for; matrix products, arithmetic and copies ran while one was open for 0% of the time, Pallas kernels for 28%

profile of v5, /device:TPU:0, one launch (start us, length us, event | category | flops | bytes accessed | tf_op | source)
XLA Modules:
  0.0 84.1 jit_solution(5125852621264009933)
XLA Ops:
  0.8 4.0 %collective-permute-start = (bf16[56,256]{1,0:T(8,128)(2,1)S(1)}, bf16[56,256]{1,0:T(8,128)(2,1)S(1)}, u32[]{:S(2)}, u32[]{:S(2)}) collective-permute-start(bf16[56,256]{1,0:T(8,128)(2,1)S(1)} %fusion.1), channel_id=1, source_target_pairs={{0,8},{1,9},{2,10},{3,11},{4,12},{5,13},{6,14},{7,15},{8,0},{9,1},... | collective-permute-start | bytes 86024 | tf_op jit(solution)/shard_map/ppermute | solution.py:50
  6.9 1.7 %collective-permute-start.1 = (bf16[112,256]{1,0:T(8,128)(2,1)S(1)}, bf16[112,256]{1,0:T(8,128)(2,1)S(1)}, u32[]{:S(2)}, u32[]{:S(2)}) collective-permute-start(bf16[112,256]{1,0:T(8,128)(2,1)S(1)} %pad_maximum_fusion.2), channel_id=1, source_target_pairs={{0,4},{1,5},{2,6},{3,7},{4,0},{5,1},{6,2},{7,3},{8,12},{9,13},{10,... | collective-permute-start | bytes 172040 | tf_op jit(solution)/shard_map/ppermute | solution.py:50
  8.6 1.9 %shard_map.56.embeddings_ref = bf16[2048,768]{1,0:T(8,128)(2,1)S(1)} custom-call(bf16[2048,768]{1,0:T(8,128)(2,1)} %embeddings_ref.1), custom_call_target="tpu_custom_call" | custom-call | bytes 6291456 | tf_op jit(solution)/shard_map/pallas_call | solution.py:301
  11.1 1.8 %collective-permute-start.2 = (bf16[224,256]{1,0:T(8,128)(2,1)S(1)}, bf16[224,256]{1,0:T(8,128)(2,1)S(1)}, u32[]{:S(2)}, u32[]{:S(2)}) collective-permute-start(bf16[224,256]{1,0:T(8,128)(2,1)S(1)} %pad_maximum_fusion.1), channel_id=1, source_target_pairs={{0,2},{1,3},{2,0},{3,1},{4,6},{5,7},{6,4},{7,5},{8,10},{9,11},{10,... | collective-permute-start | bytes 344072 | tf_op jit(solution)/shard_map/ppermute | solution.py:50
  12.9 2.6 %shard_map.57.lead_ref = bf16[768,768]{1,0:T(8,128)(2,1)S(1)} custom-call(s32[1]{0:T(128)} %bitcast.3.me_ref, s32[1,2048]{1,0:T(1,128)S(1)} %get-tuple-element.59.place_ref, bf16[2048,768]{1,0:T(8,128)(2,1)S(1)} %shard_map.56.embeddings_ref), custom_call_target="tpu_custom_call" | custom-call | tf_op jit(solution)/shard_map/pallas_call | solution.py:29
  16.1 1.5 %collective-permute-done.3.refs_1_ = bf16[448,256]{1,0:T(8,128)(2,1)S(1)} collective-permute-done((bf16[448,256]{1,0:T(8,128)(2,1)S(1)}, bf16[448,256]{1,0:T(8,128)(2,1)S(1)}, u32[]{:S(2)}, u32[]{:S(2)}) %collective-permute-start.3) | collective-permute-done | bytes 229408 | tf_op jit(solution)/shard_map/ppermute | solution.py:50
  18.4 2.7 %collective-permute-start.5 = (bf16[264,256]{1,0:T(8,128)(2,1)S(1)}, bf16[264,256]{1,0:T(8,128)(2,1)S(1)}, u32[]{:S(2)}, u32[]{:S(2)}) collective-permute-start(bf16[264,256]{1,0:T(8,128)(2,1)S(1)} %get-tuple-element.84), channel_id=1, source_target_pairs={{0,8},{1,9},{2,10},{3,11},{4,12},{5,13},{6,14},{7,15},{8,0},{9,1},... | collective-permute-start | bytes 405512 | tf_op jit(solution)/shard_map/ppermute | solution.py:50
  21.1 1.6 %shard_map.59 = (bf16[2048,256]{1,0:T(8,128)(2,1)S(1)}, bf16[264,256]{1,0:T(8,128)(2,1)S(1)}, bf16[264,256]{1,0:T(8,128)(2,1)S(1)}) custom-call(s32[1]{0:T(128)} %bitcast.3.me_ref, s32[1,2048]{1,0:T(1,128)S(1)} %get-tuple-element.59.place_ref, s32[16,1,256]{2,1,0:T(1,128)S(1)} %get-tuple-element.60.keys_ref, bf16[2048,768]{1,0:T(8,128)(2,1)S(1)} %shard_map.56.embeddings_ref, ...), custom_call_target="tpu_custom_call" | custom-call | flops 805306368 | tf_op jit(solution)/shard_map/pallas_call | solution.py:29
  22.7 3.6 %collective-permute-start.8 = (bf16[264,256]{1,0:T(8,128)(2,1)S(1)}, bf16[264,256]{1,0:T(8,128)(2,1)S(1)}, u32[]{:S(2)}, u32[]{:S(2)}) collective-permute-start(bf16[264,256]{1,0:T(8,128)(2,1)S(1)} %get-tuple-element.92), channel_id=1, source_target_pairs={{0,10},{1,11},{2,8},{3,9},{4,14},{5,15},{6,12},{7,13},{8,2},{9,3},... | collective-permute-start | bytes 405512 | tf_op jit(solution)/shard_map/ppermute | solution.py:50
  26.8 3.1 %shard_map.60 = (bf16[264,256]{1,0:T(8,128)(2,1)S(1)}, bf16[264,256]{1,0:T(8,128)(2,1)S(1)}, bf16[264,256]{1,0:T(8,128)(2,1)S(1)}, bf16[264,256]{1,0:T(8,128)(2,...) custom-call(s32[1]{0:T(128)} %bitcast.3.me_ref, ...), custom_call_target="tpu_custom_call" | custom-call | flops 2952790016 | tf_op jit(solution)/shard_map/pallas_call | solution.py:29
  29.9 4.5 %collective-permute-done.5.refs_1_.refs_2_ = bf16[264,256]{1,0:T(8,128)(2,1)S(1)} collective-permute-done((bf16[264,256]{1,0:T(8,128)(2,1)S(1)}, bf16[264,256]{1,0:T(8,128)(2,1)S(1)}, u32[]{:S(2)}, u32[]{:S(2)}) %collective-permute-start.5) | collective-permute-done | bytes 135200 | tf_op jit(solution)/shard_map/ppermute | solution.py:50
  37.1 4.1 %collective-permute-start.11 = (bf16[264,256]{1,0:T(8,128)(2,1)S(1)}, bf16[264,256]{1,0:T(8,128)(2,1)S(1)}, u32[]{:S(2)}, u32[]{:S(2)}) collective-permute-start(bf16[264,256]{1,0:T(8,128)(2,1)S(1)} %get-tuple-element.98), channel_id=1, source_target_pairs={{0,4},{1,5},{2,6},{3,7},{4,0},{5,1},{6,2},{7,3},{8,12},{9,13},{10,... | collective-permute-start | bytes 405512 | tf_op jit(solution)/shard_map/ppermute | solution.py:50
  45.0 3.5 %collective-permute-start.14 = (bf16[264,256]{1,0:T(8,128)(2,1)S(1)}, bf16[264,256]{1,0:T(8,128)(2,1)S(1)}, u32[]{:S(2)}, u32[]{:S(2)}) collective-permute-start(bf16[264,256]{1,0:T(8,128)(2,1)S(1)} %get-tuple-element.104), channel_id=1, source_target_pairs={{0,13},{1,12},{2,15},{3,14},{4,9},{5,8},{6,11},{7,10},{8,5},{9,4},... | collective-permute-start | bytes 405512 | tf_op jit(solution)/shard_map/ppermute | solution.py:50
  48.5 1.1 %shard_map.67.refs_0_ = f32[1,4096]{1,0:T(1,128)S(1)} custom-call(s32[1]{0:T(128)} %bitcast.3.me_ref, f32[1,4096]{1,0:T(1,128)S(1)} %shard_map.66.refs_0_, bf16[264,256]{1,0:T(8,128)(2,1)S(1)} %get-tuple-element.83.refs_0_.refs_1_, bf16[264,256]{1,0:T(8,128)(2,1)S(1)} %collective-permute-done.5.refs_1_.refs_2_, ...), custom_call_target="tpu_custom_call" | custom-call | flops 268435456 | tf_op jit(solution)/shard_map/pallas_call | solution.py:29
  49.6 1.3 %collective-permute-start.15 = (bf16[264,256]{1,0:T(8,128)(2,1)S(1)}, bf16[264,256]{1,0:T(8,128)(2,1)S(1)}, u32[]{:S(2)}, u32[]{:S(2)}) collective-permute-start(bf16[264,256]{1,0:T(8,128)(2,1)S(1)} %get-tuple-element.105), channel_id=1, source_target_pairs={{0,6},{1,7},{2,4},{3,5},{4,2},{5,3},{6,0},{7,1},{8,14},{9,15},{10,... | collective-permute-start | bytes 405512 | tf_op jit(solution)/shard_map/ppermute | solution.py:50
  51.9 7.4 %collective-permute-start.16 = (bf16[264,256]{1,0:T(8,128)(2,1)S(1)}, bf16[264,256]{1,0:T(8,128)(2,1)S(1)}, u32[]{:S(2)}, u32[]{:S(2)}) collective-permute-start(bf16[264,256]{1,0:T(8,128)(2,1)S(1)} %get-tuple-element.106), channel_id=1, source_target_pairs={{0,14},{1,15},{2,12},{3,13},{4,10},{5,11},{6,8},{7,9},{8,6},{9,7},... | collective-permute-start | bytes 405512 | tf_op jit(solution)/shard_map/ppermute | solution.py:50
  60.4 1.1 %shard_map.70.refs_0_ = f32[1,4096]{1,0:T(1,128)S(1)} custom-call(s32[1]{0:T(128)} %bitcast.3.me_ref, f32[1,4096]{1,0:T(1,128)S(1)} %shard_map.69.refs_0_, bf16[264,256]{1,0:T(8,128)(2,1)S(1)} %get-tuple-element.83.refs_0_.refs_1_, bf16[264,256]{1,0:T(8,128)(2,1)S(1)} %collective-permute-done.5.refs_1_.refs_2_, ...), custom_call_target="tpu_custom_call" | custom-call | flops 369098752 | tf_op jit(solution)/shard_map/pallas_call | solution.py:29
  61.5 3.9 %collective-permute-start.18 = (bf16[264,256]{1,0:T(8,128)(2,1)S(1)}, bf16[264,256]{1,0:T(8,128)(2,1)S(1)}, u32[]{:S(2)}, u32[]{:S(2)}) collective-permute-start(bf16[264,256]{1,0:T(8,128)(2,1)S(1)} %get-tuple-element.108), channel_id=1, source_target_pairs={{0,15},{1,14},{2,13},{3,12},{4,11},{5,10},{6,9},{7,8},{8,7},{9,6},... | collective-permute-start | bytes 405512 | tf_op jit(solution)/shard_map/ppermute | solution.py:50
  65.4 1.2 %shard_map.71.refs_0_ = f32[1,4096]{1,0:T(1,128)S(1)} custom-call(s32[1]{0:T(128)} %bitcast.3.me_ref, f32[1,4096]{1,0:T(1,128)S(1)} %shard_map.70.refs_0_, bf16[264,256]{1,0:T(8,128)(2,1)S(1)} %get-tuple-element.83.refs_0_.refs_1_, bf16[264,256]{1,0:T(8,128)(2,1)S(1)} %collective-permute-done.5.refs_1_.refs_2_, ...), custom_call_target="tpu_custom_call" | custom-call | flops 402653184 | tf_op jit(solution)/shard_map/pallas_call | solution.py:29
  66.6 1.3 %shard_map.72.refs_0_ = f32[1,4096]{1,0:T(1,128)S(1)} custom-call(s32[1]{0:T(128)} %bitcast.3.me_ref, f32[1,4096]{1,0:T(1,128)S(1)} %shard_map.71.refs_0_, bf16[264,256]{1,0:T(8,128)(2,1)S(1)} %get-tuple-element.83.refs_0_.refs_1_, bf16[264,256]{1,0:T(8,128)(2,1)S(1)} %collective-permute-done.5.refs_1_.refs_2_, ...), custom_call_target="tpu_custom_call" | custom-call | flops 436207616 | tf_op jit(solution)/shard_map/pallas_call | solution.py:29
  67.9 1.4 %shard_map.73.refs_0_ = f32[1,4096]{1,0:T(1,128)S(1)} custom-call(s32[1]{0:T(128)} %bitcast.3.me_ref, f32[1,4096]{1,0:T(1,128)S(1)} %shard_map.72.refs_0_, bf16[264,256]{1,0:T(8,128)(2,1)S(1)} %get-tuple-element.83.refs_0_.refs_1_, bf16[264,256]{1,0:T(8,128)(2,1)S(1)} %collective-permute-done.5.refs_1_.refs_2_, ...), custom_call_target="tpu_custom_call" | custom-call | flops 469762048 | tf_op jit(solution)/shard_map/pallas_call | solution.py:29
  69.3 1.4 %shard_map.74.refs_0_ = f32[1,4096]{1,0:T(1,128)S(1)} custom-call(s32[1]{0:T(128)} %bitcast.3.me_ref, f32[1,4096]{1,0:T(1,128)S(1)} %shard_map.73.refs_0_, bf16[264,256]{1,0:T(8,128)(2,1)S(1)} %get-tuple-element.83.refs_0_.refs_1_, bf16[264,256]{1,0:T(8,128)(2,1)S(1)} %collective-permute-done.5.refs_1_.refs_2_, ...), custom_call_target="tpu_custom_call" | custom-call | flops 503316480 | tf_op jit(solution)/shard_map/pallas_call | solution.py:29
  70.7 1.5 %shard_map.75 = f32[16,1,256]{2,1,0:T(1,128)S(1)} custom-call(s32[1]{0:T(128)} %bitcast.3.me_ref, f32[1,4096]{1,0:T(1,128)S(1)} %shard_map.74.refs_0_, bf16[264,256]{1,0:T(8,128)(2,1)S(1)} %get-tuple-element.83.refs_0_.refs_1_, bf16[264,256]{1,0:T(8,128)(2,1)S(1)} %collective-permute-done.5.refs_1_.refs_2_, ...), custom_call_target="tpu_custom_call" | custom-call | flops 536870912 | tf_op jit(solution)/shard_map/pallas_call | solution.py:29
  72.2 10.9 %all_to_all.5.returned_ref = f32[16,1,256]{2,1,0:T(1,128)S(1)} all-to-all(f32[16,1,256]{2,1,0:T(1,128)S(1)} %shard_map.75), channel_id=1, replica_groups=mesh['groups'=2,'wide'=16] {'wide'}, dimensions={0} | all-to-all | bytes 32768 | tf_op jit(solution)/shard_map/all_to_all | solution.py:397
  (45 shorter events, 14.9 us)
Async XLA Ops:
  0.8 6.1 %collective-permute-start = (bf16[56,256]{1,0:T(8,128)(2,1)S(1)}, bf16[56,256]{1,0:T(8,128)(2,1)S(1)}, u32[]{:S(2)}, u32[]{:S(2)}) collective-permute-start(bf16[56,256]{1,0:T(8,128)(2,1)S(1)} %fusion.1), channel_id=1, source_target_pairs={{0,8},{1,9},{2,10},{3,11},{4,12},{5,13},{6,14},{7,15},{8,0},{9,1},... | collective-permute-start | bytes 86024 | tf_op jit(solution)/shard_map/ppermute | solution.py:50
  4.8 0.7 copy-start
  5.5 0.7 copy-start.1
  6.9 4.2 %collective-permute-start.1 = (bf16[112,256]{1,0:T(8,128)(2,1)S(1)}, bf16[112,256]{1,0:T(8,128)(2,1)S(1)}, u32[]{:S(2)}, u32[]{:S(2)}) collective-permute-start(bf16[112,256]{1,0:T(8,128)(2,1)S(1)} %pad_maximum_fusion.2), channel_id=1, source_target_pairs={{0,4},{1,5},{2,6},{3,7},{4,0},{5,1},{6,2},{7,3},{8,12},{9,13},{10,... | collective-permute-start | bytes 172040 | tf_op jit(solution)/shard_map/ppermute | solution.py:50
  11.1 4.9 %collective-permute-start.2 = (bf16[224,256]{1,0:T(8,128)(2,1)S(1)}, bf16[224,256]{1,0:T(8,128)(2,1)S(1)}, u32[]{:S(2)}, u32[]{:S(2)}) collective-permute-start(bf16[224,256]{1,0:T(8,128)(2,1)S(1)} %pad_maximum_fusion.1), channel_id=1, source_target_pairs={{0,2},{1,3},{2,0},{3,1},{4,6},{5,7},{6,4},{7,5},{8,10},{9,11},{10,... | collective-permute-start | bytes 344072 | tf_op jit(solution)/shard_map/ppermute | solution.py:50
  16.0 1.6 %collective-permute-start.3 = (bf16[448,256]{1,0:T(8,128)(2,1)S(1)}, bf16[448,256]{1,0:T(8,128)(2,1)S(1)}, u32[]{:S(2)}, u32[]{:S(2)}) collective-permute-start(bf16[448,256]{1,0:T(8,128)(2,1)S(1)} %pad_maximum_fusion.refs_0_), channel_id=1, source_target_pairs={{0,1},{1,0},{2,3},{3,2},{4,5},{5,4},{6,7},{7,6},{8,9},{9,8},{10,11... | collective-permute-start | bytes 688136 | tf_op jit(solution)/shard_map/ppermute | solution.py:50
  18.2 2.9 %collective-permute-start.4 = (bf16[264,256]{1,0:T(8,128)(2,1)S(1)}, bf16[264,256]{1,0:T(8,128)(2,1)S(1)}, u32[]{:S(2)}, u32[]{:S(2)}) collective-permute-start(bf16[264,256]{1,0:T(8,128)(2,1)S(1)} %get-tuple-element.66), channel_id=1, source_target_pairs={{0,1},{1,0},{2,3},{3,2},{4,5},{5,4},{6,7},{7,6},{8,9},{9,8},{10,11... | collective-permute-start | bytes 405512 | tf_op jit(solution)/shard_map/ppermute | solution.py:50
  18.4 16.0 %collective-permute-start.5 = (bf16[264,256]{1,0:T(8,128)(2,1)S(1)}, bf16[264,256]{1,0:T(8,128)(2,1)S(1)}, u32[]{:S(2)}, u32[]{:S(2)}) collective-permute-start(bf16[264,256]{1,0:T(8,128)(2,1)S(1)} %get-tuple-element.84), channel_id=1, source_target_pairs={{0,8},{1,9},{2,10},{3,11},{4,12},{5,13},{6,14},{7,15},{8,0},{9,1},... | collective-permute-start | bytes 405512 | tf_op jit(solution)/shard_map/ppermute | solution.py:50
  21.1 15.4 %collective-permute-start.6 = (bf16[264,256]{1,0:T(8,128)(2,1)S(1)}, bf16[264,256]{1,0:T(8,128)(2,1)S(1)}, u32[]{:S(2)}, u32[]{:S(2)}) collective-permute-start(bf16[264,256]{1,0:T(8,128)(2,1)S(1)} %get-tuple-element.88), channel_id=1, source_target_pairs={{0,9},{1,8},{2,11},{3,10},{4,13},{5,12},{6,15},{7,14},{8,1},{9,0},... | collective-permute-start | bytes 405512 | tf_op jit(solution)/shard_map/ppermute | solution.py:50
  22.7 20.1 %collective-permute-start.8 = (bf16[264,256]{1,0:T(8,128)(2,1)S(1)}, bf16[264,256]{1,0:T(8,128)(2,1)S(1)}, u32[]{:S(2)}, u32[]{:S(2)}) collective-permute-start(bf16[264,256]{1,0:T(8,128)(2,1)S(1)} %get-tuple-element.92), channel_id=1, source_target_pairs={{0,10},{1,11},{2,8},{3,9},{4,14},{5,15},{6,12},{7,13},{8,2},{9,3},... | collective-permute-start | bytes 405512 | tf_op jit(solution)/shard_map/ppermute | solution.py:50
  26.3 14.9 %collective-permute-start.7 = (bf16[264,256]{1,0:T(8,128)(2,1)S(1)}, bf16[264,256]{1,0:T(8,128)(2,1)S(1)}, u32[]{:S(2)}, u32[]{:S(2)}) collective-permute-start(bf16[264,256]{1,0:T(8,128)(2,1)S(1)} %get-tuple-element.90), channel_id=1, source_target_pairs={{0,2},{1,3},{2,0},{3,1},{4,6},{5,7},{6,4},{7,5},{8,10},{9,11},{10,... | collective-permute-start | bytes 405512 | tf_op jit(solution)/shard_map/ppermute | solution.py:50
  35.1 9.1 %collective-permute-start.9 = (bf16[264,256]{1,0:T(8,128)(2,1)S(1)}, bf16[264,256]{1,0:T(8,128)(2,1)S(1)}, u32[]{:S(2)}, u32[]{:S(2)}) collective-permute-start(bf16[264,256]{1,0:T(8,128)(2,1)S(1)} %get-tuple-element.94), channel_id=1, source_target_pairs={{0,3},{1,2},{2,1},{3,0},{4,7},{5,6},{6,5},{7,4},{8,11},{9,10},{10,... | collective-permute-start | bytes 405512 | tf_op jit(solution)/shard_map/ppermute | solution.py:50
  36.0 12.5 %collective-permute-start.10 = (bf16[264,256]{1,0:T(8,128)(2,1)S(1)}, bf16[264,256]{1,0:T(8,128)(2,1)S(1)}, u32[]{:S(2)}, u32[]{:S(2)}) collective-permute-start(bf16[264,256]{1,0:T(8,128)(2,1)S(1)} %get-tuple-element.96), channel_id=1, source_target_pairs={{0,11},{1,10},{2,9},{3,8},{4,15},{5,14},{6,13},{7,12},{8,3},{9,2},... | collective-permute-start | bytes 405512 | tf_op jit(solution)/shard_map/ppermute | solution.py:50
  37.1 13.8 %collective-permute-start.11 = (bf16[264,256]{1,0:T(8,128)(2,1)S(1)}, bf16[264,256]{1,0:T(8,128)(2,1)S(1)}, u32[]{:S(2)}, u32[]{:S(2)}) collective-permute-start(bf16[264,256]{1,0:T(8,128)(2,1)S(1)} %get-tuple-element.98), channel_id=1, source_target_pairs={{0,4},{1,5},{2,6},{3,7},{4,0},{5,1},{6,2},{7,3},{8,12},{9,13},{10,... | collective-permute-start | bytes 405512 | tf_op jit(solution)/shard_map/ppermute | solution.py:50
  41.9 17.4 %collective-permute-start.12 = (bf16[264,256]{1,0:T(8,128)(2,1)S(1)}, bf16[264,256]{1,0:T(8,128)(2,1)S(1)}, u32[]{:S(2)}, u32[]{:S(2)}) collective-permute-start(bf16[264,256]{1,0:T(8,128)(2,1)S(1)} %get-tuple-element.100), channel_id=1, source_target_pairs={{0,12},{1,13},{2,14},{3,15},{4,8},{5,9},{6,10},{7,11},{8,4},{9,5},... | collective-permute-start | bytes 405512 | tf_op jit(solution)/shard_map/ppermute | solution.py:50
  43.5 16.9 %collective-permute-start.13 = (bf16[264,256]{1,0:T(8,128)(2,1)S(1)}, bf16[264,256]{1,0:T(8,128)(2,1)S(1)}, u32[]{:S(2)}, u32[]{:S(2)}) collective-permute-start(bf16[264,256]{1,0:T(8,128)(2,1)S(1)} %get-tuple-element.102), channel_id=1, source_target_pairs={{0,5},{1,4},{2,7},{3,6},{4,1},{5,0},{6,3},{7,2},{8,13},{9,12},{10,... | collective-permute-start | bytes 405512 | tf_op jit(solution)/shard_map/ppermute | solution.py:50
  45.0 20.4 %collective-permute-start.14 = (bf16[264,256]{1,0:T(8,128)(2,1)S(1)}, bf16[264,256]{1,0:T(8,128)(2,1)S(1)}, u32[]{:S(2)}, u32[]{:S(2)}) collective-permute-start(bf16[264,256]{1,0:T(8,128)(2,1)S(1)} %get-tuple-element.104), channel_id=1, source_target_pairs={{0,13},{1,12},{2,15},{3,14},{4,9},{5,8},{6,11},{7,10},{8,5},{9,4},... | collective-permute-start | bytes 405512 | tf_op jit(solution)/shard_map/ppermute | solution.py:50
  49.6 17.0 %collective-permute-start.15 = (bf16[264,256]{1,0:T(8,128)(2,1)S(1)}, bf16[264,256]{1,0:T(8,128)(2,1)S(1)}, u32[]{:S(2)}, u32[]{:S(2)}) collective-permute-start(bf16[264,256]{1,0:T(8,128)(2,1)S(1)} %get-tuple-element.105), channel_id=1, source_target_pairs={{0,6},{1,7},{2,4},{3,5},{4,2},{5,3},{6,0},{7,1},{8,14},{9,15},{10,... | collective-permute-start | bytes 405512 | tf_op jit(solution)/shard_map/ppermute | solution.py:50
  51.9 16.0 %collective-permute-start.16 = (bf16[264,256]{1,0:T(8,128)(2,1)S(1)}, bf16[264,256]{1,0:T(8,128)(2,1)S(1)}, u32[]{:S(2)}, u32[]{:S(2)}) collective-permute-start(bf16[264,256]{1,0:T(8,128)(2,1)S(1)} %get-tuple-element.106), channel_id=1, source_target_pairs={{0,14},{1,15},{2,12},{3,13},{4,10},{5,11},{6,8},{7,9},{8,6},{9,7},... | collective-permute-start | bytes 405512 | tf_op jit(solution)/shard_map/ppermute | solution.py:50
  60.3 9.0 %collective-permute-start.17 = (bf16[264,256]{1,0:T(8,128)(2,1)S(1)}, bf16[264,256]{1,0:T(8,128)(2,1)S(1)}, u32[]{:S(2)}, u32[]{:S(2)}) collective-permute-start(bf16[264,256]{1,0:T(8,128)(2,1)S(1)} %get-tuple-element.107), channel_id=1, source_target_pairs={{0,7},{1,6},{2,5},{3,4},{4,3},{5,2},{6,1},{7,0},{8,15},{9,14},{10,... | collective-permute-start | bytes 405512 | tf_op jit(solution)/shard_map/ppermute | solution.py:50
  61.5 9.2 %collective-permute-start.18 = (bf16[264,256]{1,0:T(8,128)(2,1)S(1)}, bf16[264,256]{1,0:T(8,128)(2,1)S(1)}, u32[]{:S(2)}, u32[]{:S(2)}) collective-permute-start(bf16[264,256]{1,0:T(8,128)(2,1)S(1)} %get-tuple-element.108), channel_id=1, source_target_pairs={{0,15},{1,14},{2,13},{3,12},{4,11},{5,10},{6,9},{7,8},{8,7},{9,6},... | collective-permute-start | bytes 405512 | tf_op jit(solution)/shard_map/ppermute | solution.py:50
